TPU v7x, 128 devices: a whole 4x4x4 slice. The times are simulated.
128 devices in a mesh: tm: 64 (over z, y, x), col: 2 (over core).
Axes of the slice: x: 4, y: 4, z: 4, core: 2. Of those that a mesh axis runs over, the one named last changes fastest.
Arguments:
- diagonal_blocks: float32 [128, 512, 512], P('tm', 'col'), as said below
- upper_blocks: float32 [128, 512, 512], P('tm', 'col')
- right_sides: float32 [128, 512, 512], P('tm', 'col'), may hold values from -6 to 6
Outputs:
- reduced_blocks: float32 [128, 512, 512], P('tm', 'col')
- reduced_uppers: float32 [128, 512, 512], P('tm', 'col')
- reduced_sources: float32 [128, 512, 512], P('tm', 'col')
Inputs may be any that keep to these rules, and one draw needn't show every extreme that they name: `diagonal_blocks`: every block is symmetric, and the block-tridiagonal matrix built from these blocks and upper_blocks is positive definite.
All inputs are finite; a program needn't handle non-finite values.
Results may differ from a plain program's by a relative error of at most 0.0001.
Values sent between devices are 32-bit elements; how exact they have to be, the bound alone decides.
No kernel may reach another device: no remote copies, remote signals or barrier semaphores. Data moves between devices by JAX's collectives and lax.ppermute only.
A program may use at most 64 MiB of HBM per device.

v0:
```python
import jax
import jax.numpy as jnp
from jax import lax
from jax.experimental import pallas as pl
from jax.experimental.pallas import tpu as pltpu
from jax.sharding import PartitionSpec as P

F32 = jnp.float32
BF16 = jnp.bfloat16
N = 512
H = N // 2

NN = (((1,), (0,)), ((), ()))
NT = (((1,), (1,)), ((), ()))
TN = (((0,), (0,)), ((), ()))

VMEM = pl.BlockSpec(memory_space=pltpu.VMEM)
SMEM = pl.BlockSpec(memory_space=pltpu.SMEM)

SQUARINGS = 5
TARGET = 3e-3
USABLE = 0.6


def dot(a, b, dims=NN):
    return lax.dot_general(a, b, dims, preferred_element_type=F32)


def halves(x):
    high = x.astype(BF16)
    return high, (x - high.astype(F32)).astype(BF16)


def dot3(a, b, dims=NN):
    (ah, al), (bh, bl) = a, b
    return dot(ah, bh, dims) + (dot(ah, bl, dims) + dot(al, bh, dims))


def identity():
    rows = lax.broadcasted_iota(jnp.int32, (N, N), 0)
    lanes = lax.broadcasted_iota(jnp.int32, (N, N), 1)
    return jnp.where(rows == lanes, 1.0, 0.0).astype(F32)


def sweep_inverse(d_ref, x_ref):
    x_ref[...] = d_ref[...]

    def step(k, carry):
        rows = lax.broadcasted_iota(jnp.int32, (N, N), 0)
        lanes = lax.broadcasted_iota(jnp.int32, (N, N), 1)
        a = x_ref[...]
        row = x_ref[pl.ds(k, 1), :]
        col = jnp.sum(jnp.where(lanes == k, a, 0.0), axis=1, keepdims=True)
        lane = lax.broadcasted_iota(jnp.int32, (1, N), 1)
        inv = 1.0 / jnp.sum(jnp.where(lane == k, row, 0.0), axis=1, keepdims=True)
        row = row * inv
        new = a - col * row
        new = jnp.where(rows == k, jnp.broadcast_to(row, (N, N)), new)
        new = jnp.where(lanes == k, jnp.broadcast_to(col * inv, (N, N)), new)
        new = jnp.where(jnp.logical_and(rows == k, lanes == k), -inv, new)
        x_ref[...] = new
        return carry

    lax.fori_loop(0, N, step, 0)
    x_ref[...] = -x_ref[...]


def invert(d_ref, x_ref, res_ref):
    block = d_ref[...]
    top = jnp.max(jnp.sum(jnp.abs(block), axis=1, keepdims=True), axis=0, keepdims=True)
    alpha = 1.9 / top
    r = identity() - block * alpha
    y = identity() + r
    r = r.astype(BF16)
    r = dot(r, r).astype(BF16)
    for _ in range(SQUARINGS - 1):
        squared = dot(r, r)
        y = y + dot(y.astype(BF16), r)
        r = squared.astype(BF16)
    y = y + dot(y.astype(BF16), r)
    x_ref[...] = y * alpha

    def measure():
        residual = identity() - dot3(halves(d_ref[...]), halves(x_ref[...]))
        res_ref[...] = residual
        return jnp.sum(residual * residual)

    def improve():
        x = x_ref[...]
        x_ref[...] = x + dot(x.astype(BF16), res_ref[...].astype(BF16))

    def going(carry):
        size, count = carry
        return (size > TARGET * TARGET) & (size < USABLE * USABLE) & (count < 6)

    def refine(carry):
        improve()
        return measure(), carry[1] + 1

    size, _ = lax.while_loop(going, refine, (measure(), 0))
    converged = size <= TARGET * TARGET

    @pl.when(converged)
    def _():
        improve()

    @pl.when(jnp.logical_not(converged))
    def _():
        sweep_inverse(d_ref, x_ref)


def join(info_ref, own_ref, other_ref, full_ref):
    core = info_ref[0]
    full_ref[pl.ds(pl.multiple_of(core * H, H), H), :] = own_ref[...]
    full_ref[pl.ds(pl.multiple_of((1 - core) * H, H), H), :] = other_ref[...]


def own_rows(info_ref, full_ref):
    return full_ref[pl.ds(pl.multiple_of(info_ref[0] * H, H), H), :]


def own_columns(info_ref, full_ref):
    return full_ref[:, pl.ds(pl.multiple_of(info_ref[0] * H, H), H)]


def call(kernel, outs, operands, scratch, flops, limit=32):
    moved = sum(o.size * 4 for o in operands) + sum(4 * jnp.zeros(o, F32).size for o in outs)
    return pl.pallas_call(
        kernel,
        out_shape=[jax.ShapeDtypeStruct(o, F32) for o in outs],
        in_specs=[SMEM] + [VMEM] * (len(operands) - 1),
        out_specs=[VMEM] * len(outs),
        scratch_shapes=[pltpu.VMEM(s, F32) for s in scratch],
        compiler_params=pltpu.CompilerParams(vmem_limit_bytes=limit * 2**20),
        cost_estimate=pl.CostEstimate(flops=flops, bytes_accessed=moved, transcendentals=0),
    )(*operands)


CUBE = 2 * N * N * N
FULL = (N, N)
SLAB = (H, N)
PAIR = (2, H, N)


def first_inverse(info, own, other):
    def kernel(info_ref, own_ref, other_ref, z_ref, zc_ref, d_ref, res_ref):
        join(info_ref, own_ref, other_ref, d_ref)
        invert(d_ref, z_ref, res_ref)
        zc_ref[...] = own_rows(info_ref, z_ref)

    return call(kernel, [FULL, SLAB], [info, own, other], [FULL, FULL], 20 * CUBE)


def left_updates(info, z, uo, uo_other, de, de_other, fe, fo):
    def kernel(info_ref, z_ref, uo_ref, uox_ref, de_ref, dex_ref, fe_ref, fo_ref, a_ref, b_ref, u_ref):
        join(info_ref, uo_ref, uox_ref, u_ref)
        join(info_ref, de_ref, dex_ref, a_ref)
        z2 = halves(z_ref[...])
        u2 = halves(u_ref[...])
        v = dot3(u2, z2)
        a_ref[...] = a_ref[...] - dot3(halves(v), u2, NT)
        g = dot3(halves(fo_ref[...]), z2)
        b_ref[...] = fe_ref[...] - dot3(halves(g), u2, NT)

    return call(
        kernel, [FULL, SLAB], [info, z, uo, uo_other, de, de_other, fe, fo], [FULL], 9 * CUBE
    )


def coupled_upper(info, zq, zq_other, ue, ue_other, uq):
    def kernel(info_ref, zq_ref, zqx_ref, ue_ref, uex_ref, uq_ref, un_ref, z_ref, u_ref):
        join(info_ref, zq_ref, zqx_ref, z_ref)
        join(info_ref, ue_ref, uex_ref, u_ref)
        v = dot3(halves(uq_ref[...]), halves(z_ref[...]))
        fresh = -dot3(halves(v), halves(u_ref[...]))
        un_ref[...] = jnp.where(info_ref[1] > 0, fresh, ue_ref[...])

    return call(kernel, [SLAB, FULL, FULL], [info, zq, zq_other, ue, ue_other, uq], [], 3 * CUBE)


def second_inverse(info, a, zq, u):
    def kernel(info_ref, a_ref, zq_ref, u_ref, dc_ref, z_ref, zc_ref, d_ref, res_ref):
        u2 = halves(u_ref[...])
        w = dot3(u2, halves(zq_ref[...]), TN)
        d_ref[...] = a_ref[...] - dot3(halves(w), u2)
        dc_ref[...] = own_rows(info_ref, d_ref)

        @pl.when(info_ref[2] > 0)
        def _():
            invert(d_ref, z_ref, res_ref)
            zc_ref[...] = own_rows(info_ref, z_ref)

    return call(kernel, [SLAB, FULL, SLAB], [info, a, zq, u], [FULL, FULL], 26 * CUBE)


def level0_sources(info, b, fq, zq, u):
    def kernel(info_ref, b_ref, fq_ref, zq_ref, u_ref, f_ref):
        g = dot3(halves(fq_ref[...]), halves(zq_ref[...]))
        f_ref[...] = b_ref[...] - dot3(halves(g), halves(u_ref[...]))

    return call(kernel, [SLAB], [info, b, fq, zq, u], [], 3 * CUBE)[0]


def solved_sources(info, f, z):
    def kernel(info_ref, f_ref, z_ref, g_ref):
        @pl.when(info_ref[2] > 0)
        def _():
            g_ref[...] = dot3(halves(f_ref[...]), halves(z_ref[...]))

    return call(kernel, [SLAB], [info, f, z], [], CUBE)[0]


def level1_blocks(info, d, u_mid, u_mid_other, right, left, d_in, u_in):
    ur, urx, zr, zrx = right
    ul, zl, zlx = left

    def kernel(
        info_ref, d_ref, um_ref, umx_ref, ur_ref, urx_ref, zr_ref, zrx_ref, ul_ref, zl_ref, zlx_ref,
        din_ref, uin_ref, dout_ref, uout_ref, mid_ref, far_ref, zr_full, zl_full,
    ):
        dout_ref[1] = din_ref[1]
        uout_ref[1] = uin_ref[1]

        @pl.when(info_ref[2] > 0)
        def _():
            dout_ref[0] = d_ref[...]
            uout_ref[0] = um_ref[...]

        @pl.when(info_ref[2] == 0)
        def _():
            join(info_ref, um_ref, umx_ref, mid_ref)
            join(info_ref, ur_ref, urx_ref, far_ref)
            join(info_ref, zr_ref, zrx_ref, zr_full)
            join(info_ref, zl_ref, zlx_ref, zl_full)
            mid = halves(mid_ref[...])
            zl2 = halves(zl_full[...])
            v = dot3(halves(ur_ref[...]), halves(zr_full[...]))
            w = dot3(halves(own_columns(info_ref, mid_ref)), zl2, TN)
            dout_ref[0] = d_ref[...] - dot3(halves(v), halves(far_ref[...]), NT) - dot3(halves(w), mid)
            s = dot3(halves(ul_ref[...]), zl2)
            fresh = -dot3(halves(s), mid)
            uout_ref[0] = jnp.where(info_ref[1] > 0, fresh, um_ref[...])

    return call(
        kernel, [PAIR, PAIR],
        [info, d, u_mid, u_mid_other, ur, urx, zr, zrx, ul, zl, zlx, d_in, u_in],
        [FULL] * 4, 9 * CUBE,
    )


def level1_sources(info, f, gr, ur, urx, gl, u_mid, u_mid_other, f_in):
    def kernel(info_ref, f_ref, gr_ref, ur_ref, urx_ref, gl_ref, um_ref, umx_ref, fin_ref, out_ref, mid_ref, far_ref):
        out_ref[1] = fin_ref[1]

        @pl.when(info_ref[2] > 0)
        def _():
            out_ref[0] = f_ref[...]

        @pl.when(info_ref[2] == 0)
        def _():
            join(info_ref, um_ref, umx_ref, mid_ref)
            join(info_ref, ur_ref, urx_ref, far_ref)
            out_ref[0] = (
                f_ref[...]
                - dot3(halves(gr_ref[...]), halves(far_ref[...]), NT)
                - dot3(halves(gl_ref[...]), halves(mid_ref[...]))
            )

    return call(
        kernel, [PAIR], [info, f, gr, ur, urx, gl, u_mid, u_mid_other, f_in], [FULL, FULL], 3 * CUBE
    )[0]


def body(diagonal_blocks, upper_blocks, right_sides):
    chips = lax.axis_size("tm")
    position = lax.axis_index("tm")
    info = jnp.stack([lax.axis_index("col"), (position > 0).astype(jnp.int32), position % 2]).astype(jnp.int32)

    def swap(a):
        return lax.ppermute(a, "col", [(0, 1), (1, 0)])

    def onward(a):
        return lax.ppermute(a, "tm", [(i, i + 1) for i in range(chips - 1)])

    def odd_left(a):
        return lax.ppermute(a, "tm", [(i, i - 1) for i in range(1, chips, 2)])

    def odd_right(a):
        return lax.ppermute(a, "tm", [(i, i + 1) for i in range(1, chips - 1, 2)])

    de, do = diagonal_blocks[0], diagonal_blocks[1]
    ue, uo = upper_blocks[0], upper_blocks[1]
    fe, fo = right_sides[0], right_sides[1]

    uq = onward(uo)
    zo, zo_own = first_inverse(info, do, swap(do))
    zq = onward(zo_own)
    fq = onward(fo)
    a, b = left_updates(info, zo, uo, swap(uo), de, swap(de), fe, fo)
    u_mid, zq_full, ue_full = coupled_upper(info, zq, swap(zq), ue, swap(ue), uq)
    ur = odd_left(u_mid)
    ul = odd_right(u_mid)
    u_mid_other = swap(u_mid)
    d_mid, z1, z1_own = second_inverse(info, a, zq_full, ue_full)
    zr = odd_left(z1_own)
    zl = odd_right(z1_own)
    f_mid = level0_sources(info, b, fq, zq_full, ue_full)
    g1 = solved_sources(info, f_mid, z1)
    gr = odd_left(g1)
    gl = odd_right(g1)
    urx = swap(ur)
    d_out, u_out = level1_blocks(
        info, d_mid, u_mid, u_mid_other, (ur, urx, zr, swap(zr)), (ul, zl, swap(zl)),
        diagonal_blocks, upper_blocks,
    )
    f_out = level1_sources(info, f_mid, gr, ur, urx, gl, u_mid, u_mid_other, right_sides)
    return d_out, u_out, f_out


def solution(mesh):
    placed = (P("tm", "col", None),) * 3
    return jax.shard_map(body, mesh=mesh, in_specs=placed, out_specs=placed, check_vma=False)
```

profile of v0, /device:TPU:64, one launch (start us, length us, event | category | flops | bytes accessed | tf_op | source)
XLA Modules:
  0.0 111.0 jit_solution(16177295602489269580)
XLA Ops:
  0.6 1.3 %slice_bitcast_fusion.3 = (f32[256,512]{1,0:T(8,128)S(1)}, f32[256,512]{1,0:T(8,128)S(1)}) fusion(f32[2,256,512]{2,1,0:T(8,128)} %din_ref.1), kind=kLoop, calls=%fused_computation.3 | loop fusion | bytes 2097152 | tf_op jit(solution)/shard_map/squeeze | solution.py:291
  1.9 0.1 collective-permute-start
  2.0 0.1 pad_add_fusion.info_ref
  2.1 0.0 copy-start.2
  2.1 1.8 %collective-permute-done.other_ref = f32[256,512]{1,0:T(8,128)S(1)} collective-permute-done((f32[256,512]{1,0:T(8,128)S(1)}, f32[256,512]{1,0:T(8,128)S(1)}, u32[]{:S(2)}, u32[]{:S(2)}) %collective-permute-start) | collective-permute-done | bytes 524320 | tf_op jit(solution)/shard_map/ppermute | solution.py:280
  3.9 8.8 %shard_map.58 = (f32[512,512]{1,0:T(8,128)S(1)}, f32[256,512]{1,0:T(8,128)S(1)}) custom-call(s32[3]{0:T(128)S(1)} %pad_add_fusion.info_ref, f32[256,512]{1,0:T(8,128)S(1)} %get-tuple-element.32.own_ref, f32[256,512]{1,0:T(8,128)S(1)} %collective-permute-done.other_ref), custom_call_target="tpu_custom_call" | custom-call | flops 5368709120 | bytes 2621452 | tf_op jit(solution)/shard_map/pallas_call | solution.py:128
  12.7 0.0 copy-start
  12.7 3.5 %collective-permute-start.3 = (f32[256,512]{1,0:T(8,128)S(1)}, f32[256,512]{1,0:T(8,128)S(1)}, u32[]{:S(2)}, u32[]{:S(2)}) collective-permute-start(f32[256,512]{1,0:T(8,128)S(1)} %get-tuple-element.17), channel_id=1, source_target_pairs={{0,2},{2,4},{4,6},{6,8},{8,10},{10,12},{12,14},{14,16},{16,18},{18... | collective-permute-start | bytes 1572872 | tf_op jit(solution)/shard_map/ppermute | solution.py:283
  16.2 0.0 copy-done.2
  16.2 0.1 slice_bitcast_fusion
  16.3 0.1 collective-permute-start.1
  16.4 0.5 collective-permute-start.2
  16.9 3.4 %collective-permute-start.6 = (f32[256,512]{1,0:T(8,128)S(1)}, f32[256,512]{1,0:T(8,128)S(1)}, u32[]{:S(2)}, u32[]{:S(2)}) collective-permute-start(f32[256,512]{1,0:T(8,128)S(1)} %get-tuple-element.28.uo_ref), channel_id=1, source_target_pairs={{0,2},{2,4},{4,6},{6,8},{8,10},{10,12},{12,14},{14,16},{16,18},{18... | collective-permute-start | bytes 1572872 | tf_op jit(solution)/shard_map/ppermute | solution.py:283
  20.3 0.1 collective-permute-start.5
  20.4 13.3 %collective-permute-done.3.zq_ref = f32[256,512]{1,0:T(8,128)S(1)} collective-permute-done((f32[256,512]{1,0:T(8,128)S(1)}, f32[256,512]{1,0:T(8,128)S(1)}, u32[]{:S(2)}, u32[]{:S(2)}) %collective-permute-start.3) | collective-permute-done | bytes 524320 | tf_op jit(solution)/shard_map/ppermute | solution.py:283
  33.7 0.0 collective-permute-start.4
  33.7 0.0 copy-done
  33.7 0.1 slice_bitcast_fusion.1
  33.8 0.0 collective-permute-done.1.uox_ref
  33.8 1.9 %collective-permute-start.15 = (f32[256,512]{1,0:T(8,128)S(1)}, f32[256,512]{1,0:T(8,128)S(1)}, u32[]{:S(2)}, u32[]{:S(2)}) collective-permute-start(f32[256,512]{1,0:T(8,128)S(1)} %get-tuple-element.29.fo_ref), channel_id=1, source_target_pairs={{0,2},{2,4},{4,6},{6,8},{8,10},{10,12},{12,14},{14,16},{16,18},{18... | collective-permute-start | bytes 1572872 | tf_op jit(solution)/shard_map/ppermute | solution.py:283
  35.7 0.0 collective-permute-done.2.dex_ref
  35.7 3.4 %shard_map.59 = (f32[512,512]{1,0:T(8,128)S(1)}, f32[256,512]{1,0:T(8,128)S(1)}) custom-call(s32[3]{0:T(128)S(1)} %pad_add_fusion.info_ref, f32[512,512]{1,0:T(8,128)S(1)} %get-tuple-element.15.z_ref, f32[256,512]{1,0:T(8,128)S(1)} %get-tuple-element.28.uo_ref, f32[256,512]{1,0:T(8,128)S(1)} %collective-permute-done.1.uox_ref, ...), custom_call_target="tpu_custom_call" | custom-call | flops 2415919104 | bytes 5767180 | tf_op jit(solution)/shard_map/pallas_call | solution.py:128
  39.1 5.8 %collective-permute-done.6.uq_ref = f32[256,512]{1,0:T(8,128)S(1)} collective-permute-done((f32[256,512]{1,0:T(8,128)S(1)}, f32[256,512]{1,0:T(8,128)S(1)}, u32[]{:S(2)}, u32[]{:S(2)}) %collective-permute-start.6) | collective-permute-done | bytes 524320 | tf_op jit(solution)/shard_map/ppermute | solution.py:283
  44.9 0.0 collective-permute-done.5.uex_ref
  45.0 0.0 collective-permute-done.4.zqx_ref
  45.0 1.7 %shard_map.60 = (f32[256,512]{1,0:T(8,128)S(1)}, f32[512,512]{1,0:T(8,128)S(1)}, f32[512,512]{1,0:T(8,128)S(1)}) custom-call(s32[3]{0:T(128)S(1)} %pad_add_fusion.info_ref, f32[256,512]{1,0:T(8,128)S(1)} %collective-permute-done.3.zq_ref, f32[256,512]{1,0:T(8,128)S(1)} %collective-permute-done.4.zqx_ref, f32[256,512]{1,0:T(8,128)S(1)} %get-tuple-element.27.ue_ref, ...), custom_call_target="tpu_custom_call" | custom-call | flops 805306368 | bytes 5242892 | tf_op jit(solution)/shard_map/pallas_call | solution.py:128
  46.7 2.7 %shard_map.61 = (f32[256,512]{1,0:T(8,128)S(1)}, f32[512,512]{1,0:T(8,128)S(1)}, f32[256,512]{1,0:T(8,128)S(1)}) custom-call(s32[3]{0:T(128)S(1)} %pad_add_fusion.info_ref, f32[512,512]{1,0:T(8,128)S(1)} %get-tuple-element.16.a_ref, f32[512,512]{1,0:T(8,128)S(1)} %get-tuple-element.18.zq_ref, f32[512,512]{1,0:T(8,128)S(1)} %get-tuple-element.19.u_ref), custom_call_target="tpu_custom_call" | custom-call | flops 6979321856 | bytes 5242892 | tf_op jit(solution)/shard_map/pallas_call | solution.py:128
  49.4 6.0 %collective-permute-done.15.fq_ref = f32[256,512]{1,0:T(8,128)S(1)} collective-permute-done((f32[256,512]{1,0:T(8,128)S(1)}, f32[256,512]{1,0:T(8,128)S(1)}, u32[]{:S(2)}, u32[]{:S(2)}) %collective-permute-start.15) | collective-permute-done | bytes 524320 | tf_op jit(solution)/shard_map/ppermute | solution.py:283
  55.4 1.7 %shard_map.63.f_ref = f32[256,512]{1,0:T(8,128)S(1)} custom-call(s32[3]{0:T(128)S(1)} %pad_add_fusion.info_ref, f32[256,512]{1,0:T(8,128)S(1)} %get-tuple-element.25.b_ref, f32[256,512]{1,0:T(8,128)S(1)} %collective-permute-done.15.fq_ref, f32[512,512]{1,0:T(8,128)S(1)} %get-tuple-element.18.zq_ref, f32[512,512]{1,0:T(8,128)S(1)} %get-tuple-element.19.u_ref), custom_call_target="tpu_custom_call" | custom-call | flops 805306368 | bytes 3670028 | tf_op jit(solution)/shard_map/pallas_call | solution.py:128
  57.1 0.5 shard_map.64
  57.6 1.3 %collective-permute-start.16 = (f32[256,512]{1,0:T(8,128)S(1)}, f32[256,512]{1,0:T(8,128)S(1)}, u32[]{:S(2)}, u32[]{:S(2)}) collective-permute-start(f32[256,512]{1,0:T(8,128)S(1)} %shard_map.64), channel_id=1, source_target_pairs={{2,0},{6,4},{10,8},{14,12},{18,16},{22,20},{26,24},{30,28},{34,32}... | collective-permute-start | bytes 1572872 | tf_op jit(solution)/shard_map/ppermute | solution.py:286
  58.9 1.3 %collective-permute-start.8 = (f32[256,512]{1,0:T(8,128)S(1)}, f32[256,512]{1,0:T(8,128)S(1)}, u32[]{:S(2)}, u32[]{:S(2)}) collective-permute-start(f32[256,512]{1,0:T(8,128)S(1)} %get-tuple-element.21.um_ref), channel_id=1, source_target_pairs={{2,0},{6,4},{10,8},{14,12},{18,16},{22,20},{26,24},{30,28},{34,32}... | collective-permute-start | bytes 1572872 | tf_op jit(solution)/shard_map/ppermute | solution.py:286
  60.2 1.3 %collective-permute-start.17 = (f32[256,512]{1,0:T(8,128)S(1)}, f32[256,512]{1,0:T(8,128)S(1)}, u32[]{:S(2)}, u32[]{:S(2)}) collective-permute-start(f32[256,512]{1,0:T(8,128)S(1)} %shard_map.64), channel_id=1, source_target_pairs={{2,4},{6,8},{10,12},{14,16},{18,20},{22,24},{26,28},{30,32},{34,36... | collective-permute-start | bytes 1572872 | tf_op jit(solution)/shard_map/ppermute | solution.py:289
  61.5 0.0 copy-start.1
  61.5 1.4 %collective-permute-start.10 = (f32[256,512]{1,0:T(8,128)S(1)}, f32[256,512]{1,0:T(8,128)S(1)}, u32[]{:S(2)}, u32[]{:S(2)}) collective-permute-start(f32[256,512]{1,0:T(8,128)S(1)} %get-tuple-element.22), channel_id=1, source_target_pairs={{2,0},{6,4},{10,8},{14,12},{18,16},{22,20},{26,24},{30,28},{34,32}... | collective-permute-start | bytes 1572872 | tf_op jit(solution)/shard_map/ppermute | solution.py:286
  63.0 1.3 %collective-permute-start.13 = (f32[256,512]{1,0:T(8,128)S(1)}, f32[256,512]{1,0:T(8,128)S(1)}, u32[]{:S(2)}, u32[]{:S(2)}) collective-permute-start(f32[256,512]{1,0:T(8,128)S(1)} %get-tuple-element.22), channel_id=1, source_target_pairs={{2,4},{6,8},{10,12},{14,16},{18,20},{22,24},{26,28},{30,32},{34,36... | collective-permute-start | bytes 1572872 | tf_op jit(solution)/shard_map/ppermute | solution.py:289
  64.3 10.1 %collective-permute-done.16.gr_ref = f32[256,512]{1,0:T(8,128)S(1)} collective-permute-done((f32[256,512]{1,0:T(8,128)S(1)}, f32[256,512]{1,0:T(8,128)S(1)}, u32[]{:S(2)}, u32[]{:S(2)}) %collective-permute-start.16) | collective-permute-done | bytes 524320 | tf_op jit(solution)/shard_map/ppermute | solution.py:286
  74.4 0.0 collective-permute-start.7
  74.4 11.2 %collective-permute-done.8.ur_ref = f32[256,512]{1,0:T(8,128)S(1)} collective-permute-done((f32[256,512]{1,0:T(8,128)S(1)}, f32[256,512]{1,0:T(8,128)S(1)}, u32[]{:S(2)}, u32[]{:S(2)}) %collective-permute-start.8) | collective-permute-done | bytes 524320 | tf_op jit(solution)/shard_map/ppermute | solution.py:286
  85.6 0.0 collective-permute-start.9
  85.6 0.0 collective-permute-done.17.gl_ref
  85.6 1.3 %collective-permute-start.12 = (f32[256,512]{1,0:T(8,128)S(1)}, f32[256,512]{1,0:T(8,128)S(1)}, u32[]{:S(2)}, u32[]{:S(2)}) collective-permute-start(f32[256,512]{1,0:T(8,128)S(1)} %get-tuple-element.21.um_ref), channel_id=1, source_target_pairs={{2,4},{6,8},{10,12},{14,16},{18,20},{22,24},{26,28},{30,32},{34,36... | collective-permute-start | bytes 1572872 | tf_op jit(solution)/shard_map/ppermute | solution.py:289
  86.9 8.2 %collective-permute-done.10.zr_ref = f32[256,512]{1,0:T(8,128)S(1)} collective-permute-done((f32[256,512]{1,0:T(8,128)S(1)}, f32[256,512]{1,0:T(8,128)S(1)}, u32[]{:S(2)}, u32[]{:S(2)}) %collective-permute-start.10) | collective-permute-done | bytes 524320 | tf_op jit(solution)/shard_map/ppermute | solution.py:286
  95.1 0.0 collective-permute-start.11
  95.1 0.0 collective-permute-done.13.zl_ref
  95.1 0.5 collective-permute-start.14
  95.6 0.0 collective-permute-done.7.umx_ref
  95.6 0.0 collective-permute-done.9.urx_ref
  95.6 2.7 %shard_map.65 = f32[2,256,512]{2,1,0:T(8,128)} custom-call(s32[3]{0:T(128)S(1)} %pad_add_fusion.info_ref, f32[256,512]{1,0:T(8,128)S(1)} %shard_map.63.f_ref, f32[256,512]{1,0:T(8,128)S(1)} %collective-permute-done.16.gr_ref, f32[256,512]{1,0:T(8,128)S(1)} %collective-permute-done.8.ur_ref, f32[256,512]{1,0:T(8,128)S(1)} %collective-permute-done.9.urx_ref, ...), custom_call_target="tpu_custom_call" | custom-call | flops 805306368 | bytes 5767180 | tf_op jit(solution)/shard_map/pallas_call | solution.py:128
  98.4 7.7 %collective-permute-done.12.ul_ref = f32[256,512]{1,0:T(8,128)S(1)} collective-permute-done((f32[256,512]{1,0:T(8,128)S(1)}, f32[256,512]{1,0:T(8,128)S(1)}, u32[]{:S(2)}, u32[]{:S(2)}) %collective-permute-start.12) | collective-permute-done | bytes 524320 | tf_op jit(solution)/shard_map/ppermute | solution.py:289
  106.0 0.0 collective-permute-done.11.zrx_ref
  106.0 0.0 collective-permute-done.14.zlx_ref
  106.1 0.0 copy-done.1
  106.1 4.9 %shard_map.62 = (f32[2,256,512]{2,1,0:T(8,128)}, f32[2,256,512]{2,1,0:T(8,128)}) custom-call(s32[3]{0:T(128)S(1)} %pad_add_fusion.info_ref, f32[256,512]{1,0:T(8,128)S(1)} %get-tuple-element.20.d_ref, f32[256,512]{1,0:T(8,128)S(1)} %get-tuple-element.21.um_ref, f32[256,512]{1,0:T(8,128)S(1)} %collective-permute-done.7.umx_ref, ...), custom_call_target="tpu_custom_call" | custom-call | flops 2415919104 | bytes 9437196 | tf_op jit(solution)/shard_map/pallas_call | solution.py:128
Async XLA Ops:
  1.9 2.0 %collective-permute-start = (f32[256,512]{1,0:T(8,128)S(1)}, f32[256,512]{1,0:T(8,128)S(1)}, u32[]{:S(2)}, u32[]{:S(2)}) collective-permute-start(f32[256,512]{1,0:T(8,128)S(1)} %get-tuple-element.32.own_ref), channel_id=1, source_target_pairs={{0,1},{1,0},{2,3},{3,2},{4,5},{5,4},{6,7},{7,6},{8,9},{9,8},{10,11... | collective-permute-start | bytes 1572872 | tf_op jit(solution)/shard_map/ppermute | solution.py:280
  2.1 14.2 %copy-start.2 = (f32[2,256,512]{2,1,0:T(8,128)S(1)}, f32[2,256,512]{2,1,0:T(8,128)}, u32[]{:S(2)}) copy-start(f32[2,256,512]{2,1,0:T(8,128)} %uin_ref.1) | copy-start | bytes 3145732
  12.7 21.0 %copy-start = (f32[2,256,512]{2,1,0:T(8,128)S(1)}, f32[2,256,512]{2,1,0:T(8,128)}, u32[]{:S(2)}) copy-start(f32[2,256,512]{2,1,0:T(8,128)} %fin_ref.1) | copy-start | bytes 3145732
  12.7 21.0 %collective-permute-start.3 = (f32[256,512]{1,0:T(8,128)S(1)}, f32[256,512]{1,0:T(8,128)S(1)}, u32[]{:S(2)}, u32[]{:S(2)}) collective-permute-start(f32[256,512]{1,0:T(8,128)S(1)} %get-tuple-element.17), channel_id=1, source_target_pairs={{0,2},{2,4},{4,6},{6,8},{8,10},{10,12},{12,14},{14,16},{16,18},{18... | collective-permute-start | bytes 1572872 | tf_op jit(solution)/shard_map/ppermute | solution.py:283
  16.3 17.5 %collective-permute-start.1 = (f32[256,512]{1,0:T(8,128)S(1)}, f32[256,512]{1,0:T(8,128)S(1)}, u32[]{:S(2)}, u32[]{:S(2)}) collective-permute-start(f32[256,512]{1,0:T(8,128)S(1)} %get-tuple-element.28.uo_ref), channel_id=1, source_target_pairs={{0,1},{1,0},{2,3},{3,2},{4,5},{5,4},{6,7},{7,6},{8,9},{9,8},{10,11... | collective-permute-start | bytes 1572872 | tf_op jit(solution)/shard_map/ppermute | solution.py:280
  16.4 19.3 %collective-permute-start.2 = (f32[256,512]{1,0:T(8,128)S(1)}, f32[256,512]{1,0:T(8,128)S(1)}, u32[]{:S(2)}, u32[]{:S(2)}) collective-permute-start(f32[256,512]{1,0:T(8,128)S(1)} %get-tuple-element.31.de_ref), channel_id=1, source_target_pairs={{0,1},{1,0},{2,3},{3,2},{4,5},{5,4},{6,7},{7,6},{8,9},{9,8},{10,11... | collective-permute-start | bytes 1572872 | tf_op jit(solution)/shard_map/ppermute | solution.py:280
  16.9 28.0 %collective-permute-start.6 = (f32[256,512]{1,0:T(8,128)S(1)}, f32[256,512]{1,0:T(8,128)S(1)}, u32[]{:S(2)}, u32[]{:S(2)}) collective-permute-start(f32[256,512]{1,0:T(8,128)S(1)} %get-tuple-element.28.uo_ref), channel_id=1, source_target_pairs={{0,2},{2,4},{4,6},{6,8},{8,10},{10,12},{12,14},{14,16},{16,18},{18... | collective-permute-start | bytes 1572872 | tf_op jit(solution)/shard_map/ppermute | solution.py:283
  20.3 24.6 %collective-permute-start.5 = (f32[256,512]{1,0:T(8,128)S(1)}, f32[256,512]{1,0:T(8,128)S(1)}, u32[]{:S(2)}, u32[]{:S(2)}) collective-permute-start(f32[256,512]{1,0:T(8,128)S(1)} %get-tuple-element.27.ue_ref), channel_id=1, source_target_pairs={{0,1},{1,0},{2,3},{3,2},{4,5},{5,4},{6,7},{7,6},{8,9},{9,8},{10,11... | collective-permute-start | bytes 1572872 | tf_op jit(solution)/shard_map/ppermute | solution.py:280
  33.7 11.2 %collective-permute-start.4 = (f32[256,512]{1,0:T(8,128)S(1)}, f32[256,512]{1,0:T(8,128)S(1)}, u32[]{:S(2)}, u32[]{:S(2)}) collective-permute-start(f32[256,512]{1,0:T(8,128)S(1)} %collective-permute-done.3.zq_ref), channel_id=1, source_target_pairs={{0,1},{1,0},{2,3},{3,2},{4,5},{5,4},{6,7},{7,6},{8,9},{9,8},{10,11... | collective-permute-start | bytes 1572872 | tf_op jit(solution)/shard_map/ppermute | solution.py:280
  33.8 21.6 %collective-permute-start.15 = (f32[256,512]{1,0:T(8,128)S(1)}, f32[256,512]{1,0:T(8,128)S(1)}, u32[]{:S(2)}, u32[]{:S(2)}) collective-permute-start(f32[256,512]{1,0:T(8,128)S(1)} %get-tuple-element.29.fo_ref), channel_id=1, source_target_pairs={{0,2},{2,4},{4,6},{6,8},{8,10},{10,12},{12,14},{14,16},{16,18},{18... | collective-permute-start | bytes 1572872 | tf_op jit(solution)/shard_map/ppermute | solution.py:283
  57.6 16.8 %collective-permute-start.16 = (f32[256,512]{1,0:T(8,128)S(1)}, f32[256,512]{1,0:T(8,128)S(1)}, u32[]{:S(2)}, u32[]{:S(2)}) collective-permute-start(f32[256,512]{1,0:T(8,128)S(1)} %shard_map.64), channel_id=1, source_target_pairs={{2,0},{6,4},{10,8},{14,12},{18,16},{22,20},{26,24},{30,28},{34,32}... | collective-permute-start | bytes 1572872 | tf_op jit(solution)/shard_map/ppermute | solution.py:286
  58.9 26.7 %collective-permute-start.8 = (f32[256,512]{1,0:T(8,128)S(1)}, f32[256,512]{1,0:T(8,128)S(1)}, u32[]{:S(2)}, u32[]{:S(2)}) collective-permute-start(f32[256,512]{1,0:T(8,128)S(1)} %get-tuple-element.21.um_ref), channel_id=1, source_target_pairs={{2,0},{6,4},{10,8},{14,12},{18,16},{22,20},{26,24},{30,28},{34,32}... | collective-permute-start | bytes 1572872 | tf_op jit(solution)/shard_map/ppermute | solution.py:286
  60.2 25.4 %collective-permute-start.17 = (f32[256,512]{1,0:T(8,128)S(1)}, f32[256,512]{1,0:T(8,128)S(1)}, u32[]{:S(2)}, u32[]{:S(2)}) collective-permute-start(f32[256,512]{1,0:T(8,128)S(1)} %shard_map.64), channel_id=1, source_target_pairs={{2,4},{6,8},{10,12},{14,16},{18,20},{22,24},{26,28},{30,32},{34,36... | collective-permute-start | bytes 1572872 | tf_op jit(solution)/shard_map/ppermute | solution.py:289
  61.5 44.5 %copy-start.1 = (f32[2,256,512]{2,1,0:T(8,128)S(1)}, f32[2,256,512]{2,1,0:T(8,128)}, u32[]{:S(2)}) copy-start(f32[2,256,512]{2,1,0:T(8,128)} %din_ref.1) | copy-start | bytes 3145732
  61.5 33.6 %collective-permute-start.10 = (f32[256,512]{1,0:T(8,128)S(1)}, f32[256,512]{1,0:T(8,128)S(1)}, u32[]{:S(2)}, u32[]{:S(2)}) collective-permute-start(f32[256,512]{1,0:T(8,128)S(1)} %get-tuple-element.22), channel_id=1, source_target_pairs={{2,0},{6,4},{10,8},{14,12},{18,16},{22,20},{26,24},{30,28},{34,32}... | collective-permute-start | bytes 1572872 | tf_op jit(solution)/shard_map/ppermute | solution.py:286
  63.0 32.2 %collective-permute-start.13 = (f32[256,512]{1,0:T(8,128)S(1)}, f32[256,512]{1,0:T(8,128)S(1)}, u32[]{:S(2)}, u32[]{:S(2)}) collective-permute-start(f32[256,512]{1,0:T(8,128)S(1)} %get-tuple-element.22), channel_id=1, source_target_pairs={{2,4},{6,8},{10,12},{14,16},{18,20},{22,24},{26,28},{30,32},{34,36... | collective-permute-start | bytes 1572872 | tf_op jit(solution)/shard_map/ppermute | solution.py:289
  74.4 21.3 %collective-permute-start.7 = (f32[256,512]{1,0:T(8,128)S(1)}, f32[256,512]{1,0:T(8,128)S(1)}, u32[]{:S(2)}, u32[]{:S(2)}) collective-permute-start(f32[256,512]{1,0:T(8,128)S(1)} %get-tuple-element.21.um_ref), channel_id=1, source_target_pairs={{0,1},{1,0},{2,3},{3,2},{4,5},{5,4},{6,7},{7,6},{8,9},{9,8},{10,11... | collective-permute-start | bytes 1572872 | tf_op jit(solution)/shard_map/ppermute | solution.py:280
  85.6 10.0 %collective-permute-start.9 = (f32[256,512]{1,0:T(8,128)S(1)}, f32[256,512]{1,0:T(8,128)S(1)}, u32[]{:S(2)}, u32[]{:S(2)}) collective-permute-start(f32[256,512]{1,0:T(8,128)S(1)} %collective-permute-done.8.ur_ref), channel_id=1, source_target_pairs={{0,1},{1,0},{2,3},{3,2},{4,5},{5,4},{6,7},{7,6},{8,9},{9,8},{10,11... | collective-permute-start | bytes 1572872 | tf_op jit(solution)/shard_map/ppermute | solution.py:280
  85.6 20.4 %collective-permute-start.12 = (f32[256,512]{1,0:T(8,128)S(1)}, f32[256,512]{1,0:T(8,128)S(1)}, u32[]{:S(2)}, u32[]{:S(2)}) collective-permute-start(f32[256,512]{1,0:T(8,128)S(1)} %get-tuple-element.21.um_ref), channel_id=1, source_target_pairs={{2,4},{6,8},{10,12},{14,16},{18,20},{22,24},{26,28},{30,32},{34,36... | collective-permute-start | bytes 1572872 | tf_op jit(solution)/shard_map/ppermute | solution.py:289
  95.1 10.9 %collective-permute-start.11 = (f32[256,512]{1,0:T(8,128)S(1)}, f32[256,512]{1,0:T(8,128)S(1)}, u32[]{:S(2)}, u32[]{:S(2)}) collective-permute-start(f32[256,512]{1,0:T(8,128)S(1)} %collective-permute-done.10.zr_ref), channel_id=1, source_target_pairs={{0,1},{1,0},{2,3},{3,2},{4,5},{5,4},{6,7},{7,6},{8,9},{9,8},{10,11... | collective-permute-start | bytes 1572872 | tf_op jit(solution)/shard_map/ppermute | solution.py:280
  95.1 10.9 %collective-permute-start.14 = (f32[256,512]{1,0:T(8,128)S(1)}, f32[256,512]{1,0:T(8,128)S(1)}, u32[]{:S(2)}, u32[]{:S(2)}) collective-permute-start(f32[256,512]{1,0:T(8,128)S(1)} %collective-permute-done.13.zl_ref), channel_id=1, source_target_pairs={{0,1},{1,0},{2,3},{3,2},{4,5},{5,4},{6,7},{7,6},{8,9},{9,8},{10,11... | collective-permute-start | bytes 1572872 | tf_op jit(solution)/shard_map/ppermute | solution.py:280
where the time goes:
time: 111 us
  waiting for transfers between devices  64.2 us (58%)
  Pallas kernels  26.4 us (24%)
  starting transfers between devices  18 us (16%)
  local copies, waits for them, and re-layouts  1.43 us (1%)
    ppermute x3, waiting for transfers between devices, odd_left(): return lax.ppermute(a, 'tm', [(i, i - 1) for i in range(1, chips, 2)])  29.5 us
    pallas_call x8, Pallas kernels, call(): pl.pallas_call(kernel, out_shape=[jax.ShapeDtypeStruct(o, F32) for o in o...  26.4 us
    ppermute x3, waiting for transfers between devices, onward(): return lax.ppermute(a, 'tm', [(i, i + 1) for i in range(chips - 1)])  25.1 us
    ppermute x3, starting transfers between devices, onward(): return lax.ppermute(a, 'tm', [(i, i + 1) for i in range(chips - 1)])  8.83 us
    ppermute x3, waiting for transfers between devices, odd_right(): return lax.ppermute(a, 'tm', [(i, i + 1) for i in range(1, chips - 1, 2)])  7.7 us
    ppermute x3, starting transfers between devices, odd_left(): return lax.ppermute(a, 'tm', [(i, i - 1) for i in range(1, chips, 2)])  4.01 us
    ppermute x3, starting transfers between devices, odd_right(): return lax.ppermute(a, 'tm', [(i, i + 1) for i in range(1, chips - 1, 2)])  3.87 us
  transfers between devices with their start and end apart: 18, of which 8 were waited for; matrix products, arithmetic and copies ran while one was open for 0% of the time, Pallas kernels for 9%

commit v1 on v0

--- a/solution.py
+++ b/solution.py
@@ -123,17 +123,31 @@
     return full_ref[:, pl.ds(pl.multiple_of(info_ref[0] * H, H), H)]
 
 
-def call(kernel, outs, operands, scratch, flops, limit=32):
-    moved = sum(o.size * 4 for o in operands) + sum(4 * jnp.zeros(o, F32).size for o in outs)
-    return pl.pallas_call(
-        kernel,
-        out_shape=[jax.ShapeDtypeStruct(o, F32) for o in outs],
-        in_specs=[SMEM] + [VMEM] * (len(operands) - 1),
-        out_specs=[VMEM] * len(outs),
-        scratch_shapes=[pltpu.VMEM(s, F32) for s in scratch],
-        compiler_params=pltpu.CompilerParams(vmem_limit_bytes=limit * 2**20),
-        cost_estimate=pl.CostEstimate(flops=flops, bytes_accessed=moved, transcendentals=0),
-    )(*operands)
+B = 128
+PACK = ((0, 0), (1, 0), (1, 1), (2, 0), (2, 1)), ((2, 2), (3, 0), (3, 1), (3, 2), (3, 3))
+PACKED = (5 * B, B)
+
+
+def pack(info_ref, full_ref, out_ref):
+    for core in range(2):
+
+        @pl.when(info_ref[0] == core)
+        def _():
+            for at, (i, j) in enumerate(PACK[core]):
+                out_ref[at * B : (at + 1) * B, :] = full_ref[i * B : (i + 1) * B, j * B : (j + 1) * B]
+
+
+def unpack(info_ref, own_ref, other_ref, full_ref):
+    for core in range(2):
+
+        @pl.when(info_ref[0] == core)
+        def _():
+            for half, ref in ((core, own_ref), (1 - core, other_ref)):
+                for at, (i, j) in enumerate(PACK[half]):
+                    block = ref[at * B : (at + 1) * B, :]
+                    full_ref[i * B : (i + 1) * B, j * B : (j + 1) * B] = block
+                    if i != j:
+                        full_ref[j * B : (j + 1) * B, i * B : (i + 1) * B] = block.T
 
 
 CUBE = 2 * N * N * N
@@ -142,44 +156,69 @@
 PAIR = (2, H, N)
 
 
+def call(kernel, outs, operands, scratch, cubes, after=(), limit=32):
+    count = len(operands)
+
+    def entry(*refs):
+        kernel(*refs[:count], *refs[count + len(after) :])
+
+    return pl.pallas_call(
+        entry,
+        out_shape=[jax.ShapeDtypeStruct(o, F32) for o in outs],
+        in_specs=[SMEM] + [VMEM] * (count - 1) + [pl.BlockSpec(memory_space=pl.ANY)] * len(after),
+        out_specs=[VMEM] * len(outs),
+        scratch_shapes=[pltpu.VMEM(s, F32) for s in scratch],
+        compiler_params=pltpu.CompilerParams(vmem_limit_bytes=limit * 2**20),
+        cost_estimate=pl.CostEstimate(
+            flops=cubes * CUBE, bytes_accessed=(count + len(outs)) * 4 * H * N, transcendentals=0
+        ),
+    )(*operands, *after)
+
+
 def first_inverse(info, own, other):
-    def kernel(info_ref, own_ref, other_ref, z_ref, zc_ref, d_ref, res_ref):
+    def kernel(info_ref, own_ref, other_ref, z_ref, d_ref, res_ref):
         join(info_ref, own_ref, other_ref, d_ref)
         invert(d_ref, z_ref, res_ref)
-        zc_ref[...] = own_rows(info_ref, z_ref)
-
-    return call(kernel, [FULL, SLAB], [info, own, other], [FULL, FULL], 20 * CUBE)
-
-
-def left_updates(info, z, uo, uo_other, de, de_other, fe, fo):
-    def kernel(info_ref, z_ref, uo_ref, uox_ref, de_ref, dex_ref, fe_ref, fo_ref, a_ref, b_ref, u_ref):
+
+    return call(kernel, [FULL], [info, own, other], [FULL, FULL], 20)[0]
+
+
+def left_updates(info, z, uo, uo_other, de, de_other, fe, fo, after):
+    def kernel(
+        info_ref, z_ref, uo_ref, uox_ref, de_ref, dex_ref, fe_ref, fo_ref,
+        a_ref, b_ref, v_ref, g_ref, zp_ref, u_ref,
+    ):
+        pack(info_ref, z_ref, zp_ref)
         join(info_ref, uo_ref, uox_ref, u_ref)
         join(info_ref, de_ref, dex_ref, a_ref)
         z2 = halves(z_ref[...])
         u2 = halves(u_ref[...])
         v = dot3(u2, z2)
+        v_ref[...] = v
         a_ref[...] = a_ref[...] - dot3(halves(v), u2, NT)
         g = dot3(halves(fo_ref[...]), z2)
+        g_ref[...] = g
         b_ref[...] = fe_ref[...] - dot3(halves(g), u2, NT)
 
     return call(
-        kernel, [FULL, SLAB], [info, z, uo, uo_other, de, de_other, fe, fo], [FULL], 9 * CUBE
+        kernel, [FULL, SLAB, FULL, SLAB, PACKED], [info, z, uo, uo_other, de, de_other, fe, fo],
+        [FULL], 9, after,
     )
 
 
 def coupled_upper(info, zq, zq_other, ue, ue_other, uq):
     def kernel(info_ref, zq_ref, zqx_ref, ue_ref, uex_ref, uq_ref, un_ref, z_ref, u_ref):
-        join(info_ref, zq_ref, zqx_ref, z_ref)
+        unpack(info_ref, zq_ref, zqx_ref, z_ref)
         join(info_ref, ue_ref, uex_ref, u_ref)
         v = dot3(halves(uq_ref[...]), halves(z_ref[...]))
         fresh = -dot3(halves(v), halves(u_ref[...]))
         un_ref[...] = jnp.where(info_ref[1] > 0, fresh, ue_ref[...])
 
-    return call(kernel, [SLAB, FULL, FULL], [info, zq, zq_other, ue, ue_other, uq], [], 3 * CUBE)
+    return call(kernel, [SLAB, FULL, FULL], [info, zq, zq_other, ue, ue_other, uq], [], 3)
 
 
 def second_inverse(info, a, zq, u):
-    def kernel(info_ref, a_ref, zq_ref, u_ref, dc_ref, z_ref, zc_ref, d_ref, res_ref):
+    def kernel(info_ref, a_ref, zq_ref, u_ref, dc_ref, z_ref, zp_ref, d_ref, res_ref):
         u2 = halves(u_ref[...])
         w = dot3(u2, halves(zq_ref[...]), TN)
         d_ref[...] = a_ref[...] - dot3(halves(w), u2)
@@ -188,26 +227,29 @@
         @pl.when(info_ref[2] > 0)
         def _():
             invert(d_ref, z_ref, res_ref)
-            zc_ref[...] = own_rows(info_ref, z_ref)
-
-    return call(kernel, [SLAB, FULL, SLAB], [info, a, zq, u], [FULL, FULL], 26 * CUBE)
-
-
-def level0_sources(info, b, fq, zq, u):
-    def kernel(info_ref, b_ref, fq_ref, zq_ref, u_ref, f_ref):
-        g = dot3(halves(fq_ref[...]), halves(zq_ref[...]))
-        f_ref[...] = b_ref[...] - dot3(halves(g), halves(u_ref[...]))
-
-    return call(kernel, [SLAB], [info, b, fq, zq, u], [], 3 * CUBE)[0]
-
-
-def solved_sources(info, f, z):
-    def kernel(info_ref, f_ref, z_ref, g_ref):
+            pack(info_ref, z_ref, zp_ref)
+
+    return call(kernel, [SLAB, FULL, PACKED], [info, a, zq, u], [FULL, FULL], 26)
+
+
+def odd_sources(info, b, fq, zq, u, z, go, v, after):
+    def kernel(
+        info_ref, b_ref, fq_ref, zq_ref, u_ref, z_ref, go_ref, v_ref, f_ref, g_ref, gt_ref,
+    ):
         @pl.when(info_ref[2] > 0)
         def _():
-            g_ref[...] = dot3(halves(f_ref[...]), halves(z_ref[...]))
-
-    return call(kernel, [SLAB], [info, f, z], [], CUBE)[0]
+            gq = dot3(halves(fq_ref[...]), halves(zq_ref[...]))
+            f = b_ref[...] - dot3(halves(gq), halves(u_ref[...]))
+            f_ref[...] = f
+            g = dot3(halves(f), halves(z_ref[...]))
+            g_ref[...] = g
+            gt_ref[...] = go_ref[...] - dot3(halves(g), halves(v_ref[...]))
+
+        @pl.when(info_ref[2] == 0)
+        def _():
+            f_ref[...] = b_ref[...]
+
+    return call(kernel, [SLAB, SLAB, SLAB], [info, b, fq, zq, u, z, go, v], [], 6, after)
 
 
 def level1_blocks(info, d, u_mid, u_mid_other, right, left, d_in, u_in):
@@ -230,8 +272,8 @@
         def _():
             join(info_ref, um_ref, umx_ref, mid_ref)
             join(info_ref, ur_ref, urx_ref, far_ref)
-            join(info_ref, zr_ref, zrx_ref, zr_full)
-            join(info_ref, zl_ref, zlx_ref, zl_full)
+            unpack(info_ref, zr_ref, zrx_ref, zr_full)
+            unpack(info_ref, zl_ref, zlx_ref, zl_full)
             mid = halves(mid_ref[...])
             zl2 = halves(zl_full[...])
             v = dot3(halves(ur_ref[...]), halves(zr_full[...]))
@@ -244,12 +286,12 @@
     return call(
         kernel, [PAIR, PAIR],
         [info, d, u_mid, u_mid_other, ur, urx, zr, zrx, ul, zl, zlx, d_in, u_in],
-        [FULL] * 4, 9 * CUBE,
+        [FULL] * 4, 9,
     )
 
 
-def level1_sources(info, f, gr, ur, urx, gl, u_mid, u_mid_other, f_in):
-    def kernel(info_ref, f_ref, gr_ref, ur_ref, urx_ref, gl_ref, um_ref, umx_ref, fin_ref, out_ref, mid_ref, far_ref):
+def level1_sources(info, f, gr, ur, urx, gl, ue_full, f_in, after):
+    def kernel(info_ref, f_ref, gr_ref, ur_ref, urx_ref, gl_ref, ue_ref, fin_ref, out_ref, far_ref):
         out_ref[1] = fin_ref[1]
 
         @pl.when(info_ref[2] > 0)
@@ -258,17 +300,14 @@
 
         @pl.when(info_ref[2] == 0)
         def _():
-            join(info_ref, um_ref, umx_ref, mid_ref)
             join(info_ref, ur_ref, urx_ref, far_ref)
             out_ref[0] = (
                 f_ref[...]
                 - dot3(halves(gr_ref[...]), halves(far_ref[...]), NT)
-                - dot3(halves(gl_ref[...]), halves(mid_ref[...]))
+                - dot3(halves(gl_ref[...]), halves(ue_ref[...]))
             )
 
-    return call(
-        kernel, [PAIR], [info, f, gr, ur, urx, gl, u_mid, u_mid_other, f_in], [FULL, FULL], 3 * CUBE
-    )[0]
+    return call(kernel, [PAIR], [info, f, gr, ur, urx, gl, ue_full, f_in], [FULL], 3, after)[0]
 
 
 def body(diagonal_blocks, upper_blocks, right_sides):
@@ -279,41 +318,40 @@
     def swap(a):
         return lax.ppermute(a, "col", [(0, 1), (1, 0)])
 
-    def onward(a):
-        return lax.ppermute(a, "tm", [(i, i + 1) for i in range(chips - 1)])
+    def onward(a, first=0, step=1):
+        return lax.ppermute(a, "tm", [(i, i + 1) for i in range(first, chips - 1, step)])
 
     def odd_left(a):
         return lax.ppermute(a, "tm", [(i, i - 1) for i in range(1, chips, 2)])
 
     def odd_right(a):
-        return lax.ppermute(a, "tm", [(i, i + 1) for i in range(1, chips - 1, 2)])
+        return onward(a, 1, 2)
 
     de, do = diagonal_blocks[0], diagonal_blocks[1]
     ue, uo = upper_blocks[0], upper_blocks[1]
     fe, fo = right_sides[0], right_sides[1]
 
     uq = onward(uo)
-    zo, zo_own = first_inverse(info, do, swap(do))
-    zq = onward(zo_own)
-    fq = onward(fo)
-    a, b = left_updates(info, zo, uo, swap(uo), de, swap(de), fe, fo)
+    zo = first_inverse(info, do, swap(do))
+    a, b, vo, go, zo_packed = left_updates(info, zo, uo, swap(uo), de, swap(de), fe, fo, (uq,))
+    zq = onward(zo_packed)
+    fq = onward(fo, 0, 2)
     u_mid, zq_full, ue_full = coupled_upper(info, zq, swap(zq), ue, swap(ue), uq)
     ur = odd_left(u_mid)
     ul = odd_right(u_mid)
     u_mid_other = swap(u_mid)
-    d_mid, z1, z1_own = second_inverse(info, a, zq_full, ue_full)
-    zr = odd_left(z1_own)
-    zl = odd_right(z1_own)
-    f_mid = level0_sources(info, b, fq, zq_full, ue_full)
-    g1 = solved_sources(info, f_mid, z1)
+    d_mid, z1, z1_packed = second_inverse(info, a, zq_full, ue_full)
+    zr = odd_left(z1_packed)
+    zl = odd_right(z1_packed)
+    f_mid, g1, gt = odd_sources(info, b, fq, zq_full, ue_full, z1, go, vo, (ur, ul, u_mid_other))
     gr = odd_left(g1)
-    gl = odd_right(g1)
+    gl = odd_right(gt)
     urx = swap(ur)
     d_out, u_out = level1_blocks(
         info, d_mid, u_mid, u_mid_other, (ur, urx, zr, swap(zr)), (ul, zl, swap(zl)),
         diagonal_blocks, upper_blocks,
     )
-    f_out = level1_sources(info, f_mid, gr, ur, urx, gl, u_mid, u_mid_other, right_sides)
+    f_out = level1_sources(info, f_mid, gr, ur, urx, gl, ue_full, right_sides, (d_out,))
     return d_out, u_out, f_out
 
 

time: 111 us -> 106 us (0.955)
  waiting for transfers between devices: 64.2 us -> 58.1 us
  local copies, waits for them, and re-layouts: 1.43 us -> 4.32 us
  starting transfers between devices: 18 us -> 15.5 us
    ppermute x3, waiting for transfers between devices: 29.5 us -> 23.2 us  [odd_left(): return lax.ppermute(a, 'tm', [(i, i - 1) for i in range(1, chips, 2)])]
    ppermute x6, starting transfers between devices: 12.7 us -> 10.5 us  [onward(): lax.ppermute(a, 'tm', [(i, i + 1) for i in range(first, chips - 1, step)])]
    ppermute x6, waiting for transfers between devices: 32.8 us -> 34.6 us  [onward(): lax.ppermute(a, 'tm', [(i, i + 1) for i in range(first, chips - 1, step)])]
    ppermute x9, waiting for transfers between devices: 1.83 us -> 0.32 us  [swap(): return lax.ppermute(a, 'col', [(0, 1), (1, 0)])]
    unnamed x6 -> x8, local copies, waits for them, and re-layouts: 0.02 us -> 1.24 us
    pallas_call x8 -> x7, Pallas kernels: 26.4 us -> 27 us  [call(): pl.pallas_call(entry, out_shape=[jax.ShapeDtypeStruct(o, F32) for o in ou...]
  transfers between devices with their start and end apart: 18 -> 18, of which waited for: 8 -> 9; matrix products, arithmetic and copies ran while one was open for 0% -> 1% of each run, Pallas kernels for 9% -> 19%
where the time goes in v1:
time: 106 us
  waiting for transfers between devices  58.1 us (55%)
  Pallas kernels  27 us (25%)
  starting transfers between devices  15.5 us (15%)
  local copies, waits for them, and re-layouts  4.32 us (4%)
    ppermute x6, waiting for transfers between devices, onward(): lax.ppermute(a, 'tm', [(i, i + 1) for i in range(first, chips - 1, step)])  34.6 us
    pallas_call x7, Pallas kernels, call(): pl.pallas_call(entry, out_shape=[jax.ShapeDtypeStruct(o, F32) for o in ou...  27 us
    ppermute x3, waiting for transfers between devices, odd_left(): return lax.ppermute(a, 'tm', [(i, i - 1) for i in range(1, chips, 2)])  23.2 us
    ppermute x6, starting transfers between devices, onward(): lax.ppermute(a, 'tm', [(i, i + 1) for i in range(first, chips - 1, step)])  10.5 us
    ppermute x3, starting transfers between devices, odd_left(): return lax.ppermute(a, 'tm', [(i, i - 1) for i in range(1, chips, 2)])  4.04 us
    squeeze x1, local copies, waits for them, and re-layouts, body(): de, do = (diagonal_blocks[0], diagonal_blocks[1])  2.15 us
  transfers between devices with their start and end apart: 18, of which 9 were waited for; matrix products, arithmetic and copies ran while one was open for 1% of the time, Pallas kernels for 19%

profile of v1, /device:TPU:64, one launch (start us, length us, event | category | flops | bytes accessed | tf_op | source)
XLA Modules:
  0.0 105.8 jit_solution(7892040325537407856)
XLA Ops:
  0.6 0.0 copy-start.2
  0.6 2.1 %slice_bitcast_fusion.3 = (f32[256,512]{1,0:T(8,128)S(1)}, f32[256,512]{1,0:T(8,128)}) fusion(f32[2,256,512]{2,1,0:T(8,128)} %refs_11_.1), kind=kLoop, calls=%fused_computation.3 | loop fusion | bytes 2097152 | tf_op jit(solution)/shard_map/squeeze | solution.py:330
  2.8 0.0 copy-start
  2.8 0.0 collective-permute-start
  2.8 0.0 copy-done.2
  2.8 0.9 slice_bitcast_fusion
  3.7 3.4 %collective-permute-start.3 = (f32[256,512]{1,0:T(8,128)}, f32[256,512]{1,0:T(8,128)}, u32[]{:S(2)}, u32[]{:S(2)}) collective-permute-start(f32[256,512]{1,0:T(8,128)} %get-tuple-element.36.refs_2_), channel_id=1, source_target_pairs={{0,2},{2,4},{4,6},{6,8},{8,10},{10,12},{12,14},{14,16},{16,18},{18... | collective-permute-start | bytes 1572872 | tf_op jit(solution)/shard_map/ppermute | solution.py:322
  7.1 0.3 collective-permute-start.1
  7.4 0.3 collective-permute-start.2
  7.7 0.0 copy-done
  7.7 0.1 slice_bitcast_fusion.1
  7.7 0.1 pad_add_fusion.refs_0_
  7.8 0.0 collective-permute-done.refs_2_
  7.8 9.4 %shard_map.58.refs_1_ = f32[512,512]{1,0:T(8,128)S(1)} custom-call(s32[3]{0:T(128)S(1)} %pad_add_fusion.refs_0_, f32[256,512]{1,0:T(8,128)} %get-tuple-element.40.refs_1_, f32[256,512]{1,0:T(8,128)} %collective-permute-done.refs_2_), custom_call_target="tpu_custom_call" | custom-call | flops 5368709120 | bytes 2097152 | tf_op jit(solution)/shard_map/pallas_call | solution.py:165
  17.2 7.2 %collective-permute-done.3.refs_8_.refs_5_ = f32[256,512]{1,0:T(8,128)} collective-permute-done((f32[256,512]{1,0:T(8,128)}, f32[256,512]{1,0:T(8,128)}, u32[]{:S(2)}, u32[]{:S(2)}) %collective-permute-start.3) | collective-permute-done | bytes 524320 | tf_op jit(solution)/shard_map/ppermute | solution.py:322
  24.4 0.0 collective-permute-done.1.refs_3_
  24.4 0.0 collective-permute-done.2.refs_5_
  24.4 4.2 %shard_map.59 = (f32[512,512]{1,0:T(8,128)S(1)}, f32[256,512]{1,0:T(8,128)S(1)}, f32[512,512]{1,0:T(8,128)S(1)}, f32[256,512]{1,0:T(8,128)S(1)}, f32[640,128]{1,0:T(8,128)S(1)}) custom-call(s32[3]{0:T(128)S(1)} %pad_add_fusion.refs_0_, f32[512,512]{1,0:T(8,128)S(1)} %shard_map.58.refs_1_, f32[256,512]{1,0:T(8,128)} %get-tuple-element.36.refs_2_, ...), custom_call_target="tpu_custom_call" | custom-call | flops 2415919104 | bytes 6815744 | tf_op jit(solution)/shard_map/pallas_call | solution.py:165
  28.7 1.9 %collective-permute-start.4 = (f32[640,128]{1,0:T(8,128)S(1)}, f32[640,128]{1,0:T(8,128)S(1)}, u32[]{:S(2)}, u32[]{:S(2)}) collective-permute-start(f32[640,128]{1,0:T(8,128)S(1)} %get-tuple-element.20), channel_id=1, source_target_pairs={{0,2},{2,4},{4,6},{6,8},{8,10},{10,12},{12,14},{14,16},{16,18},{18... | collective-permute-start | bytes 983048 | tf_op jit(solution)/shard_map/ppermute | solution.py:322
  30.6 0.1 collective-permute-start.6
  30.7 13.4 %collective-permute-done.4.refs_1_ = f32[640,128]{1,0:T(8,128)S(1)} collective-permute-done((f32[640,128]{1,0:T(8,128)S(1)}, f32[640,128]{1,0:T(8,128)S(1)}, u32[]{:S(2)}, u32[]{:S(2)}) %collective-permute-start.4) | collective-permute-done | bytes 327712 | tf_op jit(solution)/shard_map/ppermute | solution.py:322
  44.1 0.0 collective-permute-start.5
  44.1 1.3 %collective-permute-start.15 = (f32[256,512]{1,0:T(8,128)S(1)}, f32[256,512]{1,0:T(8,128)S(1)}, u32[]{:S(2)}, u32[]{:S(2)}) collective-permute-start(f32[256,512]{1,0:T(8,128)S(1)} %get-tuple-element.37.refs_7_), channel_id=1, source_target_pairs={{0,2},{4,6},{8,10},{12,14},{16,18},{20,22},{24,26},{28,30},{32,34}... | collective-permute-start | bytes 1572872 | tf_op jit(solution)/shard_map/ppermute | solution.py:322
  45.4 0.0 collective-permute-done.6.refs_4_
  45.5 0.3 collective-permute-done.5.refs_2_
  45.7 2.4 %shard_map.60 = (f32[256,512]{1,0:T(8,128)S(1)}, f32[512,512]{1,0:T(8,128)S(1)}, f32[512,512]{1,0:T(8,128)S(1)}) custom-call(s32[3]{0:T(128)S(1)} %pad_add_fusion.refs_0_, f32[640,128]{1,0:T(8,128)S(1)} %collective-permute-done.4.refs_1_, f32[640,128]{1,0:T(8,128)S(1)} %collective-permute-done.5.refs_2_, f32[256,512]{1,0:T(8,128)S(1)} %get-tuple-element.35.refs_3_, ...), custom_call_target="tpu_custom_call" | custom-call | flops 805306368 | bytes 4718592 | tf_op jit(solution)/shard_map/pallas_call | solution.py:165
  48.1 1.3 %collective-permute-start.12 = (f32[256,512]{1,0:T(8,128)S(1)}, f32[256,512]{1,0:T(8,128)S(1)}, u32[]{:S(2)}, u32[]{:S(2)}) collective-permute-start(f32[256,512]{1,0:T(8,128)S(1)} %get-tuple-element.24.refs_2_), channel_id=1, source_target_pairs={{2,4},{6,8},{10,12},{14,16},{18,20},{22,24},{26,28},{30,32},{34,36... | collective-permute-start | bytes 1572872 | tf_op jit(solution)/shard_map/ppermute | solution.py:322
  49.4 0.3 collective-permute-start.7
  49.7 1.5 %collective-permute-start.8 = (f32[256,512]{1,0:T(8,128)S(1)}, f32[256,512]{1,0:T(8,128)S(1)}, u32[]{:S(2)}, u32[]{:S(2)}) collective-permute-start(f32[256,512]{1,0:T(8,128)S(1)} %get-tuple-element.24.refs_2_), channel_id=1, source_target_pairs={{2,0},{6,4},{10,8},{14,12},{18,16},{22,20},{26,24},{30,28},{34,32}... | collective-permute-start | bytes 1572872 | tf_op jit(solution)/shard_map/ppermute | solution.py:325
  51.2 2.4 %shard_map.61 = (f32[256,512]{1,0:T(8,128)S(1)}, f32[512,512]{1,0:T(8,128)S(1)}, f32[640,128]{1,0:T(8,128)S(1)}) custom-call(s32[3]{0:T(128)S(1)} %pad_add_fusion.refs_0_, f32[512,512]{1,0:T(8,128)S(1)} %get-tuple-element.19.refs_1_, f32[512,512]{1,0:T(8,128)S(1)} %get-tuple-element.21.refs_2_.refs_3_, f32[512,512]{1,0:T(8,128)S(1)} %get-tuple-element.22.refs_3_.refs_4_.refs_6_), custom_call_target="tpu_custom_call" | custom-call | flops 6979321856 | bytes 3670016 | tf_op jit(solution)/shard_map/pallas_call | solution.py:165
  53.7 1.3 %collective-permute-start.10 = (f32[640,128]{1,0:T(8,128)S(1)}, f32[640,128]{1,0:T(8,128)S(1)}, u32[]{:S(2)}, u32[]{:S(2)}) collective-permute-start(f32[640,128]{1,0:T(8,128)S(1)} %get-tuple-element.25), channel_id=1, source_target_pairs={{2,0},{6,4},{10,8},{14,12},{18,16},{22,20},{26,24},{30,28},{34,32}... | collective-permute-start | bytes 983048 | tf_op jit(solution)/shard_map/ppermute | solution.py:325
  55.0 2.6 %collective-permute-done.15.refs_2_ = f32[256,512]{1,0:T(8,128)S(1)} collective-permute-done((f32[256,512]{1,0:T(8,128)S(1)}, f32[256,512]{1,0:T(8,128)S(1)}, u32[]{:S(2)}, u32[]{:S(2)}) %collective-permute-start.15) | collective-permute-done | bytes 524320 | tf_op jit(solution)/shard_map/ppermute | solution.py:322
  57.5 1.3 %collective-permute-start.13 = (f32[640,128]{1,0:T(8,128)S(1)}, f32[640,128]{1,0:T(8,128)S(1)}, u32[]{:S(2)}, u32[]{:S(2)}) collective-permute-start(f32[640,128]{1,0:T(8,128)S(1)} %get-tuple-element.25), channel_id=1, source_target_pairs={{2,4},{6,8},{10,12},{14,16},{18,20},{22,24},{26,28},{30,32},{34,36... | collective-permute-start | bytes 983048 | tf_op jit(solution)/shard_map/ppermute | solution.py:322
  58.8 6.9 %collective-permute-done.8.refs_4_.refs_8_.refs_3_ = f32[256,512]{1,0:T(8,128)S(1)} collective-permute-done((f32[256,512]{1,0:T(8,128)S(1)}, f32[256,512]{1,0:T(8,128)S(1)}, u32[]{:S(2)}, u32[]{:S(2)}) %collective-permute-start.8) | collective-permute-done | bytes 524320 | tf_op jit(solution)/shard_map/ppermute | solution.py:325
  65.7 0.0 collective-permute-start.9
  65.7 7.9 %collective-permute-done.10.refs_6_ = f32[640,128]{1,0:T(8,128)S(1)} collective-permute-done((f32[640,128]{1,0:T(8,128)S(1)}, f32[640,128]{1,0:T(8,128)S(1)}, u32[]{:S(2)}, u32[]{:S(2)}) %collective-permute-start.10) | collective-permute-done | bytes 327712 | tf_op jit(solution)/shard_map/ppermute | solution.py:325
  73.7 0.0 collective-permute-start.11
  73.7 5.9 %collective-permute-done.13.refs_9_ = f32[640,128]{1,0:T(8,128)S(1)} collective-permute-done((f32[640,128]{1,0:T(8,128)S(1)}, f32[640,128]{1,0:T(8,128)S(1)}, u32[]{:S(2)}, u32[]{:S(2)}) %collective-permute-start.13) | collective-permute-done | bytes 327712 | tf_op jit(solution)/shard_map/ppermute | solution.py:322
  79.5 0.0 collective-permute-start.14
  79.6 0.0 collective-permute-done.12.refs_8_.refs_9_
  79.6 0.0 collective-permute-done.7.refs_3_.refs_10_
  79.6 0.0 copy-start.1
  79.6 0.6 shard_map.63
  80.2 1.3 %collective-permute-start.16 = (f32[256,512]{1,0:T(8,128)S(1)}, f32[256,512]{1,0:T(8,128)S(1)}, u32[]{:S(2)}, u32[]{:S(2)}) collective-permute-start(f32[256,512]{1,0:T(8,128)S(1)} %get-tuple-element.33), channel_id=1, source_target_pairs={{2,0},{6,4},{10,8},{14,12},{18,16},{22,20},{26,24},{30,28},{34,32}... | collective-permute-start | bytes 1572872 | tf_op jit(solution)/shard_map/ppermute | solution.py:325
  81.5 1.3 %collective-permute-start.17 = (f32[256,512]{1,0:T(8,128)S(1)}, f32[256,512]{1,0:T(8,128)S(1)}, u32[]{:S(2)}, u32[]{:S(2)}) collective-permute-start(f32[256,512]{1,0:T(8,128)S(1)} %get-tuple-element.34), channel_id=1, source_target_pairs={{2,4},{6,8},{10,12},{14,16},{18,20},{22,24},{26,28},{30,32},{34,36... | collective-permute-start | bytes 1572872 | tf_op jit(solution)/shard_map/ppermute | solution.py:322
  82.8 0.0 collective-permute-done.11.refs_7_
  82.8 0.0 collective-permute-done.14.refs_10_
  82.8 0.0 collective-permute-done.9.refs_5_.refs_4_
  82.8 0.0 copy-done.1
  82.8 5.2 %shard_map.62 = (f32[2,256,512]{2,1,0:T(8,128)}, f32[2,256,512]{2,1,0:T(8,128)}) custom-call(s32[3]{0:T(128)S(1)} %pad_add_fusion.refs_0_, f32[256,512]{1,0:T(8,128)S(1)} %get-tuple-element.23.refs_1_, f32[256,512]{1,0:T(8,128)S(1)} %get-tuple-element.24.refs_2_, f32[256,512]{1,0:T(8,128)S(1)} %collective-permute-done.7.refs_3_.refs_10_, ...), custom_call_target="tpu_custom_call" | custom-call | flops 2415919104 | bytes 7864320 | tf_op jit(solution)/shard_map/pallas_call | solution.py:165
  88.0 8.3 %collective-permute-done.16.refs_2_ = f32[256,512]{1,0:T(8,128)S(1)} collective-permute-done((f32[256,512]{1,0:T(8,128)S(1)}, f32[256,512]{1,0:T(8,128)S(1)}, u32[]{:S(2)}, u32[]{:S(2)}) %collective-permute-start.16) | collective-permute-done | bytes 524320 | tf_op jit(solution)/shard_map/ppermute | solution.py:325
  96.4 5.5 %collective-permute-done.17.refs_5_ = f32[256,512]{1,0:T(8,128)S(1)} collective-permute-done((f32[256,512]{1,0:T(8,128)S(1)}, f32[256,512]{1,0:T(8,128)S(1)}, u32[]{:S(2)}, u32[]{:S(2)}) %collective-permute-start.17) | collective-permute-done | bytes 524320 | tf_op jit(solution)/shard_map/ppermute | solution.py:322
  101.9 0.0 copy-start.3
  101.9 1.2 %copy-done.3 = f32[2,256,512]{2,1,0:T(8,128)S(1)} copy-done((f32[2,256,512]{2,1,0:T(8,128)S(1)}, f32[2,256,512]{2,1,0:T(8,128)}, u32[]{:S(2)}) %copy-start.3) | copy-done | bytes 1048600
  103.1 2.7 %shard_map.64 = f32[2,256,512]{2,1,0:T(8,128)} custom-call(s32[3]{0:T(128)S(1)} %pad_add_fusion.refs_0_, f32[256,512]{1,0:T(8,128)S(1)} %get-tuple-element.32.refs_1_, f32[256,512]{1,0:T(8,128)S(1)} %collective-permute-done.16.refs_2_, f32[256,512]{1,0:T(8,128)S(1)} %collective-permute-done.8.refs_4_.refs_8_.refs_3_, ...), custom_call_target="tpu_custom_call" | custom-call | flops 805306368 | bytes 4718592 | tf_op jit(solution)/shard_map/pallas_call | solution.py:165
Async XLA Ops:
  0.6 2.2 %copy-start.2 = (f32[2,256,512]{2,1,0:T(8,128)S(1)}, f32[2,256,512]{2,1,0:T(8,128)}, u32[]{:S(2)}) copy-start(f32[2,256,512]{2,1,0:T(8,128)} %refs_12_.1) | copy-start | bytes 3145732
  2.8 4.9 %copy-start = (f32[2,256,512]{2,1,0:T(8,128)S(1)}, f32[2,256,512]{2,1,0:T(8,128)}, u32[]{:S(2)}) copy-start(f32[2,256,512]{2,1,0:T(8,128)} %refs_7_.1) | copy-start | bytes 3145732
  2.8 5.0 %collective-permute-start = (f32[256,512]{1,0:T(8,128)}, f32[256,512]{1,0:T(8,128)}, u32[]{:S(2)}, u32[]{:S(2)}) collective-permute-start(f32[256,512]{1,0:T(8,128)} %get-tuple-element.40.refs_1_), channel_id=1, source_target_pairs={{0,1},{1,0},{2,3},{3,2},{4,5},{5,4},{6,7},{7,6},{8,9},{9,8},{10,11... | collective-permute-start | bytes 1572872 | tf_op jit(solution)/shard_map/ppermute | solution.py:319
  3.7 20.8 %collective-permute-start.3 = (f32[256,512]{1,0:T(8,128)}, f32[256,512]{1,0:T(8,128)}, u32[]{:S(2)}, u32[]{:S(2)}) collective-permute-start(f32[256,512]{1,0:T(8,128)} %get-tuple-element.36.refs_2_), channel_id=1, source_target_pairs={{0,2},{2,4},{4,6},{6,8},{8,10},{10,12},{12,14},{14,16},{16,18},{18... | collective-permute-start | bytes 1572872 | tf_op jit(solution)/shard_map/ppermute | solution.py:322
  7.1 17.4 %collective-permute-start.1 = (f32[256,512]{1,0:T(8,128)}, f32[256,512]{1,0:T(8,128)}, u32[]{:S(2)}, u32[]{:S(2)}) collective-permute-start(f32[256,512]{1,0:T(8,128)} %get-tuple-element.36.refs_2_), channel_id=1, source_target_pairs={{0,1},{1,0},{2,3},{3,2},{4,5},{5,4},{6,7},{7,6},{8,9},{9,8},{10,11... | collective-permute-start | bytes 1572872 | tf_op jit(solution)/shard_map/ppermute | solution.py:319
  7.4 17.1 %collective-permute-start.2 = (f32[256,512]{1,0:T(8,128)S(1)}, f32[256,512]{1,0:T(8,128)}, u32[]{:S(2)}, u32[]{:S(2)}) collective-permute-start(f32[256,512]{1,0:T(8,128)S(1)} %get-tuple-element.39.refs_4_), channel_id=1, source_target_pairs={{0,1},{1,0},{2,3},{3,2},{4,5},{5,4},{6,7},{7,6},{8,9},{9,8},{10,11... | collective-permute-start | bytes 1572872 | tf_op jit(solution)/shard_map/ppermute | solution.py:319
  28.7 15.5 %collective-permute-start.4 = (f32[640,128]{1,0:T(8,128)S(1)}, f32[640,128]{1,0:T(8,128)S(1)}, u32[]{:S(2)}, u32[]{:S(2)}) collective-permute-start(f32[640,128]{1,0:T(8,128)S(1)} %get-tuple-element.20), channel_id=1, source_target_pairs={{0,2},{2,4},{4,6},{6,8},{8,10},{10,12},{12,14},{14,16},{16,18},{18... | collective-permute-start | bytes 983048 | tf_op jit(solution)/shard_map/ppermute | solution.py:322
  30.6 14.9 %collective-permute-start.6 = (f32[256,512]{1,0:T(8,128)S(1)}, f32[256,512]{1,0:T(8,128)S(1)}, u32[]{:S(2)}, u32[]{:S(2)}) collective-permute-start(f32[256,512]{1,0:T(8,128)S(1)} %get-tuple-element.35.refs_3_), channel_id=1, source_target_pairs={{0,1},{1,0},{2,3},{3,2},{4,5},{5,4},{6,7},{7,6},{8,9},{9,8},{10,11... | collective-permute-start | bytes 1572872 | tf_op jit(solution)/shard_map/ppermute | solution.py:319
  44.1 1.6 %collective-permute-start.5 = (f32[640,128]{1,0:T(8,128)S(1)}, f32[640,128]{1,0:T(8,128)S(1)}, u32[]{:S(2)}, u32[]{:S(2)}) collective-permute-start(f32[640,128]{1,0:T(8,128)S(1)} %collective-permute-done.4.refs_1_), channel_id=1, source_target_pairs={{0,1},{1,0},{2,3},{3,2},{4,5},{5,4},{6,7},{7,6},{8,9},{9,8},{10,11... | collective-permute-start | bytes 983048 | tf_op jit(solution)/shard_map/ppermute | solution.py:319
  44.1 13.4 %collective-permute-start.15 = (f32[256,512]{1,0:T(8,128)S(1)}, f32[256,512]{1,0:T(8,128)S(1)}, u32[]{:S(2)}, u32[]{:S(2)}) collective-permute-start(f32[256,512]{1,0:T(8,128)S(1)} %get-tuple-element.37.refs_7_), channel_id=1, source_target_pairs={{0,2},{4,6},{8,10},{12,14},{16,18},{20,22},{24,26},{28,30},{32,34}... | collective-permute-start | bytes 1572872 | tf_op jit(solution)/shard_map/ppermute | solution.py:322
  48.1 31.4 %collective-permute-start.12 = (f32[256,512]{1,0:T(8,128)S(1)}, f32[256,512]{1,0:T(8,128)S(1)}, u32[]{:S(2)}, u32[]{:S(2)}) collective-permute-start(f32[256,512]{1,0:T(8,128)S(1)} %get-tuple-element.24.refs_2_), channel_id=1, source_target_pairs={{2,4},{6,8},{10,12},{14,16},{18,20},{22,24},{26,28},{30,32},{34,36... | collective-permute-start | bytes 1572872 | tf_op jit(solution)/shard_map/ppermute | solution.py:322
  49.4 30.1 %collective-permute-start.7 = (f32[256,512]{1,0:T(8,128)S(1)}, f32[256,512]{1,0:T(8,128)S(1)}, u32[]{:S(2)}, u32[]{:S(2)}) collective-permute-start(f32[256,512]{1,0:T(8,128)S(1)} %get-tuple-element.24.refs_2_), channel_id=1, source_target_pairs={{0,1},{1,0},{2,3},{3,2},{4,5},{5,4},{6,7},{7,6},{8,9},{9,8},{10,11... | collective-permute-start | bytes 1572872 | tf_op jit(solution)/shard_map/ppermute | solution.py:319
  49.7 16.0 %collective-permute-start.8 = (f32[256,512]{1,0:T(8,128)S(1)}, f32[256,512]{1,0:T(8,128)S(1)}, u32[]{:S(2)}, u32[]{:S(2)}) collective-permute-start(f32[256,512]{1,0:T(8,128)S(1)} %get-tuple-element.24.refs_2_), channel_id=1, source_target_pairs={{2,0},{6,4},{10,8},{14,12},{18,16},{22,20},{26,24},{30,28},{34,32}... | collective-permute-start | bytes 1572872 | tf_op jit(solution)/shard_map/ppermute | solution.py:325
  53.7 20.0 %collective-permute-start.10 = (f32[640,128]{1,0:T(8,128)S(1)}, f32[640,128]{1,0:T(8,128)S(1)}, u32[]{:S(2)}, u32[]{:S(2)}) collective-permute-start(f32[640,128]{1,0:T(8,128)S(1)} %get-tuple-element.25), channel_id=1, source_target_pairs={{2,0},{6,4},{10,8},{14,12},{18,16},{22,20},{26,24},{30,28},{34,32}... | collective-permute-start | bytes 983048 | tf_op jit(solution)/shard_map/ppermute | solution.py:325
  57.5 22.0 %collective-permute-start.13 = (f32[640,128]{1,0:T(8,128)S(1)}, f32[640,128]{1,0:T(8,128)S(1)}, u32[]{:S(2)}, u32[]{:S(2)}) collective-permute-start(f32[640,128]{1,0:T(8,128)S(1)} %get-tuple-element.25), channel_id=1, source_target_pairs={{2,4},{6,8},{10,12},{14,16},{18,20},{22,24},{26,28},{30,32},{34,36... | collective-permute-start | bytes 983048 | tf_op jit(solution)/shard_map/ppermute | solution.py:322
  65.7 17.1 %collective-permute-start.9 = (f32[256,512]{1,0:T(8,128)S(1)}, f32[256,512]{1,0:T(8,128)S(1)}, u32[]{:S(2)}, u32[]{:S(2)}) collective-permute-start(f32[256,512]{1,0:T(8,128)S(1)} %collective-permute-done.8.refs_4_.refs_8_.refs_3_), channel_id=1, source_target_pairs={{0,1},{1,0},{2,3},{3,2},{4,5},{5,4},{6,7},{7,6},{8,9},{9,8},{10,11... | collective-permute-start | bytes 1572872 | tf_op jit(solution)/shard_map/ppermute | solution.py:319
  73.7 9.1 %collective-permute-start.11 = (f32[640,128]{1,0:T(8,128)S(1)}, f32[640,128]{1,0:T(8,128)S(1)}, u32[]{:S(2)}, u32[]{:S(2)}) collective-permute-start(f32[640,128]{1,0:T(8,128)S(1)} %collective-permute-done.10.refs_6_), channel_id=1, source_target_pairs={{0,1},{1,0},{2,3},{3,2},{4,5},{5,4},{6,7},{7,6},{8,9},{9,8},{10,11... | collective-permute-start | bytes 983048 | tf_op jit(solution)/shard_map/ppermute | solution.py:319
  79.5 3.2 %collective-permute-start.14 = (f32[640,128]{1,0:T(8,128)S(1)}, f32[640,128]{1,0:T(8,128)S(1)}, u32[]{:S(2)}, u32[]{:S(2)}) collective-permute-start(f32[640,128]{1,0:T(8,128)S(1)} %collective-permute-done.13.refs_9_), channel_id=1, source_target_pairs={{0,1},{1,0},{2,3},{3,2},{4,5},{5,4},{6,7},{7,6},{8,9},{9,8},{10,11... | collective-permute-start | bytes 983048 | tf_op jit(solution)/shard_map/ppermute | solution.py:319
  79.6 3.2 %copy-start.1 = (f32[2,256,512]{2,1,0:T(8,128)S(1)}, f32[2,256,512]{2,1,0:T(8,128)}, u32[]{:S(2)}) copy-start(f32[2,256,512]{2,1,0:T(8,128)} %refs_11_.1) | copy-start | bytes 3145732
  80.2 16.2 %collective-permute-start.16 = (f32[256,512]{1,0:T(8,128)S(1)}, f32[256,512]{1,0:T(8,128)S(1)}, u32[]{:S(2)}, u32[]{:S(2)}) collective-permute-start(f32[256,512]{1,0:T(8,128)S(1)} %get-tuple-element.33), channel_id=1, source_target_pairs={{2,0},{6,4},{10,8},{14,12},{18,16},{22,20},{26,24},{30,28},{34,32}... | collective-permute-start | bytes 1572872 | tf_op jit(solution)/shard_map/ppermute | solution.py:325
  81.5 20.4 %collective-permute-start.17 = (f32[256,512]{1,0:T(8,128)S(1)}, f32[256,512]{1,0:T(8,128)S(1)}, u32[]{:S(2)}, u32[]{:S(2)}) collective-permute-start(f32[256,512]{1,0:T(8,128)S(1)} %get-tuple-element.34), channel_id=1, source_target_pairs={{2,4},{6,8},{10,12},{14,16},{18,20},{22,24},{26,28},{30,32},{34,36... | collective-permute-start | bytes 1572872 | tf_op jit(solution)/shard_map/ppermute | solution.py:322
  101.9 1.2 %copy-start.3 = (f32[2,256,512]{2,1,0:T(8,128)S(1)}, f32[2,256,512]{2,1,0:T(8,128)}, u32[]{:S(2)}) copy-start(f32[2,256,512]{2,1,0:T(8,128)} %get-tuple-element.16.refs_8_) | copy-start | bytes 3145732

commit v2 on v1

--- a/solution.py
+++ b/solution.py
@@ -156,15 +156,16 @@
 PAIR = (2, H, N)
 
 
-def call(kernel, outs, operands, scratch, cubes, after=(), limit=32):
+def call(kernel, outs, operands, scratch, cubes, after=(), rounded=(), limit=24):
     count = len(operands)
+    outs = [(o, F32) for o in outs] + [(o, BF16) for o in rounded]
 
     def entry(*refs):
         kernel(*refs[:count], *refs[count + len(after) :])
 
     return pl.pallas_call(
         entry,
-        out_shape=[jax.ShapeDtypeStruct(o, F32) for o in outs],
+        out_shape=[jax.ShapeDtypeStruct(o, kind) for o, kind in outs],
         in_specs=[SMEM] + [VMEM] * (count - 1) + [pl.BlockSpec(memory_space=pl.ANY)] * len(after),
         out_specs=[VMEM] * len(outs),
         scratch_shapes=[pltpu.VMEM(s, F32) for s in scratch],
@@ -175,46 +176,42 @@
     )(*operands, *after)
 
 
-def first_inverse(info, own, other):
-    def kernel(info_ref, own_ref, other_ref, z_ref, d_ref, res_ref):
-        join(info_ref, own_ref, other_ref, d_ref)
+def first_inverse(info, d, d_other):
+    def kernel(info_ref, own_ref, other_ref, z_ref, zp_ref, d_ref, res_ref):
+        join(info_ref, own_ref.at[1], other_ref.at[1], d_ref)
         invert(d_ref, z_ref, res_ref)
-
-    return call(kernel, [FULL], [info, own, other], [FULL, FULL], 20)[0]
-
-
-def left_updates(info, z, uo, uo_other, de, de_other, fe, fo, after):
-    def kernel(
-        info_ref, z_ref, uo_ref, uox_ref, de_ref, dex_ref, fe_ref, fo_ref,
-        a_ref, b_ref, v_ref, g_ref, zp_ref, u_ref,
-    ):
         pack(info_ref, z_ref, zp_ref)
-        join(info_ref, uo_ref, uox_ref, u_ref)
-        join(info_ref, de_ref, dex_ref, a_ref)
+
+    return call(kernel, [FULL, PACKED], [info, d, d_other], [FULL, FULL], 20)
+
+
+def left_updates(info, z, u, u_other, d, d_other, f, after):
+    def kernel(info_ref, z_ref, u_ref, ux_ref, d_ref, dx_ref, f_ref, a_ref, b_ref, v_ref, g_ref, uo_ref):
+        join(info_ref, u_ref.at[1], ux_ref.at[1], uo_ref)
+        join(info_ref, d_ref.at[0], dx_ref.at[0], a_ref)
         z2 = halves(z_ref[...])
-        u2 = halves(u_ref[...])
+        u2 = halves(uo_ref[...])
+        g = dot3(halves(f_ref[1]), z2)
+        g_ref[...] = g
+        b_ref[...] = f_ref[0] - dot3(halves(g), u2, NT)
         v = dot3(u2, z2)
         v_ref[...] = v
         a_ref[...] = a_ref[...] - dot3(halves(v), u2, NT)
-        g = dot3(halves(fo_ref[...]), z2)
-        g_ref[...] = g
-        b_ref[...] = fe_ref[...] - dot3(halves(g), u2, NT)
 
     return call(
-        kernel, [FULL, SLAB, FULL, SLAB, PACKED], [info, z, uo, uo_other, de, de_other, fe, fo],
-        [FULL], 9, after,
+        kernel, [FULL, SLAB, FULL, SLAB], [info, z, u, u_other, d, d_other, f], [FULL], 9, after,
     )
 
 
-def coupled_upper(info, zq, zq_other, ue, ue_other, uq):
-    def kernel(info_ref, zq_ref, zqx_ref, ue_ref, uex_ref, uq_ref, un_ref, z_ref, u_ref):
+def coupled_upper(info, zq, zq_other, u, u_other, uq):
+    def kernel(info_ref, zq_ref, zqx_ref, ui_ref, uix_ref, uq_ref, un_ref, z_ref, u_ref):
         unpack(info_ref, zq_ref, zqx_ref, z_ref)
-        join(info_ref, ue_ref, uex_ref, u_ref)
+        join(info_ref, ui_ref.at[0], uix_ref.at[0], u_ref)
         v = dot3(halves(uq_ref[...]), halves(z_ref[...]))
         fresh = -dot3(halves(v), halves(u_ref[...]))
-        un_ref[...] = jnp.where(info_ref[1] > 0, fresh, ue_ref[...])
-
-    return call(kernel, [SLAB, FULL, FULL], [info, zq, zq_other, ue, ue_other, uq], [], 3)
+        un_ref[...] = jnp.where(info_ref[1] > 0, fresh, ui_ref[0])
+
+    return call(kernel, [SLAB, FULL, FULL], [info, zq, zq_other, u, u_other, uq], [], 3)
 
 
 def second_inverse(info, a, zq, u):
@@ -232,14 +229,11 @@
     return call(kernel, [SLAB, FULL, PACKED], [info, a, zq, u], [FULL, FULL], 26)
 
 
-def odd_sources(info, b, fq, zq, u, z, go, v, after):
-    def kernel(
-        info_ref, b_ref, fq_ref, zq_ref, u_ref, z_ref, go_ref, v_ref, f_ref, g_ref, gt_ref,
-    ):
+def odd_sources(info, b, gq, u, z, go, v, after):
+    def kernel(info_ref, b_ref, gq_ref, u_ref, z_ref, go_ref, v_ref, f_ref, g_ref, gt_ref):
         @pl.when(info_ref[2] > 0)
         def _():
-            gq = dot3(halves(fq_ref[...]), halves(zq_ref[...]))
-            f = b_ref[...] - dot3(halves(gq), halves(u_ref[...]))
+            f = b_ref[...] - dot3(halves(gq_ref[...]), halves(u_ref[...]))
             f_ref[...] = f
             g = dot3(halves(f), halves(z_ref[...]))
             g_ref[...] = g
@@ -249,16 +243,16 @@
         def _():
             f_ref[...] = b_ref[...]
 
-    return call(kernel, [SLAB, SLAB, SLAB], [info, b, fq, zq, u, z, go, v], [], 6, after)
-
-
-def level1_blocks(info, d, u_mid, u_mid_other, right, left, d_in, u_in):
+    return call(kernel, [SLAB, SLAB, SLAB], [info, b, gq, u, z, go, v], [], 5, after)
+
+
+def level1_blocks(info, d, u_mid, u_mid_other, right, left, ue, d_in, u_in):
     ur, urx, zr, zrx = right
     ul, zl, zlx = left
 
     def kernel(
         info_ref, d_ref, um_ref, umx_ref, ur_ref, urx_ref, zr_ref, zrx_ref, ul_ref, zl_ref, zlx_ref,
-        din_ref, uin_ref, dout_ref, uout_ref, mid_ref, far_ref, zr_full, zl_full,
+        ue_ref, din_ref, uin_ref, dout_ref, uout_ref, fh_ref, fl_ref, uh_ref, ul2_ref, mid_ref, far_ref, zr_full, zl_full,
     ):
         dout_ref[1] = din_ref[1]
         uout_ref[1] = uin_ref[1]
@@ -274,24 +268,27 @@
             join(info_ref, ur_ref, urx_ref, far_ref)
             unpack(info_ref, zr_ref, zrx_ref, zr_full)
             unpack(info_ref, zl_ref, zlx_ref, zl_full)
+            far = halves(far_ref[...])
+            fh_ref[...], fl_ref[...] = far
+            uh_ref[...], ul2_ref[...] = halves(ue_ref[...])
             mid = halves(mid_ref[...])
             zl2 = halves(zl_full[...])
             v = dot3(halves(ur_ref[...]), halves(zr_full[...]))
             w = dot3(halves(own_columns(info_ref, mid_ref)), zl2, TN)
-            dout_ref[0] = d_ref[...] - dot3(halves(v), halves(far_ref[...]), NT) - dot3(halves(w), mid)
+            dout_ref[0] = d_ref[...] - dot3(halves(v), far, NT) - dot3(halves(w), mid)
             s = dot3(halves(ul_ref[...]), zl2)
             fresh = -dot3(halves(s), mid)
             uout_ref[0] = jnp.where(info_ref[1] > 0, fresh, um_ref[...])
 
     return call(
         kernel, [PAIR, PAIR],
-        [info, d, u_mid, u_mid_other, ur, urx, zr, zrx, ul, zl, zlx, d_in, u_in],
-        [FULL] * 4, 9,
+        [info, d, u_mid, u_mid_other, ur, urx, zr, zrx, ul, zl, zlx, ue, d_in, u_in],
+        [FULL] * 4, 0, rounded=[FULL] * 4,
     )
 
 
-def level1_sources(info, f, gr, ur, urx, gl, ue_full, f_in, after):
-    def kernel(info_ref, f_ref, gr_ref, ur_ref, urx_ref, gl_ref, ue_ref, fin_ref, out_ref, far_ref):
+def level1_sources(info, f, gr, gl, far, ue, f_in):
+    def kernel(info_ref, f_ref, gr_ref, gl_ref, fh_ref, fl_ref, uh_ref, ul_ref, fin_ref, out_ref):
         out_ref[1] = fin_ref[1]
 
         @pl.when(info_ref[2] > 0)
@@ -300,14 +297,13 @@
 
         @pl.when(info_ref[2] == 0)
         def _():
-            join(info_ref, ur_ref, urx_ref, far_ref)
             out_ref[0] = (
                 f_ref[...]
-                - dot3(halves(gr_ref[...]), halves(far_ref[...]), NT)
-                - dot3(halves(gl_ref[...]), halves(ue_ref[...]))
+                - dot3(halves(gr_ref[...]), (fh_ref[...], fl_ref[...]), NT)
+                - dot3(halves(gl_ref[...]), (uh_ref[...], ul_ref[...]))
             )
 
-    return call(kernel, [PAIR], [info, f, gr, ur, urx, gl, ue_full, f_in], [FULL], 3, after)[0]
+    return call(kernel, [PAIR], [info, f, gr, gl, *far, *ue, f_in], [], 3)[0]
 
 
 def body(diagonal_blocks, upper_blocks, right_sides):
@@ -327,31 +323,32 @@
     def odd_right(a):
         return onward(a, 1, 2)
 
-    de, do = diagonal_blocks[0], diagonal_blocks[1]
-    ue, uo = upper_blocks[0], upper_blocks[1]
-    fe, fo = right_sides[0], right_sides[1]
-
-    uq = onward(uo)
-    zo = first_inverse(info, do, swap(do))
-    a, b, vo, go, zo_packed = left_updates(info, zo, uo, swap(uo), de, swap(de), fe, fo, (uq,))
+    d_other = swap(diagonal_blocks)
+    uq = onward(upper_blocks[1])
+    u_other = swap(upper_blocks)
+    zo, zo_packed = first_inverse(info, diagonal_blocks, d_other)
     zq = onward(zo_packed)
-    fq = onward(fo, 0, 2)
-    u_mid, zq_full, ue_full = coupled_upper(info, zq, swap(zq), ue, swap(ue), uq)
+    a, b, vo, go = left_updates(
+        info, zo, upper_blocks, u_other, diagonal_blocks, d_other, right_sides, (uq,)
+    )
+    gq = onward(go, 0, 2)
+    zq, a = lax.optimization_barrier((zq, a))
+    u_mid, zq_full, ue_full = coupled_upper(info, zq, swap(zq), upper_blocks, u_other, uq)
     ur = odd_left(u_mid)
     ul = odd_right(u_mid)
     u_mid_other = swap(u_mid)
     d_mid, z1, z1_packed = second_inverse(info, a, zq_full, ue_full)
     zr = odd_left(z1_packed)
     zl = odd_right(z1_packed)
-    f_mid, g1, gt = odd_sources(info, b, fq, zq_full, ue_full, z1, go, vo, (ur, ul, u_mid_other))
+    f_mid, g1, gt = odd_sources(info, b, gq, ue_full, z1, go, vo, (ur, ul, u_mid_other))
     gr = odd_left(g1)
     gl = odd_right(gt)
     urx = swap(ur)
-    d_out, u_out = level1_blocks(
-        info, d_mid, u_mid, u_mid_other, (ur, urx, zr, swap(zr)), (ul, zl, swap(zl)),
+    d_out, u_out, fh, fl, uh, ul2 = level1_blocks(
+        info, d_mid, u_mid, u_mid_other, (ur, urx, zr, swap(zr)), (ul, zl, swap(zl)), ue_full,
         diagonal_blocks, upper_blocks,
     )
-    f_out = level1_sources(info, f_mid, gr, ur, urx, gl, ue_full, right_sides, (d_out,))
+    f_out = level1_sources(info, f_mid, gr, gl, (fh, fl), (uh, ul2), right_sides)
     return d_out, u_out, f_out
 
 

time: 106 us -> 78.9 us (0.74)
  waiting for transfers between devices: 58.1 us -> 32.6 us
  local copies, waits for them, and re-layouts: 4.32 us -> 1.09 us
  starting transfers between devices: 15.5 us -> 17.2 us
    ppermute x3, waiting for transfers between devices: 23.2 us -> 6.7 us  [odd_left(): return lax.ppermute(a, 'tm', [(i, i - 1) for i in range(1, chips, 2)])]
    ppermute x6, waiting for transfers between devices: 34.6 us -> 24 us  [onward(): lax.ppermute(a, 'tm', [(i, i + 1) for i in range(first, chips - 1, step)])]
    squeeze x3 -> x1, local copies, waits for them, and re-layouts: 3.08 us -> 1.08 us  [body(): uq = onward(upper_blocks[1])]
    ppermute x9 -> x7, waiting for transfers between devices: 0.32 us -> 1.9 us  [swap(): return lax.ppermute(a, 'col', [(0, 1), (1, 0)])]
    ppermute x6, starting transfers between devices: 10.5 us -> 12 us  [onward(): lax.ppermute(a, 'tm', [(i, i + 1) for i in range(first, chips - 1, step)])]
    unnamed x8 -> x6, local copies, waits for them, and re-layouts: 1.24 us -> 0.01 us
  transfers between devices with their start and end apart: 18 -> 16, of which waited for: 9 -> 11; matrix products, arithmetic and copies ran while one was open for 1% -> 1% of each run, Pallas kernels for 19% -> 31%
where the time goes in v2:
time: 78.9 us; the launch traced here: 78.6 us
  waiting for transfers between devices  32.6 us (41%)
  Pallas kernels  26.9 us (34%)
  starting transfers between devices  17.2 us (22%)
  local copies, waits for them, and re-layouts  1.09 us (1%)
  between operations  0.8 us (1%)
    pallas_call x7, Pallas kernels, call(): pl.pallas_call(entry, out_shape=[jax.ShapeDtypeStruct(o, kind) for o, kin...  26.9 us
    ppermute x6, waiting for transfers between devices, onward(): lax.ppermute(a, 'tm', [(i, i + 1) for i in range(first, chips - 1, step)])  24 us
    ppermute x6, starting transfers between devices, onward(): lax.ppermute(a, 'tm', [(i, i + 1) for i in range(first, chips - 1, step)])  12 us
    ppermute x3, waiting for transfers between devices, odd_left(): return lax.ppermute(a, 'tm', [(i, i - 1) for i in range(1, chips, 2)])  6.7 us
    ppermute x3, starting transfers between devices, odd_left(): return lax.ppermute(a, 'tm', [(i, i - 1) for i in range(1, chips, 2)])  3.85 us
    ppermute x7, waiting for transfers between devices, swap(): return lax.ppermute(a, 'col', [(0, 1), (1, 0)])  1.9 us
  transfers between devices with their start and end apart: 16, of which 11 were waited for; matrix products, arithmetic and copies ran while one was open for 1% of the time, Pallas kernels for 31%

profile of v2, /device:TPU:64, one launch (start us, length us, event | category | flops | bytes accessed | tf_op | source)
XLA Modules:
  0.0 78.6 jit_solution(1540729214403638087)
XLA Ops:
  0.6 0.0 copy-start.1
  0.6 0.1 collective-permute-start
  0.7 0.5 collective-permute-start.2
  1.2 1.1 %slice_bitcast_fusion = f32[256,512]{1,0:T(8,128)S(1)} fusion(f32[2,256,512]{2,1,0:T(8,128)} %refs_13_.1), kind=kLoop, calls=%fused_computation | loop fusion | bytes 1048576 | tf_op jit(solution)/shard_map/squeeze | solution.py:327
  2.3 3.4 %collective-permute-start.3 = (f32[256,512]{1,0:T(8,128)S(1)}, f32[256,512]{1,0:T(8,128)S(1)}, u32[]{:S(2)}, u32[]{:S(2)}) collective-permute-start(f32[256,512]{1,0:T(8,128)S(1)} %slice_bitcast_fusion), channel_id=1, source_target_pairs={{0,2},{2,4},{4,6},{6,8},{8,10},{10,12},{12,14},{14,16},{16,18},{18... | collective-permute-start | bytes 1572872 | tf_op jit(solution)/shard_map/ppermute | solution.py:318
  5.7 0.1 pad_add_fusion.refs_0_
  5.8 0.0 copy-start
  5.8 0.0 copy-start.2
  5.8 0.0 collective-permute-done.refs_2_.refs_5_
  5.8 0.0 copy-done.1
  5.8 9.6 %shard_map.58 = (f32[512,512]{1,0:T(8,128)S(1)}, f32[640,128]{1,0:T(8,128)S(1)}) custom-call(s32[3]{0:T(128)S(1)} %pad_add_fusion.refs_0_, f32[2,256,512]{2,1,0:T(8,128)S(1)} %copy-done.1, f32[2,256,512]{2,1,0:T(8,128)} %collective-permute-done.refs_2_.refs_5_), custom_call_target="tpu_custom_call" | custom-call | flops 5368709120 | bytes 2621440 | tf_op jit(solution)/shard_map/pallas_call | solution.py:166
  15.5 3.4 %collective-permute-start.1 = (f32[640,128]{1,0:T(8,128)S(1)}, f32[640,128]{1,0:T(8,128)S(1)}, u32[]{:S(2)}, u32[]{:S(2)}) collective-permute-start(f32[640,128]{1,0:T(8,128)S(1)} %get-tuple-element.26), channel_id=1, source_target_pairs={{0,2},{2,4},{4,6},{6,8},{8,10},{10,12},{12,14},{14,16},{16,18},{18... | collective-permute-start | bytes 983048 | tf_op jit(solution)/shard_map/ppermute | solution.py:318
  18.9 3.5 %collective-permute-done.3.refs_7_.refs_5_ = f32[256,512]{1,0:T(8,128)S(1)} collective-permute-done((f32[256,512]{1,0:T(8,128)S(1)}, f32[256,512]{1,0:T(8,128)S(1)}, u32[]{:S(2)}, u32[]{:S(2)}) %collective-permute-start.3) | collective-permute-done | bytes 524320 | tf_op jit(solution)/shard_map/ppermute | solution.py:318
  22.3 0.0 collective-permute-done.2.refs_3_.refs_4_
  22.3 0.0 copy-done
  22.4 0.0 copy-done.2
  22.4 4.0 %shard_map.59 = (f32[512,512]{1,0:T(8,128)S(1)}, f32[256,512]{1,0:T(8,128)S(1)}, f32[512,512]{1,0:T(8,128)S(1)}, f32[256,512]{1,0:T(8,128)S(1)}) custom-call(s32[3]{0:T(128)S(1)} %pad_add_fusion.refs_0_, f32[512,512]{1,0:T(8,128)S(1)} %get-tuple-element.27.refs_1_, f32[2,256,512]{2,1,0:T(8,128)S(1)} %copy-done, ...), custom_call_target="tpu_custom_call" | custom-call | flops 2415919104 | bytes 5767168 | tf_op jit(solution)/shard_map/pallas_call | solution.py:166
  26.3 4.7 %collective-permute-done.1.refs_1_ = f32[640,128]{1,0:T(8,128)S(1)} collective-permute-done((f32[640,128]{1,0:T(8,128)S(1)}, f32[640,128]{1,0:T(8,128)S(1)}, u32[]{:S(2)}, u32[]{:S(2)}) %collective-permute-start.1) | collective-permute-done | bytes 327712 | tf_op jit(solution)/shard_map/ppermute | solution.py:318
  31.0 0.0 collective-permute-start.4
  31.0 1.3 %collective-permute-start.13 = (f32[256,512]{1,0:T(8,128)S(1)}, f32[256,512]{1,0:T(8,128)S(1)}, u32[]{:S(2)}, u32[]{:S(2)}) collective-permute-start(f32[256,512]{1,0:T(8,128)S(1)} %get-tuple-element.39.refs_5_), channel_id=1, source_target_pairs={{0,2},{4,6},{8,10},{12,14},{16,18},{20,22},{24,26},{28,30},{32,34}... | collective-permute-start | bytes 1572872 | tf_op jit(solution)/shard_map/ppermute | solution.py:318
  32.3 0.3 collective-permute-done.4.refs_2_
  32.6 1.9 %shard_map.60 = (f32[256,512]{1,0:T(8,128)S(1)}, f32[512,512]{1,0:T(8,128)S(1)}, f32[512,512]{1,0:T(8,128)S(1)}) custom-call(s32[3]{0:T(128)S(1)} %pad_add_fusion.refs_0_, f32[640,128]{1,0:T(8,128)S(1)} %collective-permute-done.1.refs_1_, f32[640,128]{1,0:T(8,128)S(1)} %collective-permute-done.4.refs_2_, f32[2,256,512]{2,1,0:T(8,128)S(1)} %copy-done, ...), custom_call_target="tpu_custom_call" | custom-call | flops 805306368 | bytes 4718592 | tf_op jit(solution)/shard_map/pallas_call | solution.py:166
  34.5 1.3 %collective-permute-start.10 = (f32[256,512]{1,0:T(8,128)S(1)}, f32[256,512]{1,0:T(8,128)S(1)}, u32[]{:S(2)}, u32[]{:S(2)}) collective-permute-start(f32[256,512]{1,0:T(8,128)S(1)} %get-tuple-element.34.refs_2_), channel_id=1, source_target_pairs={{2,4},{6,8},{10,12},{14,16},{18,20},{22,24},{26,28},{30,32},{34,36... | collective-permute-start | bytes 1572872 | tf_op jit(solution)/shard_map/ppermute | solution.py:318
  35.8 0.3 collective-permute-start.5
  36.1 1.3 %collective-permute-start.6 = (f32[256,512]{1,0:T(8,128)S(1)}, f32[256,512]{1,0:T(8,128)S(1)}, u32[]{:S(2)}, u32[]{:S(2)}) collective-permute-start(f32[256,512]{1,0:T(8,128)S(1)} %get-tuple-element.34.refs_2_), channel_id=1, source_target_pairs={{2,0},{6,4},{10,8},{14,12},{18,16},{22,20},{26,24},{30,28},{34,32}... | collective-permute-start | bytes 1572872 | tf_op jit(solution)/shard_map/ppermute | solution.py:321
  37.4 2.7 %shard_map.61 = (f32[256,512]{1,0:T(8,128)S(1)}, f32[512,512]{1,0:T(8,128)S(1)}, f32[640,128]{1,0:T(8,128)S(1)}) custom-call(s32[3]{0:T(128)S(1)} %pad_add_fusion.refs_0_, f32[512,512]{1,0:T(8,128)S(1)} %get-tuple-element.29.refs_1_, f32[512,512]{1,0:T(8,128)S(1)} %get-tuple-element.31.refs_2_, f32[512,512]{1,0:T(8,128)S(1)} %get-tuple-element.32.refs_3_.refs_11_), custom_call_target="tpu_custom_call" | custom-call | flops 6979321856 | bytes 3670016 | tf_op jit(solution)/shard_map/pallas_call | solution.py:166
  40.1 1.3 %collective-permute-start.11 = (f32[640,128]{1,0:T(8,128)S(1)}, f32[640,128]{1,0:T(8,128)S(1)}, u32[]{:S(2)}, u32[]{:S(2)}) collective-permute-start(f32[640,128]{1,0:T(8,128)S(1)} %get-tuple-element.35), channel_id=1, source_target_pairs={{2,4},{6,8},{10,12},{14,16},{18,20},{22,24},{26,28},{30,32},{34,36... | collective-permute-start | bytes 983048 | tf_op jit(solution)/shard_map/ppermute | solution.py:318
  41.4 3.0 %collective-permute-done.13.refs_2_ = f32[256,512]{1,0:T(8,128)S(1)} collective-permute-done((f32[256,512]{1,0:T(8,128)S(1)}, f32[256,512]{1,0:T(8,128)S(1)}, u32[]{:S(2)}, u32[]{:S(2)}) %collective-permute-start.13) | collective-permute-done | bytes 524320 | tf_op jit(solution)/shard_map/ppermute | solution.py:318
  44.4 1.3 %collective-permute-start.8 = (f32[640,128]{1,0:T(8,128)S(1)}, f32[640,128]{1,0:T(8,128)S(1)}, u32[]{:S(2)}, u32[]{:S(2)}) collective-permute-start(f32[640,128]{1,0:T(8,128)S(1)} %get-tuple-element.35), channel_id=1, source_target_pairs={{2,0},{6,4},{10,8},{14,12},{18,16},{22,20},{26,24},{30,28},{34,32}... | collective-permute-start | bytes 983048 | tf_op jit(solution)/shard_map/ppermute | solution.py:321
  45.7 6.4 %collective-permute-done.6.refs_4_.refs_7_ = f32[256,512]{1,0:T(8,128)S(1)} collective-permute-done((f32[256,512]{1,0:T(8,128)S(1)}, f32[256,512]{1,0:T(8,128)S(1)}, u32[]{:S(2)}, u32[]{:S(2)}) %collective-permute-start.6) | collective-permute-done | bytes 524320 | tf_op jit(solution)/shard_map/ppermute | solution.py:321
  52.1 0.0 collective-permute-start.7
  52.1 2.6 %collective-permute-done.10.refs_8_ = f32[256,512]{1,0:T(8,128)S(1)} collective-permute-done((f32[256,512]{1,0:T(8,128)S(1)}, f32[256,512]{1,0:T(8,128)S(1)}, u32[]{:S(2)}, u32[]{:S(2)}) %collective-permute-start.10) | collective-permute-done | bytes 524320 | tf_op jit(solution)/shard_map/ppermute | solution.py:318
  54.7 0.0 collective-permute-done.5.refs_3_.refs_9_
  54.7 0.6 shard_map.63
  55.3 1.3 %collective-permute-start.14 = (f32[256,512]{1,0:T(8,128)S(1)}, f32[256,512]{1,0:T(8,128)S(1)}, u32[]{:S(2)}, u32[]{:S(2)}) collective-permute-start(f32[256,512]{1,0:T(8,128)S(1)} %get-tuple-element.43), channel_id=1, source_target_pairs={{2,0},{6,4},{10,8},{14,12},{18,16},{22,20},{26,24},{30,28},{34,32}... | collective-permute-start | bytes 1572872 | tf_op jit(solution)/shard_map/ppermute | solution.py:321
  56.6 1.3 %collective-permute-start.15 = (f32[256,512]{1,0:T(8,128)S(1)}, f32[256,512]{1,0:T(8,128)S(1)}, u32[]{:S(2)}, u32[]{:S(2)}) collective-permute-start(f32[256,512]{1,0:T(8,128)S(1)} %get-tuple-element.44), channel_id=1, source_target_pairs={{2,4},{6,8},{10,12},{14,16},{18,20},{22,24},{26,28},{30,32},{34,36... | collective-permute-start | bytes 1572872 | tf_op jit(solution)/shard_map/ppermute | solution.py:318
  57.9 7.0 %collective-permute-done.11.refs_9_ = f32[640,128]{1,0:T(8,128)S(1)} collective-permute-done((f32[640,128]{1,0:T(8,128)S(1)}, f32[640,128]{1,0:T(8,128)S(1)}, u32[]{:S(2)}, u32[]{:S(2)}) %collective-permute-start.11) | collective-permute-done | bytes 327712 | tf_op jit(solution)/shard_map/ppermute | solution.py:318
  64.9 0.0 collective-permute-start.12
  64.9 0.0 collective-permute-done.8.refs_6_
  64.9 0.5 collective-permute-start.9
  65.4 1.1 %collective-permute-done.12.refs_10_ = f32[640,128]{1,0:T(8,128)S(1)} collective-permute-done((f32[640,128]{1,0:T(8,128)S(1)}, f32[640,128]{1,0:T(8,128)S(1)}, u32[]{:S(2)}, u32[]{:S(2)}) %collective-permute-start.12) | collective-permute-done | bytes 327712 | tf_op jit(solution)/shard_map/ppermute | solution.py:315
  66.5 0.5 collective-permute-done.9.refs_7_
  67.0 0.0 collective-permute-done.7.refs_5_
  67.0 5.6 %shard_map.62 = (f32[2,256,512]{2,1,0:T(8,128)}, f32[2,256,512]{2,1,0:T(8,128)}, bf16[512,512]{1,0:T(8,128)(2,1)S(1)}, bf16[512,512]{1,0:T(8,128)(2,1)S(1)}, bf1...) custom-call(s32[3]{0:T(128)S(1)} %pad_add_fusion.refs_0_, f32[256,512]{1,0:T(8,128)S(1)} %get-tuple-element.33.refs_1_, ...), custom_call_target="tpu_custom_call" | custom-call | bytes 10485760 | tf_op jit(solution)/shard_map/pallas_call | solution.py:166
  72.5 0.3 collective-permute-done.14.refs_2_
  72.8 3.2 %collective-permute-done.15.refs_3_ = f32[256,512]{1,0:T(8,128)S(1)} collective-permute-done((f32[256,512]{1,0:T(8,128)S(1)}, f32[256,512]{1,0:T(8,128)S(1)}, u32[]{:S(2)}, u32[]{:S(2)}) %collective-permute-start.15) | collective-permute-done | bytes 524320 | tf_op jit(solution)/shard_map/ppermute | solution.py:318
  76.1 2.6 %shard_map.64 = f32[2,256,512]{2,1,0:T(8,128)} custom-call(s32[3]{0:T(128)S(1)} %pad_add_fusion.refs_0_, f32[256,512]{1,0:T(8,128)S(1)} %get-tuple-element.42.refs_1_, f32[256,512]{1,0:T(8,128)S(1)} %collective-permute-done.14.refs_2_, f32[256,512]{1,0:T(8,128)S(1)} %collective-permute-done.15.refs_3_, bf16[512,512]{1,0:T(8,128)(2,1)S(1)} %get-tuple-element.45.refs_4_, ...), custom_call_target="tpu_custom_call" | custom-call | flops 805306368 | bytes 5242880 | tf_op jit(solution)/shard_map/pallas_call | solution.py:166
Async XLA Ops:
  0.6 5.2 %copy-start.1 = (f32[2,256,512]{2,1,0:T(8,128)S(1)}, f32[2,256,512]{2,1,0:T(8,128)}, u32[]{:S(2)}) copy-start(f32[2,256,512]{2,1,0:T(8,128)} %refs_12_.1) | copy-start | bytes 3145732
  0.6 5.2 %collective-permute-start = (f32[2,256,512]{2,1,0:T(8,128)}, f32[2,256,512]{2,1,0:T(8,128)}, u32[]{:S(2)}, u32[]{:S(2)}) collective-permute-start(f32[2,256,512]{2,1,0:T(8,128)} %refs_12_.1), channel_id=1, source_target_pairs={{0,1},{1,0},{2,3},{3,2},{4,5},{5,4},{6,7},{7,6},{8,9},{9,8},{10,11... | collective-permute-start | bytes 3145736 | tf_op jit(solution)/shard_map/ppermute | solution.py:315
  0.7 21.6 %collective-permute-start.2 = (f32[2,256,512]{2,1,0:T(8,128)}, f32[2,256,512]{2,1,0:T(8,128)S(1)}, u32[]{:S(2)}, u32[]{:S(2)}) collective-permute-start(f32[2,256,512]{2,1,0:T(8,128)} %refs_13_.1), channel_id=1, source_target_pairs={{0,1},{1,0},{2,3},{3,2},{4,5},{5,4},{6,7},{7,6},{8,9},{9,8},{10,11... | collective-permute-start | bytes 3145736 | tf_op jit(solution)/shard_map/ppermute | solution.py:315
  2.3 20.0 %collective-permute-start.3 = (f32[256,512]{1,0:T(8,128)S(1)}, f32[256,512]{1,0:T(8,128)S(1)}, u32[]{:S(2)}, u32[]{:S(2)}) collective-permute-start(f32[256,512]{1,0:T(8,128)S(1)} %slice_bitcast_fusion), channel_id=1, source_target_pairs={{0,2},{2,4},{4,6},{6,8},{8,10},{10,12},{12,14},{14,16},{16,18},{18... | collective-permute-start | bytes 1572872 | tf_op jit(solution)/shard_map/ppermute | solution.py:318
  5.8 16.5 %copy-start = (f32[2,256,512]{2,1,0:T(8,128)S(1)}, f32[2,256,512]{2,1,0:T(8,128)}, u32[]{:S(2)}) copy-start(f32[2,256,512]{2,1,0:T(8,128)} %refs_13_.1) | copy-start | bytes 3145732
  5.8 16.5 %copy-start.2 = (f32[2,256,512]{2,1,0:T(8,128)S(1)}, f32[2,256,512]{2,1,0:T(8,128)}, u32[]{:S(2)}) copy-start(f32[2,256,512]{2,1,0:T(8,128)} %refs_8_.1) | copy-start | bytes 3145732
  15.5 15.6 %collective-permute-start.1 = (f32[640,128]{1,0:T(8,128)S(1)}, f32[640,128]{1,0:T(8,128)S(1)}, u32[]{:S(2)}, u32[]{:S(2)}) collective-permute-start(f32[640,128]{1,0:T(8,128)S(1)} %get-tuple-element.26), channel_id=1, source_target_pairs={{0,2},{2,4},{4,6},{6,8},{8,10},{10,12},{12,14},{14,16},{16,18},{18... | collective-permute-start | bytes 983048 | tf_op jit(solution)/shard_map/ppermute | solution.py:318
  31.0 1.6 %collective-permute-start.4 = (f32[640,128]{1,0:T(8,128)S(1)}, f32[640,128]{1,0:T(8,128)S(1)}, u32[]{:S(2)}, u32[]{:S(2)}) collective-permute-start(f32[640,128]{1,0:T(8,128)S(1)} %collective-permute-done.1.refs_1_), channel_id=1, source_target_pairs={{0,1},{1,0},{2,3},{3,2},{4,5},{5,4},{6,7},{7,6},{8,9},{9,8},{10,11... | collective-permute-start | bytes 983048 | tf_op jit(solution)/shard_map/ppermute | solution.py:315
  31.0 13.4 %collective-permute-start.13 = (f32[256,512]{1,0:T(8,128)S(1)}, f32[256,512]{1,0:T(8,128)S(1)}, u32[]{:S(2)}, u32[]{:S(2)}) collective-permute-start(f32[256,512]{1,0:T(8,128)S(1)} %get-tuple-element.39.refs_5_), channel_id=1, source_target_pairs={{0,2},{4,6},{8,10},{12,14},{16,18},{20,22},{24,26},{28,30},{32,34}... | collective-permute-start | bytes 1572872 | tf_op jit(solution)/shard_map/ppermute | solution.py:318
  34.5 20.2 %collective-permute-start.10 = (f32[256,512]{1,0:T(8,128)S(1)}, f32[256,512]{1,0:T(8,128)S(1)}, u32[]{:S(2)}, u32[]{:S(2)}) collective-permute-start(f32[256,512]{1,0:T(8,128)S(1)} %get-tuple-element.34.refs_2_), channel_id=1, source_target_pairs={{2,4},{6,8},{10,12},{14,16},{18,20},{22,24},{26,28},{30,32},{34,36... | collective-permute-start | bytes 1572872 | tf_op jit(solution)/shard_map/ppermute | solution.py:318
  35.8 18.9 %collective-permute-start.5 = (f32[256,512]{1,0:T(8,128)S(1)}, f32[256,512]{1,0:T(8,128)S(1)}, u32[]{:S(2)}, u32[]{:S(2)}) collective-permute-start(f32[256,512]{1,0:T(8,128)S(1)} %get-tuple-element.34.refs_2_), channel_id=1, source_target_pairs={{0,1},{1,0},{2,3},{3,2},{4,5},{5,4},{6,7},{7,6},{8,9},{9,8},{10,11... | collective-permute-start | bytes 1572872 | tf_op jit(solution)/shard_map/ppermute | solution.py:315
  36.1 16.0 %collective-permute-start.6 = (f32[256,512]{1,0:T(8,128)S(1)}, f32[256,512]{1,0:T(8,128)S(1)}, u32[]{:S(2)}, u32[]{:S(2)}) collective-permute-start(f32[256,512]{1,0:T(8,128)S(1)} %get-tuple-element.34.refs_2_), channel_id=1, source_target_pairs={{2,0},{6,4},{10,8},{14,12},{18,16},{22,20},{26,24},{30,28},{34,32}... | collective-permute-start | bytes 1572872 | tf_op jit(solution)/shard_map/ppermute | solution.py:321
  40.1 24.8 %collective-permute-start.11 = (f32[640,128]{1,0:T(8,128)S(1)}, f32[640,128]{1,0:T(8,128)S(1)}, u32[]{:S(2)}, u32[]{:S(2)}) collective-permute-start(f32[640,128]{1,0:T(8,128)S(1)} %get-tuple-element.35), channel_id=1, source_target_pairs={{2,4},{6,8},{10,12},{14,16},{18,20},{22,24},{26,28},{30,32},{34,36... | collective-permute-start | bytes 983048 | tf_op jit(solution)/shard_map/ppermute | solution.py:318
  44.4 20.5 %collective-permute-start.8 = (f32[640,128]{1,0:T(8,128)S(1)}, f32[640,128]{1,0:T(8,128)S(1)}, u32[]{:S(2)}, u32[]{:S(2)}) collective-permute-start(f32[640,128]{1,0:T(8,128)S(1)} %get-tuple-element.35), channel_id=1, source_target_pairs={{2,0},{6,4},{10,8},{14,12},{18,16},{22,20},{26,24},{30,28},{34,32}... | collective-permute-start | bytes 983048 | tf_op jit(solution)/shard_map/ppermute | solution.py:321
  52.1 14.9 %collective-permute-start.7 = (f32[256,512]{1,0:T(8,128)S(1)}, f32[256,512]{1,0:T(8,128)S(1)}, u32[]{:S(2)}, u32[]{:S(2)}) collective-permute-start(f32[256,512]{1,0:T(8,128)S(1)} %collective-permute-done.6.refs_4_.refs_7_), channel_id=1, source_target_pairs={{0,1},{1,0},{2,3},{3,2},{4,5},{5,4},{6,7},{7,6},{8,9},{9,8},{10,11... | collective-permute-start | bytes 1572872 | tf_op jit(solution)/shard_map/ppermute | solution.py:315
  55.3 17.6 %collective-permute-start.14 = (f32[256,512]{1,0:T(8,128)S(1)}, f32[256,512]{1,0:T(8,128)S(1)}, u32[]{:S(2)}, u32[]{:S(2)}) collective-permute-start(f32[256,512]{1,0:T(8,128)S(1)} %get-tuple-element.43), channel_id=1, source_target_pairs={{2,0},{6,4},{10,8},{14,12},{18,16},{22,20},{26,24},{30,28},{34,32}... | collective-permute-start | bytes 1572872 | tf_op jit(solution)/shard_map/ppermute | solution.py:321
  56.6 19.5 %collective-permute-start.15 = (f32[256,512]{1,0:T(8,128)S(1)}, f32[256,512]{1,0:T(8,128)S(1)}, u32[]{:S(2)}, u32[]{:S(2)}) collective-permute-start(f32[256,512]{1,0:T(8,128)S(1)} %get-tuple-element.44), channel_id=1, source_target_pairs={{2,4},{6,8},{10,12},{14,16},{18,20},{22,24},{26,28},{30,32},{34,36... | collective-permute-start | bytes 1572872 | tf_op jit(solution)/shard_map/ppermute | solution.py:318
  64.9 1.6 %collective-permute-start.12 = (f32[640,128]{1,0:T(8,128)S(1)}, f32[640,128]{1,0:T(8,128)S(1)}, u32[]{:S(2)}, u32[]{:S(2)}) collective-permute-start(f32[640,128]{1,0:T(8,128)S(1)} %collective-permute-done.11.refs_9_), channel_id=1, source_target_pairs={{0,1},{1,0},{2,3},{3,2},{4,5},{5,4},{6,7},{7,6},{8,9},{9,8},{10,11... | collective-permute-start | bytes 983048 | tf_op jit(solution)/shard_map/ppermute | solution.py:315
  64.9 2.1 %collective-permute-start.9 = (f32[640,128]{1,0:T(8,128)S(1)}, f32[640,128]{1,0:T(8,128)S(1)}, u32[]{:S(2)}, u32[]{:S(2)}) collective-permute-start(f32[640,128]{1,0:T(8,128)S(1)} %collective-permute-done.8.refs_6_), channel_id=1, source_target_pairs={{0,1},{1,0},{2,3},{3,2},{4,5},{5,4},{6,7},{7,6},{8,9},{9,8},{10,11... | collective-permute-start | bytes 983048 | tf_op jit(solution)/shard_map/ppermute | solution.py:315

commit v3 on v2

--- a/solution.py
+++ b/solution.py
@@ -17,7 +17,7 @@
 VMEM = pl.BlockSpec(memory_space=pltpu.VMEM)
 SMEM = pl.BlockSpec(memory_space=pltpu.SMEM)
 
-SQUARINGS = 5
+SQUARINGS = 4
 TARGET = 3e-3
 USABLE = 0.6
 
@@ -67,18 +67,24 @@
 
 def invert(d_ref, x_ref, res_ref):
     block = d_ref[...]
-    top = jnp.max(jnp.sum(jnp.abs(block), axis=1, keepdims=True), axis=0, keepdims=True)
-    alpha = 1.9 / top
-    r = identity() - block * alpha
-    y = identity() + r
-    r = r.astype(BF16)
-    r = dot(r, r).astype(BF16)
+    low = block.astype(BF16)
+    square = dot(low, low)
+    top = jnp.max(jnp.sum(jnp.abs(square), axis=1, keepdims=True), axis=0, keepdims=True)
+    alpha = 1.9 * lax.rsqrt(top)
+    scaled = block * alpha
+    y = 2.0 * identity() - scaled
+    r = (y - scaled + square * (alpha * alpha) - identity()).astype(BF16)
     for _ in range(SQUARINGS - 1):
         squared = dot(r, r)
         y = y + dot(y.astype(BF16), r)
         r = squared.astype(BF16)
     y = y + dot(y.astype(BF16), r)
-    x_ref[...] = y * alpha
+    start = (y * alpha).astype(BF16)
+    high, rest = halves(d_ref[...])
+    residual = identity() - (dot(high, start) + dot(rest, start))
+    res_ref[...] = residual
+    x_ref[...] = start.astype(F32)
+    first = jnp.sum(residual * residual)
 
     def measure():
         residual = identity() - dot3(halves(d_ref[...]), halves(x_ref[...]))
@@ -97,7 +103,7 @@
         improve()
         return measure(), carry[1] + 1
 
-    size, _ = lax.while_loop(going, refine, (measure(), 0))
+    size, _ = lax.while_loop(going, refine, (first, 0))
     converged = size <= TARGET * TARGET
 
     @pl.when(converged)
@@ -204,29 +210,43 @@
 
 
 def coupled_upper(info, zq, zq_other, u, u_other, uq):
-    def kernel(info_ref, zq_ref, zqx_ref, ui_ref, uix_ref, uq_ref, un_ref, z_ref, u_ref):
-        unpack(info_ref, zq_ref, zqx_ref, z_ref)
-        join(info_ref, ui_ref.at[0], uix_ref.at[0], u_ref)
-        v = dot3(halves(uq_ref[...]), halves(z_ref[...]))
-        fresh = -dot3(halves(v), halves(u_ref[...]))
-        un_ref[...] = jnp.where(info_ref[1] > 0, fresh, ui_ref[0])
-
-    return call(kernel, [SLAB, FULL, FULL], [info, zq, zq_other, u, u_other, uq], [], 3)
-
-
-def second_inverse(info, a, zq, u):
-    def kernel(info_ref, a_ref, zq_ref, u_ref, dc_ref, z_ref, zp_ref, d_ref, res_ref):
-        u2 = halves(u_ref[...])
-        w = dot3(u2, halves(zq_ref[...]), TN)
-        d_ref[...] = a_ref[...] - dot3(halves(w), u2)
-        dc_ref[...] = own_rows(info_ref, d_ref)
-
-        @pl.when(info_ref[2] > 0)
-        def _():
+    def kernel(info_ref, zq_ref, zqx_ref, ui_ref, uix_ref, uq_ref, un_ref, t_ref, u_ref, z_ref):
+        @pl.when(info_ref[2] > 0)
+        def _():
+            unpack(info_ref, zq_ref, zqx_ref, z_ref)
+            join(info_ref, ui_ref.at[0], uix_ref.at[0], u_ref)
+            t = dot3(halves(z_ref[...]), halves(u_ref[...]))
+            t_ref[...] = t
+            un_ref[...] = -dot3(halves(uq_ref[...]), halves(t))
+
+    return call(kernel, [SLAB, FULL, FULL], [info, zq, zq_other, u, u_other, uq], [FULL], 3)
+
+
+def second_inverse(info, a, t, u_full, zq, zq_other, u, u_other, uq, uq_other):
+    def kernel(
+        info_ref, a_ref, t_ref, u_ref, zq_ref, zqx_ref, ui_ref, uix_ref, uq_ref, uqx_ref,
+        dc_ref, un_ref, z_ref, zp_ref, d_ref, res_ref,
+    ):
+        @pl.when(info_ref[2] > 0)
+        def _():
+            d_ref[...] = a_ref[...] - dot3(halves(u_ref[...]), halves(t_ref[...]), TN)
+            dc_ref[...] = own_rows(info_ref, d_ref)
             invert(d_ref, z_ref, res_ref)
             pack(info_ref, z_ref, zp_ref)
 
-    return call(kernel, [SLAB, FULL, PACKED], [info, a, zq, u], [FULL, FULL], 26)
+        @pl.when(info_ref[2] == 0)
+        def _():
+            unpack(info_ref, zq_ref, zqx_ref, z_ref)
+            join(info_ref, ui_ref.at[0], uix_ref.at[0], d_ref)
+            t = halves(dot3(halves(z_ref[...]), halves(d_ref[...])))
+            join(info_ref, uq_ref, uqx_ref, z_ref)
+            un_ref[...] = jnp.where(info_ref[1] > 0, -dot3(halves(z_ref[...]), t), d_ref[...])
+            dc_ref[...] = own_rows(info_ref, a_ref) - dot3(halves(own_columns(info_ref, d_ref)), t, TN)
+
+    return call(
+        kernel, [SLAB, FULL, FULL, PACKED], [info, a, t, u_full, zq, zq_other, u, u_other, uq, uq_other],
+        [FULL, FULL], 24,
+    )
 
 
 def odd_sources(info, b, gq, u, z, go, v, after):
@@ -246,13 +266,13 @@
     return call(kernel, [SLAB, SLAB, SLAB], [info, b, gq, u, z, go, v], [], 5, after)
 
 
-def level1_blocks(info, d, u_mid, u_mid_other, right, left, ue, d_in, u_in):
+def level1_blocks(info, d, u_odd, mid, right, left, d_in, u_in, u_other):
     ur, urx, zr, zrx = right
     ul, zl, zlx = left
 
     def kernel(
-        info_ref, d_ref, um_ref, umx_ref, ur_ref, urx_ref, zr_ref, zrx_ref, ul_ref, zl_ref, zlx_ref,
-        ue_ref, din_ref, uin_ref, dout_ref, uout_ref, fh_ref, fl_ref, uh_ref, ul2_ref, mid_ref, far_ref, zr_full, zl_full,
+        info_ref, d_ref, uo_ref, mid_ref, ur_ref, urx_ref, zr_ref, zrx_ref, ul_ref, zl_ref, zlx_ref,
+        din_ref, uin_ref, uix_ref, dout_ref, uout_ref, fh_ref, fl_ref, uh_ref, uw_ref, far_ref, z_ref,
     ):
         dout_ref[1] = din_ref[1]
         uout_ref[1] = uin_ref[1]
@@ -260,30 +280,30 @@
         @pl.when(info_ref[2] > 0)
         def _():
             dout_ref[0] = d_ref[...]
-            uout_ref[0] = um_ref[...]
+            uout_ref[0] = uo_ref[...]
 
         @pl.when(info_ref[2] == 0)
         def _():
-            join(info_ref, um_ref, umx_ref, mid_ref)
+            join(info_ref, uin_ref.at[0], uix_ref.at[0], far_ref)
+            uh_ref[...], uw_ref[...] = halves(far_ref[...])
             join(info_ref, ur_ref, urx_ref, far_ref)
-            unpack(info_ref, zr_ref, zrx_ref, zr_full)
-            unpack(info_ref, zl_ref, zlx_ref, zl_full)
             far = halves(far_ref[...])
             fh_ref[...], fl_ref[...] = far
-            uh_ref[...], ul2_ref[...] = halves(ue_ref[...])
             mid = halves(mid_ref[...])
-            zl2 = halves(zl_full[...])
-            v = dot3(halves(ur_ref[...]), halves(zr_full[...]))
-            w = dot3(halves(own_columns(info_ref, mid_ref)), zl2, TN)
+            unpack(info_ref, zr_ref, zrx_ref, z_ref)
+            v = dot3(halves(ur_ref[...]), halves(z_ref[...]))
+            unpack(info_ref, zl_ref, zlx_ref, z_ref)
+            z2 = halves(z_ref[...])
+            w = dot3(halves(own_columns(info_ref, mid_ref)), z2, TN)
             dout_ref[0] = d_ref[...] - dot3(halves(v), far, NT) - dot3(halves(w), mid)
-            s = dot3(halves(ul_ref[...]), zl2)
+            s = dot3(halves(ul_ref[...]), z2)
             fresh = -dot3(halves(s), mid)
-            uout_ref[0] = jnp.where(info_ref[1] > 0, fresh, um_ref[...])
+            uout_ref[0] = jnp.where(info_ref[1] > 0, fresh, own_rows(info_ref, mid_ref))
 
     return call(
         kernel, [PAIR, PAIR],
-        [info, d, u_mid, u_mid_other, ur, urx, zr, zrx, ul, zl, zlx, ue, d_in, u_in],
-        [FULL] * 4, 0, rounded=[FULL] * 4,
+        [info, d, u_odd, mid, ur, urx, zr, zrx, ul, zl, zlx, d_in, u_in, u_other],
+        [FULL] * 2, 0, rounded=[FULL] * 4,
     )
 
 
@@ -331,24 +351,27 @@
     a, b, vo, go = left_updates(
         info, zo, upper_blocks, u_other, diagonal_blocks, d_other, right_sides, (uq,)
     )
+    uqx = swap(uq)
     gq = onward(go, 0, 2)
     zq, a = lax.optimization_barrier((zq, a))
-    u_mid, zq_full, ue_full = coupled_upper(info, zq, swap(zq), upper_blocks, u_other, uq)
-    ur = odd_left(u_mid)
-    ul = odd_right(u_mid)
-    u_mid_other = swap(u_mid)
-    d_mid, z1, z1_packed = second_inverse(info, a, zq_full, ue_full)
+    zqx = swap(zq)
+    u_odd, t, ue_full = coupled_upper(info, zq, zqx, upper_blocks, u_other, uq)
+    ur = odd_left(u_odd)
+    ul = odd_right(u_odd)
+    d_mid, u_even, z1, z1_packed = second_inverse(
+        info, a, t, ue_full, zq, zqx, upper_blocks, u_other, uq, uqx
+    )
     zr = odd_left(z1_packed)
     zl = odd_right(z1_packed)
-    f_mid, g1, gt = odd_sources(info, b, gq, ue_full, z1, go, vo, (ur, ul, u_mid_other))
+    f_mid, g1, gt = odd_sources(info, b, gq, ue_full, z1, go, vo, (ur, ul))
     gr = odd_left(g1)
     gl = odd_right(gt)
     urx = swap(ur)
-    d_out, u_out, fh, fl, uh, ul2 = level1_blocks(
-        info, d_mid, u_mid, u_mid_other, (ur, urx, zr, swap(zr)), (ul, zl, swap(zl)), ue_full,
-        diagonal_blocks, upper_blocks,
-    )
-    f_out = level1_sources(info, f_mid, gr, gl, (fh, fl), (uh, ul2), right_sides)
+    d_out, u_out, fh, fl, uh, uw = level1_blocks(
+        info, d_mid, u_odd, u_even, (ur, urx, zr, swap(zr)), (ul, zl, swap(zl)),
+        diagonal_blocks, upper_blocks, u_other,
+    )
+    f_out = level1_sources(info, f_mid, gr, gl, (fh, fl), (uh, uw), right_sides)
     return d_out, u_out, f_out
 
 

time: 78.9 us -> 76.8 us (0.973)
  waiting for transfers between devices: 32.6 us -> 31.3 us
    ppermute x6, waiting for transfers between devices: 24 us -> 20.8 us  [onward(): lax.ppermute(a, 'tm', [(i, i + 1) for i in range(first, chips - 1, step)])]
    ppermute x3, waiting for transfers between devices: 6.7 us -> 8.68 us  [odd_left(): return lax.ppermute(a, 'tm', [(i, i - 1) for i in range(1, chips, 2)])]
  transfers between devices with their start and end apart: 16 -> 16, of which waited for: 11 -> 9; matrix products, arithmetic and copies ran while one was open for 1% -> 2% of each run, Pallas kernels for 31% -> 31%
where the time goes in v3:
time: 76.8 us; the launch traced here: 76.5 us
  waiting for transfers between devices  31.3 us (41%)
  Pallas kernels  26.2 us (34%)
  starting transfers between devices  17 us (22%)
  local copies, waits for them, and re-layouts  1.09 us (1%)
  between operations  0.82 us (1%)
    pallas_call x7, Pallas kernels, call(): pl.pallas_call(entry, out_shape=[jax.ShapeDtypeStruct(o, kind) for o, kin...  26.2 us
    ppermute x6, waiting for transfers between devices, onward(): lax.ppermute(a, 'tm', [(i, i + 1) for i in range(first, chips - 1, step)])  20.8 us
    ppermute x6, starting transfers between devices, onward(): lax.ppermute(a, 'tm', [(i, i + 1) for i in range(first, chips - 1, step)])  12 us
    ppermute x3, waiting for transfers between devices, odd_left(): return lax.ppermute(a, 'tm', [(i, i - 1) for i in range(1, chips, 2)])  8.68 us
    ppermute x3, starting transfers between devices, odd_left(): return lax.ppermute(a, 'tm', [(i, i - 1) for i in range(1, chips, 2)])  3.88 us
    ppermute x7, waiting for transfers between devices, swap(): return lax.ppermute(a, 'col', [(0, 1), (1, 0)])  1.9 us
  transfers between devices with their start and end apart: 16, of which 9 were waited for; matrix products, arithmetic and copies ran while one was open for 2% of the time, Pallas kernels for 31%

profile of v3, /device:TPU:64, one launch (start us, length us, event | category | flops | bytes accessed | tf_op | source)
XLA Modules:
  0.0 76.5 jit_solution(16687945908330589566)
XLA Ops:
  0.6 0.0 copy-start.2
  0.6 0.1 collective-permute-start
  0.7 0.5 collective-permute-start.2
  1.2 1.1 %slice_bitcast_fusion = f32[256,512]{1,0:T(8,128)S(1)} fusion(f32[2,256,512]{2,1,0:T(8,128)} %refs_12_.1), kind=kLoop, calls=%fused_computation | loop fusion | bytes 1048576 | tf_op jit(solution)/shard_map/squeeze | solution.py:347
  2.3 3.4 %collective-permute-start.3 = (f32[256,512]{1,0:T(8,128)S(1)}, f32[256,512]{1,0:T(8,128)S(1)}, u32[]{:S(2)}, u32[]{:S(2)}) collective-permute-start(f32[256,512]{1,0:T(8,128)S(1)} %slice_bitcast_fusion), channel_id=1, source_target_pairs={{0,2},{2,4},{4,6},{6,8},{8,10},{10,12},{12,14},{14,16},{16,18},{18... | collective-permute-start | bytes 1572872 | tf_op jit(solution)/shard_map/ppermute | solution.py:338
  5.7 0.1 pad_add_fusion.refs_0_
  5.8 0.0 copy-start
  5.8 0.0 copy-start.1
  5.8 0.0 collective-permute-done.refs_2_.refs_5_
  5.8 0.0 copy-done.2
  5.8 8.9 %shard_map.58 = (f32[512,512]{1,0:T(8,128)S(1)}, f32[640,128]{1,0:T(8,128)S(1)}) custom-call(s32[3]{0:T(128)S(1)} %pad_add_fusion.refs_0_, f32[2,256,512]{2,1,0:T(8,128)S(1)} %copy-done.2, f32[2,256,512]{2,1,0:T(8,128)} %collective-permute-done.refs_2_.refs_5_), custom_call_target="tpu_custom_call" | custom-call | flops 5368709120 | bytes 2621440 | tf_op jit(solution)/shard_map/pallas_call | solution.py:172
  14.8 3.4 %collective-permute-start.1 = (f32[640,128]{1,0:T(8,128)S(1)}, f32[640,128]{1,0:T(8,128)S(1)}, u32[]{:S(2)}, u32[]{:S(2)}) collective-permute-start(f32[640,128]{1,0:T(8,128)S(1)} %get-tuple-element.27), channel_id=1, source_target_pairs={{0,2},{2,4},{4,6},{6,8},{8,10},{10,12},{12,14},{14,16},{16,18},{18... | collective-permute-start | bytes 983048 | tf_op jit(solution)/shard_map/ppermute | solution.py:338
  18.2 4.2 %collective-permute-done.3.refs_7_.refs_5_.refs_8_ = f32[256,512]{1,0:T(8,128)S(1)} collective-permute-done((f32[256,512]{1,0:T(8,128)S(1)}, f32[256,512]{1,0:T(8,128)S(1)}, u32[]{:S(2)}, u32[]{:S(2)}) %collective-permute-start.3) | collective-permute-done | bytes 524320 | tf_op jit(solution)/shard_map/ppermute | solution.py:338
  22.3 0.0 collective-permute-start.5
  22.3 0.0 collective-permute-done.2.refs_3_.refs_4_.refs_7_.refs_13_
  22.4 0.0 copy-done
  22.4 0.0 copy-done.1
  22.4 4.0 %shard_map.59 = (f32[512,512]{1,0:T(8,128)S(1)}, f32[256,512]{1,0:T(8,128)S(1)}, f32[512,512]{1,0:T(8,128)S(1)}, f32[256,512]{1,0:T(8,128)S(1)}) custom-call(s32[3]{0:T(128)S(1)} %pad_add_fusion.refs_0_, f32[512,512]{1,0:T(8,128)S(1)} %get-tuple-element.28.refs_1_, f32[2,256,512]{2,1,0:T(8,128)S(1)} %copy-done, ...), custom_call_target="tpu_custom_call" | custom-call | flops 2415919104 | bytes 5767168 | tf_op jit(solution)/shard_map/pallas_call | solution.py:172
  26.4 4.0 %collective-permute-done.1.refs_1_.refs_4_ = f32[640,128]{1,0:T(8,128)S(1)} collective-permute-done((f32[640,128]{1,0:T(8,128)S(1)}, f32[640,128]{1,0:T(8,128)S(1)}, u32[]{:S(2)}, u32[]{:S(2)}) %collective-permute-start.1) | collective-permute-done | bytes 327712 | tf_op jit(solution)/shard_map/ppermute | solution.py:338
  30.3 0.0 collective-permute-start.4
  30.3 1.3 %collective-permute-start.13 = (f32[256,512]{1,0:T(8,128)S(1)}, f32[256,512]{1,0:T(8,128)S(1)}, u32[]{:S(2)}, u32[]{:S(2)}) collective-permute-start(f32[256,512]{1,0:T(8,128)S(1)} %get-tuple-element.41.refs_5_), channel_id=1, source_target_pairs={{0,2},{4,6},{8,10},{12,14},{16,18},{20,22},{24,26},{28,30},{32,34}... | collective-permute-start | bytes 1572872 | tf_op jit(solution)/shard_map/ppermute | solution.py:338
  31.7 0.3 collective-permute-done.4.refs_2_.refs_5_
  32.0 0.5 shard_map.60
  32.5 1.3 %collective-permute-start.10 = (f32[256,512]{1,0:T(8,128)S(1)}, f32[256,512]{1,0:T(8,128)S(1)}, u32[]{:S(2)}, u32[]{:S(2)}) collective-permute-start(f32[256,512]{1,0:T(8,128)S(1)} %get-tuple-element.35.refs_2_), channel_id=1, source_target_pairs={{2,4},{6,8},{10,12},{14,16},{18,20},{22,24},{26,28},{30,32},{34,36... | collective-permute-start | bytes 1572872 | tf_op jit(solution)/shard_map/ppermute | solution.py:338
  33.8 1.3 %collective-permute-start.6 = (f32[256,512]{1,0:T(8,128)S(1)}, f32[256,512]{1,0:T(8,128)S(1)}, u32[]{:S(2)}, u32[]{:S(2)}) collective-permute-start(f32[256,512]{1,0:T(8,128)S(1)} %get-tuple-element.35.refs_2_), channel_id=1, source_target_pairs={{2,0},{6,4},{10,8},{14,12},{18,16},{22,20},{26,24},{30,28},{34,32}... | collective-permute-start | bytes 1572872 | tf_op jit(solution)/shard_map/ppermute | solution.py:341
  35.1 0.0 collective-permute-done.5.refs_9_
  35.1 3.3 %shard_map.61 = (f32[256,512]{1,0:T(8,128)S(1)}, f32[512,512]{1,0:T(8,128)S(1)}, f32[512,512]{1,0:T(8,128)S(1)}, f32[640,128]{1,0:T(8,128)S(1)}) custom-call(s32[3]{0:T(128)S(1)} %pad_add_fusion.refs_0_, f32[512,512]{1,0:T(8,128)S(1)} %get-tuple-element.30.refs_1_, f32[512,512]{1,0:T(8,128)S(1)} %get-tuple-element.32.refs_2_, ...), custom_call_target="tpu_custom_call" | custom-call | flops 6442450944 | bytes 7340032 | tf_op jit(solution)/shard_map/pallas_call | solution.py:172
  38.5 1.3 %collective-permute-start.11 = (f32[640,128]{1,0:T(8,128)S(1)}, f32[640,128]{1,0:T(8,128)S(1)}, u32[]{:S(2)}, u32[]{:S(2)}) collective-permute-start(f32[640,128]{1,0:T(8,128)S(1)} %get-tuple-element.37), channel_id=1, source_target_pairs={{2,4},{6,8},{10,12},{14,16},{18,20},{22,24},{26,28},{30,32},{34,36... | collective-permute-start | bytes 983048 | tf_op jit(solution)/shard_map/ppermute | solution.py:338
  39.8 1.3 %collective-permute-start.8 = (f32[640,128]{1,0:T(8,128)S(1)}, f32[640,128]{1,0:T(8,128)S(1)}, u32[]{:S(2)}, u32[]{:S(2)}) collective-permute-start(f32[640,128]{1,0:T(8,128)S(1)} %get-tuple-element.37), channel_id=1, source_target_pairs={{2,0},{6,4},{10,8},{14,12},{18,16},{22,20},{26,24},{30,28},{34,32}... | collective-permute-start | bytes 983048 | tf_op jit(solution)/shard_map/ppermute | solution.py:341
  41.1 8.7 %collective-permute-done.6.refs_4_.refs_7_ = f32[256,512]{1,0:T(8,128)S(1)} collective-permute-done((f32[256,512]{1,0:T(8,128)S(1)}, f32[256,512]{1,0:T(8,128)S(1)}, u32[]{:S(2)}, u32[]{:S(2)}) %collective-permute-start.6) | collective-permute-done | bytes 524320 | tf_op jit(solution)/shard_map/ppermute | solution.py:341
  49.7 0.0 collective-permute-start.7
  49.8 0.0 collective-permute-done.13.refs_2_
  49.8 2.9 %collective-permute-done.10.refs_8_ = f32[256,512]{1,0:T(8,128)S(1)} collective-permute-done((f32[256,512]{1,0:T(8,128)S(1)}, f32[256,512]{1,0:T(8,128)S(1)}, u32[]{:S(2)}, u32[]{:S(2)}) %collective-permute-start.10) | collective-permute-done | bytes 524320 | tf_op jit(solution)/shard_map/ppermute | solution.py:338
  52.7 0.6 shard_map.63
  53.3 1.3 %collective-permute-start.14 = (f32[256,512]{1,0:T(8,128)S(1)}, f32[256,512]{1,0:T(8,128)S(1)}, u32[]{:S(2)}, u32[]{:S(2)}) collective-permute-start(f32[256,512]{1,0:T(8,128)S(1)} %get-tuple-element.45), channel_id=1, source_target_pairs={{2,0},{6,4},{10,8},{14,12},{18,16},{22,20},{26,24},{30,28},{34,32}... | collective-permute-start | bytes 1572872 | tf_op jit(solution)/shard_map/ppermute | solution.py:341
  54.6 1.3 %collective-permute-start.15 = (f32[256,512]{1,0:T(8,128)S(1)}, f32[256,512]{1,0:T(8,128)S(1)}, u32[]{:S(2)}, u32[]{:S(2)}) collective-permute-start(f32[256,512]{1,0:T(8,128)S(1)} %get-tuple-element.46), channel_id=1, source_target_pairs={{2,4},{6,8},{10,12},{14,16},{18,20},{22,24},{26,28},{30,32},{34,36... | collective-permute-start | bytes 1572872 | tf_op jit(solution)/shard_map/ppermute | solution.py:338
  55.9 4.7 %collective-permute-done.11.refs_9_ = f32[640,128]{1,0:T(8,128)S(1)} collective-permute-done((f32[640,128]{1,0:T(8,128)S(1)}, f32[640,128]{1,0:T(8,128)S(1)}, u32[]{:S(2)}, u32[]{:S(2)}) %collective-permute-start.11) | collective-permute-done | bytes 327712 | tf_op jit(solution)/shard_map/ppermute | solution.py:338
  60.6 0.0 collective-permute-start.12
  60.6 0.0 collective-permute-done.8.refs_6_
  60.6 0.5 collective-permute-start.9
  61.1 1.1 %collective-permute-done.12.refs_10_ = f32[640,128]{1,0:T(8,128)S(1)} collective-permute-done((f32[640,128]{1,0:T(8,128)S(1)}, f32[640,128]{1,0:T(8,128)S(1)}, u32[]{:S(2)}, u32[]{:S(2)}) %collective-permute-start.12) | collective-permute-done | bytes 327712 | tf_op jit(solution)/shard_map/ppermute | solution.py:335
  62.2 0.5 collective-permute-done.9.refs_7_
  62.7 0.0 collective-permute-done.7.refs_5_
  62.7 6.2 %shard_map.62 = (f32[2,256,512]{2,1,0:T(8,128)}, f32[2,256,512]{2,1,0:T(8,128)}, bf16[512,512]{1,0:T(8,128)(2,1)S(1)}, bf16[512,512]{1,0:T(8,128)(2,1)S(1)}, bf1...) custom-call(s32[3]{0:T(128)S(1)} %pad_add_fusion.refs_0_, f32[256,512]{1,0:T(8,128)S(1)} %get-tuple-element.34.refs_1_, ...), custom_call_target="tpu_custom_call" | custom-call | bytes 10485760 | tf_op jit(solution)/shard_map/pallas_call | solution.py:172
  68.9 0.0 collective-permute-done.14.refs_2_
  68.9 5.0 %collective-permute-done.15.refs_3_ = f32[256,512]{1,0:T(8,128)S(1)} collective-permute-done((f32[256,512]{1,0:T(8,128)S(1)}, f32[256,512]{1,0:T(8,128)S(1)}, u32[]{:S(2)}, u32[]{:S(2)}) %collective-permute-start.15) | collective-permute-done | bytes 524320 | tf_op jit(solution)/shard_map/ppermute | solution.py:338
  73.9 2.6 %shard_map.64 = f32[2,256,512]{2,1,0:T(8,128)} custom-call(s32[3]{0:T(128)S(1)} %pad_add_fusion.refs_0_, f32[256,512]{1,0:T(8,128)S(1)} %get-tuple-element.44.refs_1_, f32[256,512]{1,0:T(8,128)S(1)} %collective-permute-done.14.refs_2_, f32[256,512]{1,0:T(8,128)S(1)} %collective-permute-done.15.refs_3_, bf16[512,512]{1,0:T(8,128)(2,1)S(1)} %get-tuple-element.47.refs_4_, ...), custom_call_target="tpu_custom_call" | custom-call | flops 805306368 | bytes 5242880 | tf_op jit(solution)/shard_map/pallas_call | solution.py:172
Async XLA Ops:
  0.6 5.2 %copy-start.2 = (f32[2,256,512]{2,1,0:T(8,128)S(1)}, f32[2,256,512]{2,1,0:T(8,128)}, u32[]{:S(2)}) copy-start(f32[2,256,512]{2,1,0:T(8,128)} %refs_11_.1) | copy-start | bytes 3145732
  0.6 5.2 %collective-permute-start = (f32[2,256,512]{2,1,0:T(8,128)}, f32[2,256,512]{2,1,0:T(8,128)}, u32[]{:S(2)}, u32[]{:S(2)}) collective-permute-start(f32[2,256,512]{2,1,0:T(8,128)} %refs_11_.1), channel_id=1, source_target_pairs={{0,1},{1,0},{2,3},{3,2},{4,5},{5,4},{6,7},{7,6},{8,9},{9,8},{10,11... | collective-permute-start | bytes 3145736 | tf_op jit(solution)/shard_map/ppermute | solution.py:335
  0.7 21.6 %collective-permute-start.2 = (f32[2,256,512]{2,1,0:T(8,128)}, f32[2,256,512]{2,1,0:T(8,128)S(1)}, u32[]{:S(2)}, u32[]{:S(2)}) collective-permute-start(f32[2,256,512]{2,1,0:T(8,128)} %refs_12_.1), channel_id=1, source_target_pairs={{0,1},{1,0},{2,3},{3,2},{4,5},{5,4},{6,7},{7,6},{8,9},{9,8},{10,11... | collective-permute-start | bytes 3145736 | tf_op jit(solution)/shard_map/ppermute | solution.py:335
  2.3 20.0 %collective-permute-start.3 = (f32[256,512]{1,0:T(8,128)S(1)}, f32[256,512]{1,0:T(8,128)S(1)}, u32[]{:S(2)}, u32[]{:S(2)}) collective-permute-start(f32[256,512]{1,0:T(8,128)S(1)} %slice_bitcast_fusion), channel_id=1, source_target_pairs={{0,2},{2,4},{4,6},{6,8},{8,10},{10,12},{12,14},{14,16},{16,18},{18... | collective-permute-start | bytes 1572872 | tf_op jit(solution)/shard_map/ppermute | solution.py:338
  5.8 16.5 %copy-start = (f32[2,256,512]{2,1,0:T(8,128)S(1)}, f32[2,256,512]{2,1,0:T(8,128)}, u32[]{:S(2)}) copy-start(f32[2,256,512]{2,1,0:T(8,128)} %refs_12_.1) | copy-start | bytes 3145732
  5.8 16.6 %copy-start.1 = (f32[2,256,512]{2,1,0:T(8,128)S(1)}, f32[2,256,512]{2,1,0:T(8,128)}, u32[]{:S(2)}) copy-start(f32[2,256,512]{2,1,0:T(8,128)} %refs_8_.1) | copy-start | bytes 3145732
  14.8 15.5 %collective-permute-start.1 = (f32[640,128]{1,0:T(8,128)S(1)}, f32[640,128]{1,0:T(8,128)S(1)}, u32[]{:S(2)}, u32[]{:S(2)}) collective-permute-start(f32[640,128]{1,0:T(8,128)S(1)} %get-tuple-element.27), channel_id=1, source_target_pairs={{0,2},{2,4},{4,6},{6,8},{8,10},{10,12},{12,14},{14,16},{16,18},{18... | collective-permute-start | bytes 983048 | tf_op jit(solution)/shard_map/ppermute | solution.py:338
  22.3 12.8 %collective-permute-start.5 = (f32[256,512]{1,0:T(8,128)S(1)}, f32[256,512]{1,0:T(8,128)S(1)}, u32[]{:S(2)}, u32[]{:S(2)}) collective-permute-start(f32[256,512]{1,0:T(8,128)S(1)} %collective-permute-done.3.refs_7_.refs_5_.refs_8_), channel_id=1, source_target_pairs={{0,1},{1,0},{2,3},{3,2},{4,5},{5,4},{6,7},{7,6},{8,9},{9,8},{10,11... | collective-permute-start | bytes 1572872 | tf_op jit(solution)/shard_map/ppermute | solution.py:335
  30.3 1.6 %collective-permute-start.4 = (f32[640,128]{1,0:T(8,128)S(1)}, f32[640,128]{1,0:T(8,128)S(1)}, u32[]{:S(2)}, u32[]{:S(2)}) collective-permute-start(f32[640,128]{1,0:T(8,128)S(1)} %collective-permute-done.1.refs_1_.refs_4_), channel_id=1, source_target_pairs={{0,1},{1,0},{2,3},{3,2},{4,5},{5,4},{6,7},{7,6},{8,9},{9,8},{10,11... | collective-permute-start | bytes 983048 | tf_op jit(solution)/shard_map/ppermute | solution.py:335
  30.3 19.4 %collective-permute-start.13 = (f32[256,512]{1,0:T(8,128)S(1)}, f32[256,512]{1,0:T(8,128)S(1)}, u32[]{:S(2)}, u32[]{:S(2)}) collective-permute-start(f32[256,512]{1,0:T(8,128)S(1)} %get-tuple-element.41.refs_5_), channel_id=1, source_target_pairs={{0,2},{4,6},{8,10},{12,14},{16,18},{20,22},{24,26},{28,30},{32,34}... | collective-permute-start | bytes 1572872 | tf_op jit(solution)/shard_map/ppermute | solution.py:338
  32.5 20.2 %collective-permute-start.10 = (f32[256,512]{1,0:T(8,128)S(1)}, f32[256,512]{1,0:T(8,128)S(1)}, u32[]{:S(2)}, u32[]{:S(2)}) collective-permute-start(f32[256,512]{1,0:T(8,128)S(1)} %get-tuple-element.35.refs_2_), channel_id=1, source_target_pairs={{2,4},{6,8},{10,12},{14,16},{18,20},{22,24},{26,28},{30,32},{34,36... | collective-permute-start | bytes 1572872 | tf_op jit(solution)/shard_map/ppermute | solution.py:338
  33.8 15.9 %collective-permute-start.6 = (f32[256,512]{1,0:T(8,128)S(1)}, f32[256,512]{1,0:T(8,128)S(1)}, u32[]{:S(2)}, u32[]{:S(2)}) collective-permute-start(f32[256,512]{1,0:T(8,128)S(1)} %get-tuple-element.35.refs_2_), channel_id=1, source_target_pairs={{2,0},{6,4},{10,8},{14,12},{18,16},{22,20},{26,24},{30,28},{34,32}... | collective-permute-start | bytes 1572872 | tf_op jit(solution)/shard_map/ppermute | solution.py:341
  38.5 22.1 %collective-permute-start.11 = (f32[640,128]{1,0:T(8,128)S(1)}, f32[640,128]{1,0:T(8,128)S(1)}, u32[]{:S(2)}, u32[]{:S(2)}) collective-permute-start(f32[640,128]{1,0:T(8,128)S(1)} %get-tuple-element.37), channel_id=1, source_target_pairs={{2,4},{6,8},{10,12},{14,16},{18,20},{22,24},{26,28},{30,32},{34,36... | collective-permute-start | bytes 983048 | tf_op jit(solution)/shard_map/ppermute | solution.py:338
  39.8 20.8 %collective-permute-start.8 = (f32[640,128]{1,0:T(8,128)S(1)}, f32[640,128]{1,0:T(8,128)S(1)}, u32[]{:S(2)}, u32[]{:S(2)}) collective-permute-start(f32[640,128]{1,0:T(8,128)S(1)} %get-tuple-element.37), channel_id=1, source_target_pairs={{2,0},{6,4},{10,8},{14,12},{18,16},{22,20},{26,24},{30,28},{34,32}... | collective-permute-start | bytes 983048 | tf_op jit(solution)/shard_map/ppermute | solution.py:341
  49.7 12.9 %collective-permute-start.7 = (f32[256,512]{1,0:T(8,128)S(1)}, f32[256,512]{1,0:T(8,128)S(1)}, u32[]{:S(2)}, u32[]{:S(2)}) collective-permute-start(f32[256,512]{1,0:T(8,128)S(1)} %collective-permute-done.6.refs_4_.refs_7_), channel_id=1, source_target_pairs={{0,1},{1,0},{2,3},{3,2},{4,5},{5,4},{6,7},{7,6},{8,9},{9,8},{10,11... | collective-permute-start | bytes 1572872 | tf_op jit(solution)/shard_map/ppermute | solution.py:335
  53.3 15.6 %collective-permute-start.14 = (f32[256,512]{1,0:T(8,128)S(1)}, f32[256,512]{1,0:T(8,128)S(1)}, u32[]{:S(2)}, u32[]{:S(2)}) collective-permute-start(f32[256,512]{1,0:T(8,128)S(1)} %get-tuple-element.45), channel_id=1, source_target_pairs={{2,0},{6,4},{10,8},{14,12},{18,16},{22,20},{26,24},{30,28},{34,32}... | collective-permute-start | bytes 1572872 | tf_op jit(solution)/shard_map/ppermute | solution.py:341
  54.6 19.3 %collective-permute-start.15 = (f32[256,512]{1,0:T(8,128)S(1)}, f32[256,512]{1,0:T(8,128)S(1)}, u32[]{:S(2)}, u32[]{:S(2)}) collective-permute-start(f32[256,512]{1,0:T(8,128)S(1)} %get-tuple-element.46), channel_id=1, source_target_pairs={{2,4},{6,8},{10,12},{14,16},{18,20},{22,24},{26,28},{30,32},{34,36... | collective-permute-start | bytes 1572872 | tf_op jit(solution)/shard_map/ppermute | solution.py:338
  60.6 1.6 %collective-permute-start.12 = (f32[640,128]{1,0:T(8,128)S(1)}, f32[640,128]{1,0:T(8,128)S(1)}, u32[]{:S(2)}, u32[]{:S(2)}) collective-permute-start(f32[640,128]{1,0:T(8,128)S(1)} %collective-permute-done.11.refs_9_), channel_id=1, source_target_pairs={{0,1},{1,0},{2,3},{3,2},{4,5},{5,4},{6,7},{7,6},{8,9},{9,8},{10,11... | collective-permute-start | bytes 983048 | tf_op jit(solution)/shard_map/ppermute | solution.py:335
  60.6 2.1 %collective-permute-start.9 = (f32[640,128]{1,0:T(8,128)S(1)}, f32[640,128]{1,0:T(8,128)S(1)}, u32[]{:S(2)}, u32[]{:S(2)}) collective-permute-start(f32[640,128]{1,0:T(8,128)S(1)} %collective-permute-done.8.refs_6_), channel_id=1, source_target_pairs={{0,1},{1,0},{2,3},{3,2},{4,5},{5,4},{6,7},{7,6},{8,9},{9,8},{10,11... | collective-permute-start | bytes 983048 | tf_op jit(solution)/shard_map/ppermute | solution.py:335

commit v4 on v3

--- a/solution.py
+++ b/solution.py
@@ -307,8 +307,8 @@
     )
 
 
-def level1_sources(info, f, gr, gl, far, ue, f_in):
-    def kernel(info_ref, f_ref, gr_ref, gl_ref, fh_ref, fl_ref, uh_ref, ul_ref, fin_ref, out_ref):
+def level1_sources(info, f, gl, gr, ue, far, f_in):
+    def kernel(info_ref, f_ref, gl_ref, gr_ref, uh_ref, ul_ref, fh_ref, fl_ref, fin_ref, out_ref):
         out_ref[1] = fin_ref[1]
 
         @pl.when(info_ref[2] > 0)
@@ -323,7 +323,7 @@
                 - dot3(halves(gl_ref[...]), (uh_ref[...], ul_ref[...]))
             )
 
-    return call(kernel, [PAIR], [info, f, gr, gl, *far, *ue, f_in], [], 3)[0]
+    return call(kernel, [PAIR], [info, f, gl, gr, *ue, *far, f_in], [], 3)[0]
 
 
 def body(diagonal_blocks, upper_blocks, right_sides):
@@ -371,7 +371,7 @@
         info, d_mid, u_odd, u_even, (ur, urx, zr, swap(zr)), (ul, zl, swap(zl)),
         diagonal_blocks, upper_blocks, u_other,
     )
-    f_out = level1_sources(info, f_mid, gr, gl, (fh, fl), (uh, uw), right_sides)
+    f_out = level1_sources(info, f_mid, gl, gr, (uh, uw), (fh, fl), right_sides)
     return d_out, u_out, f_out
 
 

time: 76.8 us -> 75.5 us (0.983)
  waiting for transfers between devices: 31.3 us -> 30 us
    ppermute x6, waiting for transfers between devices: 20.8 us -> 19.5 us  [onward(): lax.ppermute(a, 'tm', [(i, i + 1) for i in range(first, chips - 1, step)])]
where the time goes in v4:
time: 75.5 us; the launch traced here: 75.2 us
  waiting for transfers between devices  30 us (40%)
  Pallas kernels  26.2 us (35%)
  starting transfers between devices  17 us (23%)
  local copies, waits for them, and re-layouts  1.09 us (1%)
  between operations  0.82 us (1%)
    pallas_call x7, Pallas kernels, call(): pl.pallas_call(entry, out_shape=[jax.ShapeDtypeStruct(o, kind) for o, kin...  26.2 us
    ppermute x6, waiting for transfers between devices, onward(): lax.ppermute(a, 'tm', [(i, i + 1) for i in range(first, chips - 1, step)])  19.5 us
    ppermute x6, starting transfers between devices, onward(): lax.ppermute(a, 'tm', [(i, i + 1) for i in range(first, chips - 1, step)])  12 us
    ppermute x3, waiting for transfers between devices, odd_left(): return lax.ppermute(a, 'tm', [(i, i - 1) for i in range(1, chips, 2)])  8.68 us
    ppermute x3, starting transfers between devices, odd_left(): return lax.ppermute(a, 'tm', [(i, i - 1) for i in range(1, chips, 2)])  3.88 us
    ppermute x7, waiting for transfers between devices, swap(): return lax.ppermute(a, 'col', [(0, 1), (1, 0)])  1.9 us
  transfers between devices with their start and end apart: 16, of which 9 were waited for; matrix products, arithmetic and copies ran while one was open for 2% of the time, Pallas kernels for 31%

profile of v4, /device:TPU:64, one launch (start us, length us, event | category | flops | bytes accessed | tf_op | source)
XLA Modules:
  0.0 75.2 jit_solution(16361956665066499123)
XLA Ops:
  0.6 0.0 copy-start.2
  0.6 0.1 collective-permute-start
  0.7 0.5 collective-permute-start.2
  1.2 1.1 %slice_bitcast_fusion = f32[256,512]{1,0:T(8,128)S(1)} fusion(f32[2,256,512]{2,1,0:T(8,128)} %refs_12_.1), kind=kLoop, calls=%fused_computation | loop fusion | bytes 1048576 | tf_op jit(solution)/shard_map/squeeze | solution.py:347
  2.3 3.4 %collective-permute-start.3 = (f32[256,512]{1,0:T(8,128)S(1)}, f32[256,512]{1,0:T(8,128)S(1)}, u32[]{:S(2)}, u32[]{:S(2)}) collective-permute-start(f32[256,512]{1,0:T(8,128)S(1)} %slice_bitcast_fusion), channel_id=1, source_target_pairs={{0,2},{2,4},{4,6},{6,8},{8,10},{10,12},{12,14},{14,16},{16,18},{18... | collective-permute-start | bytes 1572872 | tf_op jit(solution)/shard_map/ppermute | solution.py:338
  5.7 0.1 pad_add_fusion.refs_0_
  5.8 0.0 copy-start
  5.8 0.0 copy-start.1
  5.8 0.0 collective-permute-done.refs_2_.refs_5_
  5.8 0.0 copy-done.2
  5.8 8.9 %shard_map.58 = (f32[512,512]{1,0:T(8,128)S(1)}, f32[640,128]{1,0:T(8,128)S(1)}) custom-call(s32[3]{0:T(128)S(1)} %pad_add_fusion.refs_0_, f32[2,256,512]{2,1,0:T(8,128)S(1)} %copy-done.2, f32[2,256,512]{2,1,0:T(8,128)} %collective-permute-done.refs_2_.refs_5_), custom_call_target="tpu_custom_call" | custom-call | flops 5368709120 | bytes 2621440 | tf_op jit(solution)/shard_map/pallas_call | solution.py:172
  14.8 3.4 %collective-permute-start.1 = (f32[640,128]{1,0:T(8,128)S(1)}, f32[640,128]{1,0:T(8,128)S(1)}, u32[]{:S(2)}, u32[]{:S(2)}) collective-permute-start(f32[640,128]{1,0:T(8,128)S(1)} %get-tuple-element.27), channel_id=1, source_target_pairs={{0,2},{2,4},{4,6},{6,8},{8,10},{10,12},{12,14},{14,16},{16,18},{18... | collective-permute-start | bytes 983048 | tf_op jit(solution)/shard_map/ppermute | solution.py:338
  18.2 4.2 %collective-permute-done.3.refs_7_.refs_5_.refs_8_ = f32[256,512]{1,0:T(8,128)S(1)} collective-permute-done((f32[256,512]{1,0:T(8,128)S(1)}, f32[256,512]{1,0:T(8,128)S(1)}, u32[]{:S(2)}, u32[]{:S(2)}) %collective-permute-start.3) | collective-permute-done | bytes 524320 | tf_op jit(solution)/shard_map/ppermute | solution.py:338
  22.3 0.0 collective-permute-start.5
  22.3 0.0 collective-permute-done.2.refs_3_.refs_4_.refs_7_.refs_13_
  22.4 0.0 copy-done
  22.4 0.0 copy-done.1
  22.4 4.0 %shard_map.59 = (f32[512,512]{1,0:T(8,128)S(1)}, f32[256,512]{1,0:T(8,128)S(1)}, f32[512,512]{1,0:T(8,128)S(1)}, f32[256,512]{1,0:T(8,128)S(1)}) custom-call(s32[3]{0:T(128)S(1)} %pad_add_fusion.refs_0_, f32[512,512]{1,0:T(8,128)S(1)} %get-tuple-element.28.refs_1_, f32[2,256,512]{2,1,0:T(8,128)S(1)} %copy-done, ...), custom_call_target="tpu_custom_call" | custom-call | flops 2415919104 | bytes 5767168 | tf_op jit(solution)/shard_map/pallas_call | solution.py:172
  26.4 4.0 %collective-permute-done.1.refs_1_.refs_4_ = f32[640,128]{1,0:T(8,128)S(1)} collective-permute-done((f32[640,128]{1,0:T(8,128)S(1)}, f32[640,128]{1,0:T(8,128)S(1)}, u32[]{:S(2)}, u32[]{:S(2)}) %collective-permute-start.1) | collective-permute-done | bytes 327712 | tf_op jit(solution)/shard_map/ppermute | solution.py:338
  30.3 0.0 collective-permute-start.4
  30.3 1.3 %collective-permute-start.13 = (f32[256,512]{1,0:T(8,128)S(1)}, f32[256,512]{1,0:T(8,128)S(1)}, u32[]{:S(2)}, u32[]{:S(2)}) collective-permute-start(f32[256,512]{1,0:T(8,128)S(1)} %get-tuple-element.41.refs_5_), channel_id=1, source_target_pairs={{0,2},{4,6},{8,10},{12,14},{16,18},{20,22},{24,26},{28,30},{32,34}... | collective-permute-start | bytes 1572872 | tf_op jit(solution)/shard_map/ppermute | solution.py:338
  31.7 0.3 collective-permute-done.4.refs_2_.refs_5_
  32.0 0.5 shard_map.60
  32.5 1.3 %collective-permute-start.10 = (f32[256,512]{1,0:T(8,128)S(1)}, f32[256,512]{1,0:T(8,128)S(1)}, u32[]{:S(2)}, u32[]{:S(2)}) collective-permute-start(f32[256,512]{1,0:T(8,128)S(1)} %get-tuple-element.35.refs_2_), channel_id=1, source_target_pairs={{2,4},{6,8},{10,12},{14,16},{18,20},{22,24},{26,28},{30,32},{34,36... | collective-permute-start | bytes 1572872 | tf_op jit(solution)/shard_map/ppermute | solution.py:338
  33.8 1.3 %collective-permute-start.6 = (f32[256,512]{1,0:T(8,128)S(1)}, f32[256,512]{1,0:T(8,128)S(1)}, u32[]{:S(2)}, u32[]{:S(2)}) collective-permute-start(f32[256,512]{1,0:T(8,128)S(1)} %get-tuple-element.35.refs_2_), channel_id=1, source_target_pairs={{2,0},{6,4},{10,8},{14,12},{18,16},{22,20},{26,24},{30,28},{34,32}... | collective-permute-start | bytes 1572872 | tf_op jit(solution)/shard_map/ppermute | solution.py:341
  35.1 0.0 collective-permute-done.5.refs_9_
  35.1 3.3 %shard_map.61 = (f32[256,512]{1,0:T(8,128)S(1)}, f32[512,512]{1,0:T(8,128)S(1)}, f32[512,512]{1,0:T(8,128)S(1)}, f32[640,128]{1,0:T(8,128)S(1)}) custom-call(s32[3]{0:T(128)S(1)} %pad_add_fusion.refs_0_, f32[512,512]{1,0:T(8,128)S(1)} %get-tuple-element.30.refs_1_, f32[512,512]{1,0:T(8,128)S(1)} %get-tuple-element.32.refs_2_, ...), custom_call_target="tpu_custom_call" | custom-call | flops 6442450944 | bytes 7340032 | tf_op jit(solution)/shard_map/pallas_call | solution.py:172
  38.5 1.3 %collective-permute-start.11 = (f32[640,128]{1,0:T(8,128)S(1)}, f32[640,128]{1,0:T(8,128)S(1)}, u32[]{:S(2)}, u32[]{:S(2)}) collective-permute-start(f32[640,128]{1,0:T(8,128)S(1)} %get-tuple-element.37), channel_id=1, source_target_pairs={{2,4},{6,8},{10,12},{14,16},{18,20},{22,24},{26,28},{30,32},{34,36... | collective-permute-start | bytes 983048 | tf_op jit(solution)/shard_map/ppermute | solution.py:338
  39.8 1.3 %collective-permute-start.8 = (f32[640,128]{1,0:T(8,128)S(1)}, f32[640,128]{1,0:T(8,128)S(1)}, u32[]{:S(2)}, u32[]{:S(2)}) collective-permute-start(f32[640,128]{1,0:T(8,128)S(1)} %get-tuple-element.37), channel_id=1, source_target_pairs={{2,0},{6,4},{10,8},{14,12},{18,16},{22,20},{26,24},{30,28},{34,32}... | collective-permute-start | bytes 983048 | tf_op jit(solution)/shard_map/ppermute | solution.py:341
  41.1 8.7 %collective-permute-done.6.refs_4_.refs_7_ = f32[256,512]{1,0:T(8,128)S(1)} collective-permute-done((f32[256,512]{1,0:T(8,128)S(1)}, f32[256,512]{1,0:T(8,128)S(1)}, u32[]{:S(2)}, u32[]{:S(2)}) %collective-permute-start.6) | collective-permute-done | bytes 524320 | tf_op jit(solution)/shard_map/ppermute | solution.py:341
  49.7 0.0 collective-permute-start.7
  49.8 0.0 collective-permute-done.13.refs_2_
  49.8 2.9 %collective-permute-done.10.refs_8_ = f32[256,512]{1,0:T(8,128)S(1)} collective-permute-done((f32[256,512]{1,0:T(8,128)S(1)}, f32[256,512]{1,0:T(8,128)S(1)}, u32[]{:S(2)}, u32[]{:S(2)}) %collective-permute-start.10) | collective-permute-done | bytes 524320 | tf_op jit(solution)/shard_map/ppermute | solution.py:338
  52.7 0.6 shard_map.63
  53.3 1.3 %collective-permute-start.14 = (f32[256,512]{1,0:T(8,128)S(1)}, f32[256,512]{1,0:T(8,128)S(1)}, u32[]{:S(2)}, u32[]{:S(2)}) collective-permute-start(f32[256,512]{1,0:T(8,128)S(1)} %get-tuple-element.45), channel_id=1, source_target_pairs={{2,4},{6,8},{10,12},{14,16},{18,20},{22,24},{26,28},{30,32},{34,36... | collective-permute-start | bytes 1572872 | tf_op jit(solution)/shard_map/ppermute | solution.py:338
  54.6 1.3 %collective-permute-start.15 = (f32[256,512]{1,0:T(8,128)S(1)}, f32[256,512]{1,0:T(8,128)S(1)}, u32[]{:S(2)}, u32[]{:S(2)}) collective-permute-start(f32[256,512]{1,0:T(8,128)S(1)} %get-tuple-element.46), channel_id=1, source_target_pairs={{2,0},{6,4},{10,8},{14,12},{18,16},{22,20},{26,24},{30,28},{34,32}... | collective-permute-start | bytes 1572872 | tf_op jit(solution)/shard_map/ppermute | solution.py:341
  55.9 4.7 %collective-permute-done.11.refs_9_ = f32[640,128]{1,0:T(8,128)S(1)} collective-permute-done((f32[640,128]{1,0:T(8,128)S(1)}, f32[640,128]{1,0:T(8,128)S(1)}, u32[]{:S(2)}, u32[]{:S(2)}) %collective-permute-start.11) | collective-permute-done | bytes 327712 | tf_op jit(solution)/shard_map/ppermute | solution.py:338
  60.6 0.0 collective-permute-start.12
  60.6 0.0 collective-permute-done.8.refs_6_
  60.6 0.5 collective-permute-start.9
  61.1 1.1 %collective-permute-done.12.refs_10_ = f32[640,128]{1,0:T(8,128)S(1)} collective-permute-done((f32[640,128]{1,0:T(8,128)S(1)}, f32[640,128]{1,0:T(8,128)S(1)}, u32[]{:S(2)}, u32[]{:S(2)}) %collective-permute-start.12) | collective-permute-done | bytes 327712 | tf_op jit(solution)/shard_map/ppermute | solution.py:335
  62.2 0.5 collective-permute-done.9.refs_7_
  62.7 0.0 collective-permute-done.7.refs_5_
  62.7 6.2 %shard_map.62 = (f32[2,256,512]{2,1,0:T(8,128)}, f32[2,256,512]{2,1,0:T(8,128)}, bf16[512,512]{1,0:T(8,128)(2,1)S(1)}, bf16[512,512]{1,0:T(8,128)(2,1)S(1)}, bf1...) custom-call(s32[3]{0:T(128)S(1)} %pad_add_fusion.refs_0_, f32[256,512]{1,0:T(8,128)S(1)} %get-tuple-element.34.refs_1_, ...), custom_call_target="tpu_custom_call" | custom-call | bytes 10485760 | tf_op jit(solution)/shard_map/pallas_call | solution.py:172
  68.9 3.7 %collective-permute-done.14.refs_2_ = f32[256,512]{1,0:T(8,128)S(1)} collective-permute-done((f32[256,512]{1,0:T(8,128)S(1)}, f32[256,512]{1,0:T(8,128)S(1)}, u32[]{:S(2)}, u32[]{:S(2)}) %collective-permute-start.14) | collective-permute-done | bytes 524320 | tf_op jit(solution)/shard_map/ppermute | solution.py:338
  72.6 0.0 collective-permute-done.15.refs_3_
  72.6 2.6 %shard_map.64 = f32[2,256,512]{2,1,0:T(8,128)} custom-call(s32[3]{0:T(128)S(1)} %pad_add_fusion.refs_0_, f32[256,512]{1,0:T(8,128)S(1)} %get-tuple-element.44.refs_1_, f32[256,512]{1,0:T(8,128)S(1)} %collective-permute-done.14.refs_2_, f32[256,512]{1,0:T(8,128)S(1)} %collective-permute-done.15.refs_3_, bf16[512,512]{1,0:T(8,128)(2,1)S(1)} %get-tuple-element.47.refs_4_, ...), custom_call_target="tpu_custom_call" | custom-call | flops 805306368 | bytes 5242880 | tf_op jit(solution)/shard_map/pallas_call | solution.py:172
Async XLA Ops:
  0.6 5.2 %copy-start.2 = (f32[2,256,512]{2,1,0:T(8,128)S(1)}, f32[2,256,512]{2,1,0:T(8,128)}, u32[]{:S(2)}) copy-start(f32[2,256,512]{2,1,0:T(8,128)} %refs_11_.1) | copy-start | bytes 3145732
  0.6 5.2 %collective-permute-start = (f32[2,256,512]{2,1,0:T(8,128)}, f32[2,256,512]{2,1,0:T(8,128)}, u32[]{:S(2)}, u32[]{:S(2)}) collective-permute-start(f32[2,256,512]{2,1,0:T(8,128)} %refs_11_.1), channel_id=1, source_target_pairs={{0,1},{1,0},{2,3},{3,2},{4,5},{5,4},{6,7},{7,6},{8,9},{9,8},{10,11... | collective-permute-start | bytes 3145736 | tf_op jit(solution)/shard_map/ppermute | solution.py:335
  0.7 21.6 %collective-permute-start.2 = (f32[2,256,512]{2,1,0:T(8,128)}, f32[2,256,512]{2,1,0:T(8,128)S(1)}, u32[]{:S(2)}, u32[]{:S(2)}) collective-permute-start(f32[2,256,512]{2,1,0:T(8,128)} %refs_12_.1), channel_id=1, source_target_pairs={{0,1},{1,0},{2,3},{3,2},{4,5},{5,4},{6,7},{7,6},{8,9},{9,8},{10,11... | collective-permute-start | bytes 3145736 | tf_op jit(solution)/shard_map/ppermute | solution.py:335
  2.3 20.0 %collective-permute-start.3 = (f32[256,512]{1,0:T(8,128)S(1)}, f32[256,512]{1,0:T(8,128)S(1)}, u32[]{:S(2)}, u32[]{:S(2)}) collective-permute-start(f32[256,512]{1,0:T(8,128)S(1)} %slice_bitcast_fusion), channel_id=1, source_target_pairs={{0,2},{2,4},{4,6},{6,8},{8,10},{10,12},{12,14},{14,16},{16,18},{18... | collective-permute-start | bytes 1572872 | tf_op jit(solution)/shard_map/ppermute | solution.py:338
  5.8 16.5 %copy-start = (f32[2,256,512]{2,1,0:T(8,128)S(1)}, f32[2,256,512]{2,1,0:T(8,128)}, u32[]{:S(2)}) copy-start(f32[2,256,512]{2,1,0:T(8,128)} %refs_12_.1) | copy-start | bytes 3145732
  5.8 16.6 %copy-start.1 = (f32[2,256,512]{2,1,0:T(8,128)S(1)}, f32[2,256,512]{2,1,0:T(8,128)}, u32[]{:S(2)}) copy-start(f32[2,256,512]{2,1,0:T(8,128)} %refs_8_.1) | copy-start | bytes 3145732
  14.8 15.5 %collective-permute-start.1 = (f32[640,128]{1,0:T(8,128)S(1)}, f32[640,128]{1,0:T(8,128)S(1)}, u32[]{:S(2)}, u32[]{:S(2)}) collective-permute-start(f32[640,128]{1,0:T(8,128)S(1)} %get-tuple-element.27), channel_id=1, source_target_pairs={{0,2},{2,4},{4,6},{6,8},{8,10},{10,12},{12,14},{14,16},{16,18},{18... | collective-permute-start | bytes 983048 | tf_op jit(solution)/shard_map/ppermute | solution.py:338
  22.3 12.8 %collective-permute-start.5 = (f32[256,512]{1,0:T(8,128)S(1)}, f32[256,512]{1,0:T(8,128)S(1)}, u32[]{:S(2)}, u32[]{:S(2)}) collective-permute-start(f32[256,512]{1,0:T(8,128)S(1)} %collective-permute-done.3.refs_7_.refs_5_.refs_8_), channel_id=1, source_target_pairs={{0,1},{1,0},{2,3},{3,2},{4,5},{5,4},{6,7},{7,6},{8,9},{9,8},{10,11... | collective-permute-start | bytes 1572872 | tf_op jit(solution)/shard_map/ppermute | solution.py:335
  30.3 1.6 %collective-permute-start.4 = (f32[640,128]{1,0:T(8,128)S(1)}, f32[640,128]{1,0:T(8,128)S(1)}, u32[]{:S(2)}, u32[]{:S(2)}) collective-permute-start(f32[640,128]{1,0:T(8,128)S(1)} %collective-permute-done.1.refs_1_.refs_4_), channel_id=1, source_target_pairs={{0,1},{1,0},{2,3},{3,2},{4,5},{5,4},{6,7},{7,6},{8,9},{9,8},{10,11... | collective-permute-start | bytes 983048 | tf_op jit(solution)/shard_map/ppermute | solution.py:335
  30.3 19.4 %collective-permute-start.13 = (f32[256,512]{1,0:T(8,128)S(1)}, f32[256,512]{1,0:T(8,128)S(1)}, u32[]{:S(2)}, u32[]{:S(2)}) collective-permute-start(f32[256,512]{1,0:T(8,128)S(1)} %get-tuple-element.41.refs_5_), channel_id=1, source_target_pairs={{0,2},{4,6},{8,10},{12,14},{16,18},{20,22},{24,26},{28,30},{32,34}... | collective-permute-start | bytes 1572872 | tf_op jit(solution)/shard_map/ppermute | solution.py:338
  32.5 20.2 %collective-permute-start.10 = (f32[256,512]{1,0:T(8,128)S(1)}, f32[256,512]{1,0:T(8,128)S(1)}, u32[]{:S(2)}, u32[]{:S(2)}) collective-permute-start(f32[256,512]{1,0:T(8,128)S(1)} %get-tuple-element.35.refs_2_), channel_id=1, source_target_pairs={{2,4},{6,8},{10,12},{14,16},{18,20},{22,24},{26,28},{30,32},{34,36... | collective-permute-start | bytes 1572872 | tf_op jit(solution)/shard_map/ppermute | solution.py:338
  33.8 15.9 %collective-permute-start.6 = (f32[256,512]{1,0:T(8,128)S(1)}, f32[256,512]{1,0:T(8,128)S(1)}, u32[]{:S(2)}, u32[]{:S(2)}) collective-permute-start(f32[256,512]{1,0:T(8,128)S(1)} %get-tuple-element.35.refs_2_), channel_id=1, source_target_pairs={{2,0},{6,4},{10,8},{14,12},{18,16},{22,20},{26,24},{30,28},{34,32}... | collective-permute-start | bytes 1572872 | tf_op jit(solution)/shard_map/ppermute | solution.py:341
  38.5 22.1 %collective-permute-start.11 = (f32[640,128]{1,0:T(8,128)S(1)}, f32[640,128]{1,0:T(8,128)S(1)}, u32[]{:S(2)}, u32[]{:S(2)}) collective-permute-start(f32[640,128]{1,0:T(8,128)S(1)} %get-tuple-element.37), channel_id=1, source_target_pairs={{2,4},{6,8},{10,12},{14,16},{18,20},{22,24},{26,28},{30,32},{34,36... | collective-permute-start | bytes 983048 | tf_op jit(solution)/shard_map/ppermute | solution.py:338
  39.8 20.8 %collective-permute-start.8 = (f32[640,128]{1,0:T(8,128)S(1)}, f32[640,128]{1,0:T(8,128)S(1)}, u32[]{:S(2)}, u32[]{:S(2)}) collective-permute-start(f32[640,128]{1,0:T(8,128)S(1)} %get-tuple-element.37), channel_id=1, source_target_pairs={{2,0},{6,4},{10,8},{14,12},{18,16},{22,20},{26,24},{30,28},{34,32}... | collective-permute-start | bytes 983048 | tf_op jit(solution)/shard_map/ppermute | solution.py:341
  49.7 12.9 %collective-permute-start.7 = (f32[256,512]{1,0:T(8,128)S(1)}, f32[256,512]{1,0:T(8,128)S(1)}, u32[]{:S(2)}, u32[]{:S(2)}) collective-permute-start(f32[256,512]{1,0:T(8,128)S(1)} %collective-permute-done.6.refs_4_.refs_7_), channel_id=1, source_target_pairs={{0,1},{1,0},{2,3},{3,2},{4,5},{5,4},{6,7},{7,6},{8,9},{9,8},{10,11... | collective-permute-start | bytes 1572872 | tf_op jit(solution)/shard_map/ppermute | solution.py:335
  53.3 19.3 %collective-permute-start.14 = (f32[256,512]{1,0:T(8,128)S(1)}, f32[256,512]{1,0:T(8,128)S(1)}, u32[]{:S(2)}, u32[]{:S(2)}) collective-permute-start(f32[256,512]{1,0:T(8,128)S(1)} %get-tuple-element.45), channel_id=1, source_target_pairs={{2,4},{6,8},{10,12},{14,16},{18,20},{22,24},{26,28},{30,32},{34,36... | collective-permute-start | bytes 1572872 | tf_op jit(solution)/shard_map/ppermute | solution.py:338
  54.6 18.0 %collective-permute-start.15 = (f32[256,512]{1,0:T(8,128)S(1)}, f32[256,512]{1,0:T(8,128)S(1)}, u32[]{:S(2)}, u32[]{:S(2)}) collective-permute-start(f32[256,512]{1,0:T(8,128)S(1)} %get-tuple-element.46), channel_id=1, source_target_pairs={{2,0},{6,4},{10,8},{14,12},{18,16},{22,20},{26,24},{30,28},{34,32}... | collective-permute-start | bytes 1572872 | tf_op jit(solution)/shard_map/ppermute | solution.py:341
  60.6 1.6 %collective-permute-start.12 = (f32[640,128]{1,0:T(8,128)S(1)}, f32[640,128]{1,0:T(8,128)S(1)}, u32[]{:S(2)}, u32[]{:S(2)}) collective-permute-start(f32[640,128]{1,0:T(8,128)S(1)} %collective-permute-done.11.refs_9_), channel_id=1, source_target_pairs={{0,1},{1,0},{2,3},{3,2},{4,5},{5,4},{6,7},{7,6},{8,9},{9,8},{10,11... | collective-permute-start | bytes 983048 | tf_op jit(solution)/shard_map/ppermute | solution.py:335
  60.6 2.1 %collective-permute-start.9 = (f32[640,128]{1,0:T(8,128)S(1)}, f32[640,128]{1,0:T(8,128)S(1)}, u32[]{:S(2)}, u32[]{:S(2)}) collective-permute-start(f32[640,128]{1,0:T(8,128)S(1)} %collective-permute-done.8.refs_6_), channel_id=1, source_target_pairs={{0,1},{1,0},{2,3},{3,2},{4,5},{5,4},{6,7},{7,6},{8,9},{9,8},{10,11... | collective-permute-start | bytes 983048 | tf_op jit(solution)/shard_map/ppermute | solution.py:335

commit v5 on v4

--- a/solution.py
+++ b/solution.py
@@ -288,7 +288,7 @@
             uh_ref[...], uw_ref[...] = halves(far_ref[...])
             join(info_ref, ur_ref, urx_ref, far_ref)
             far = halves(far_ref[...])
-            fh_ref[...], fl_ref[...] = far
+            fh_ref[...], fl_ref[...] = halves(far_ref[...].T)
             mid = halves(mid_ref[...])
             unpack(info_ref, zr_ref, zrx_ref, z_ref)
             v = dot3(halves(ur_ref[...]), halves(z_ref[...]))
@@ -319,7 +319,7 @@
         def _():
             out_ref[0] = (
                 f_ref[...]
-                - dot3(halves(gr_ref[...]), (fh_ref[...], fl_ref[...]), NT)
+                - dot3(halves(gr_ref[...]), (fh_ref[...], fl_ref[...]))
                 - dot3(halves(gl_ref[...]), (uh_ref[...], ul_ref[...]))
             )
 

time: 75.5 us -> 75.5 us (level)
  transfers between devices with their start and end apart: 16 -> 16, of which waited for: 9 -> 9; matrix products, arithmetic and copies ran while one was open for 2% -> 2% of each run, Pallas kernels for 31% -> 32%
where the time goes in v5:
time: 75.5 us; the launch traced here: 75.2 us
  waiting for transfers between devices  30 us (40%)
  Pallas kernels  26.2 us (35%)
  starting transfers between devices  17 us (23%)
  local copies, waits for them, and re-layouts  1.09 us (1%)
  between operations  0.82 us (1%)
    pallas_call x7, Pallas kernels, call(): pl.pallas_call(entry, out_shape=[jax.ShapeDtypeStruct(o, kind) for o, kin...  26.2 us
    ppermute x6, waiting for transfers between devices, onward(): lax.ppermute(a, 'tm', [(i, i + 1) for i in range(first, chips - 1, step)])  19.4 us
    ppermute x6, starting transfers between devices, onward(): lax.ppermute(a, 'tm', [(i, i + 1) for i in range(first, chips - 1, step)])  12 us
    ppermute x3, waiting for transfers between devices, odd_left(): return lax.ppermute(a, 'tm', [(i, i - 1) for i in range(1, chips, 2)])  8.68 us
    ppermute x3, starting transfers between devices, odd_left(): return lax.ppermute(a, 'tm', [(i, i - 1) for i in range(1, chips, 2)])  3.88 us
    ppermute x7, waiting for transfers between devices, swap(): return lax.ppermute(a, 'col', [(0, 1), (1, 0)])  1.9 us
  transfers between devices with their start and end apart: 16, of which 9 were waited for; matrix products, arithmetic and copies ran while one was open for 2% of the time, Pallas kernels for 32%

profile of v5, /device:TPU:64, one launch (start us, length us, event | category | flops | bytes accessed | tf_op | source)
XLA Modules:
  0.0 75.2 jit_solution(11954877245772542741)
XLA Ops:
  0.6 0.0 copy-start.2
  0.6 0.1 collective-permute-start
  0.7 0.5 collective-permute-start.2
  1.2 1.1 %slice_bitcast_fusion = f32[256,512]{1,0:T(8,128)S(1)} fusion(f32[2,256,512]{2,1,0:T(8,128)} %refs_12_.1), kind=kLoop, calls=%fused_computation | loop fusion | bytes 1048576 | tf_op jit(solution)/shard_map/squeeze | solution.py:347
  2.3 3.4 %collective-permute-start.3 = (f32[256,512]{1,0:T(8,128)S(1)}, f32[256,512]{1,0:T(8,128)S(1)}, u32[]{:S(2)}, u32[]{:S(2)}) collective-permute-start(f32[256,512]{1,0:T(8,128)S(1)} %slice_bitcast_fusion), channel_id=1, source_target_pairs={{0,2},{2,4},{4,6},{6,8},{8,10},{10,12},{12,14},{14,16},{16,18},{18... | collective-permute-start | bytes 1572872 | tf_op jit(solution)/shard_map/ppermute | solution.py:338
  5.7 0.1 pad_add_fusion.refs_0_
  5.8 0.0 copy-start
  5.8 0.0 copy-start.1
  5.8 0.0 collective-permute-done.refs_2_.refs_5_
  5.8 0.0 copy-done.2
  5.8 8.9 %shard_map.58 = (f32[512,512]{1,0:T(8,128)S(1)}, f32[640,128]{1,0:T(8,128)S(1)}) custom-call(s32[3]{0:T(128)S(1)} %pad_add_fusion.refs_0_, f32[2,256,512]{2,1,0:T(8,128)S(1)} %copy-done.2, f32[2,256,512]{2,1,0:T(8,128)} %collective-permute-done.refs_2_.refs_5_), custom_call_target="tpu_custom_call" | custom-call | flops 5368709120 | bytes 2621440 | tf_op jit(solution)/shard_map/pallas_call | solution.py:172
  14.8 3.4 %collective-permute-start.1 = (f32[640,128]{1,0:T(8,128)S(1)}, f32[640,128]{1,0:T(8,128)S(1)}, u32[]{:S(2)}, u32[]{:S(2)}) collective-permute-start(f32[640,128]{1,0:T(8,128)S(1)} %get-tuple-element.27), channel_id=1, source_target_pairs={{0,2},{2,4},{4,6},{6,8},{8,10},{10,12},{12,14},{14,16},{16,18},{18... | collective-permute-start | bytes 983048 | tf_op jit(solution)/shard_map/ppermute | solution.py:338
  18.2 4.2 %collective-permute-done.3.refs_7_.refs_5_.refs_8_ = f32[256,512]{1,0:T(8,128)S(1)} collective-permute-done((f32[256,512]{1,0:T(8,128)S(1)}, f32[256,512]{1,0:T(8,128)S(1)}, u32[]{:S(2)}, u32[]{:S(2)}) %collective-permute-start.3) | collective-permute-done | bytes 524320 | tf_op jit(solution)/shard_map/ppermute | solution.py:338
  22.3 0.0 collective-permute-start.5
  22.3 0.0 collective-permute-done.2.refs_3_.refs_4_.refs_7_.refs_13_
  22.4 0.0 copy-done
  22.4 0.0 copy-done.1
  22.4 4.0 %shard_map.59 = (f32[512,512]{1,0:T(8,128)S(1)}, f32[256,512]{1,0:T(8,128)S(1)}, f32[512,512]{1,0:T(8,128)S(1)}, f32[256,512]{1,0:T(8,128)S(1)}) custom-call(s32[3]{0:T(128)S(1)} %pad_add_fusion.refs_0_, f32[512,512]{1,0:T(8,128)S(1)} %get-tuple-element.28.refs_1_, f32[2,256,512]{2,1,0:T(8,128)S(1)} %copy-done, ...), custom_call_target="tpu_custom_call" | custom-call | flops 2415919104 | bytes 5767168 | tf_op jit(solution)/shard_map/pallas_call | solution.py:172
  26.4 4.0 %collective-permute-done.1.refs_1_.refs_4_ = f32[640,128]{1,0:T(8,128)S(1)} collective-permute-done((f32[640,128]{1,0:T(8,128)S(1)}, f32[640,128]{1,0:T(8,128)S(1)}, u32[]{:S(2)}, u32[]{:S(2)}) %collective-permute-start.1) | collective-permute-done | bytes 327712 | tf_op jit(solution)/shard_map/ppermute | solution.py:338
  30.3 0.0 collective-permute-start.4
  30.3 1.3 %collective-permute-start.13 = (f32[256,512]{1,0:T(8,128)S(1)}, f32[256,512]{1,0:T(8,128)S(1)}, u32[]{:S(2)}, u32[]{:S(2)}) collective-permute-start(f32[256,512]{1,0:T(8,128)S(1)} %get-tuple-element.41.refs_5_), channel_id=1, source_target_pairs={{0,2},{4,6},{8,10},{12,14},{16,18},{20,22},{24,26},{28,30},{32,34}... | collective-permute-start | bytes 1572872 | tf_op jit(solution)/shard_map/ppermute | solution.py:338
  31.7 0.3 collective-permute-done.4.refs_2_.refs_5_
  32.0 0.5 shard_map.60
  32.5 1.3 %collective-permute-start.10 = (f32[256,512]{1,0:T(8,128)S(1)}, f32[256,512]{1,0:T(8,128)S(1)}, u32[]{:S(2)}, u32[]{:S(2)}) collective-permute-start(f32[256,512]{1,0:T(8,128)S(1)} %get-tuple-element.35.refs_2_), channel_id=1, source_target_pairs={{2,4},{6,8},{10,12},{14,16},{18,20},{22,24},{26,28},{30,32},{34,36... | collective-permute-start | bytes 1572872 | tf_op jit(solution)/shard_map/ppermute | solution.py:338
  33.8 1.3 %collective-permute-start.6 = (f32[256,512]{1,0:T(8,128)S(1)}, f32[256,512]{1,0:T(8,128)S(1)}, u32[]{:S(2)}, u32[]{:S(2)}) collective-permute-start(f32[256,512]{1,0:T(8,128)S(1)} %get-tuple-element.35.refs_2_), channel_id=1, source_target_pairs={{2,0},{6,4},{10,8},{14,12},{18,16},{22,20},{26,24},{30,28},{34,32}... | collective-permute-start | bytes 1572872 | tf_op jit(solution)/shard_map/ppermute | solution.py:341
  35.1 0.0 collective-permute-done.5.refs_9_
  35.1 3.3 %shard_map.61 = (f32[256,512]{1,0:T(8,128)S(1)}, f32[512,512]{1,0:T(8,128)S(1)}, f32[512,512]{1,0:T(8,128)S(1)}, f32[640,128]{1,0:T(8,128)S(1)}) custom-call(s32[3]{0:T(128)S(1)} %pad_add_fusion.refs_0_, f32[512,512]{1,0:T(8,128)S(1)} %get-tuple-element.30.refs_1_, f32[512,512]{1,0:T(8,128)S(1)} %get-tuple-element.32.refs_2_, ...), custom_call_target="tpu_custom_call" | custom-call | flops 6442450944 | bytes 7340032 | tf_op jit(solution)/shard_map/pallas_call | solution.py:172
  38.5 1.3 %collective-permute-start.11 = (f32[640,128]{1,0:T(8,128)S(1)}, f32[640,128]{1,0:T(8,128)S(1)}, u32[]{:S(2)}, u32[]{:S(2)}) collective-permute-start(f32[640,128]{1,0:T(8,128)S(1)} %get-tuple-element.37), channel_id=1, source_target_pairs={{2,4},{6,8},{10,12},{14,16},{18,20},{22,24},{26,28},{30,32},{34,36... | collective-permute-start | bytes 983048 | tf_op jit(solution)/shard_map/ppermute | solution.py:338
  39.8 1.3 %collective-permute-start.8 = (f32[640,128]{1,0:T(8,128)S(1)}, f32[640,128]{1,0:T(8,128)S(1)}, u32[]{:S(2)}, u32[]{:S(2)}) collective-permute-start(f32[640,128]{1,0:T(8,128)S(1)} %get-tuple-element.37), channel_id=1, source_target_pairs={{2,0},{6,4},{10,8},{14,12},{18,16},{22,20},{26,24},{30,28},{34,32}... | collective-permute-start | bytes 983048 | tf_op jit(solution)/shard_map/ppermute | solution.py:341
  41.1 8.7 %collective-permute-done.6.refs_4_.refs_7_ = f32[256,512]{1,0:T(8,128)S(1)} collective-permute-done((f32[256,512]{1,0:T(8,128)S(1)}, f32[256,512]{1,0:T(8,128)S(1)}, u32[]{:S(2)}, u32[]{:S(2)}) %collective-permute-start.6) | collective-permute-done | bytes 524320 | tf_op jit(solution)/shard_map/ppermute | solution.py:341
  49.7 0.0 collective-permute-start.7
  49.8 0.0 collective-permute-done.13.refs_2_
  49.8 2.9 %collective-permute-done.10.refs_8_ = f32[256,512]{1,0:T(8,128)S(1)} collective-permute-done((f32[256,512]{1,0:T(8,128)S(1)}, f32[256,512]{1,0:T(8,128)S(1)}, u32[]{:S(2)}, u32[]{:S(2)}) %collective-permute-start.10) | collective-permute-done | bytes 524320 | tf_op jit(solution)/shard_map/ppermute | solution.py:338
  52.7 0.6 shard_map.63
  53.3 1.3 %collective-permute-start.14 = (f32[256,512]{1,0:T(8,128)S(1)}, f32[256,512]{1,0:T(8,128)S(1)}, u32[]{:S(2)}, u32[]{:S(2)}) collective-permute-start(f32[256,512]{1,0:T(8,128)S(1)} %get-tuple-element.45), channel_id=1, source_target_pairs={{2,4},{6,8},{10,12},{14,16},{18,20},{22,24},{26,28},{30,32},{34,36... | collective-permute-start | bytes 1572872 | tf_op jit(solution)/shard_map/ppermute | solution.py:338
  54.6 1.3 %collective-permute-start.15 = (f32[256,512]{1,0:T(8,128)S(1)}, f32[256,512]{1,0:T(8,128)S(1)}, u32[]{:S(2)}, u32[]{:S(2)}) collective-permute-start(f32[256,512]{1,0:T(8,128)S(1)} %get-tuple-element.46), channel_id=1, source_target_pairs={{2,0},{6,4},{10,8},{14,12},{18,16},{22,20},{26,24},{30,28},{34,32}... | collective-permute-start | bytes 1572872 | tf_op jit(solution)/shard_map/ppermute | solution.py:341
  55.9 4.7 %collective-permute-done.11.refs_9_ = f32[640,128]{1,0:T(8,128)S(1)} collective-permute-done((f32[640,128]{1,0:T(8,128)S(1)}, f32[640,128]{1,0:T(8,128)S(1)}, u32[]{:S(2)}, u32[]{:S(2)}) %collective-permute-start.11) | collective-permute-done | bytes 327712 | tf_op jit(solution)/shard_map/ppermute | solution.py:338
  60.6 0.0 collective-permute-start.12
  60.6 0.0 collective-permute-done.8.refs_6_
  60.6 0.5 collective-permute-start.9
  61.1 1.1 %collective-permute-done.12.refs_10_ = f32[640,128]{1,0:T(8,128)S(1)} collective-permute-done((f32[640,128]{1,0:T(8,128)S(1)}, f32[640,128]{1,0:T(8,128)S(1)}, u32[]{:S(2)}, u32[]{:S(2)}) %collective-permute-start.12) | collective-permute-done | bytes 327712 | tf_op jit(solution)/shard_map/ppermute | solution.py:335
  62.2 0.5 collective-permute-done.9.refs_7_
  62.7 0.0 collective-permute-done.7.refs_5_
  62.7 6.3 %shard_map.62 = (f32[2,256,512]{2,1,0:T(8,128)}, f32[2,256,512]{2,1,0:T(8,128)}, bf16[512,512]{1,0:T(8,128)(2,1)S(1)}, bf16[512,512]{1,0:T(8,128)(2,1)S(1)}, bf1...) custom-call(s32[3]{0:T(128)S(1)} %pad_add_fusion.refs_0_, f32[256,512]{1,0:T(8,128)S(1)} %get-tuple-element.34.refs_1_, ...), custom_call_target="tpu_custom_call" | custom-call | bytes 10485760 | tf_op jit(solution)/shard_map/pallas_call | solution.py:172
  68.9 3.7 %collective-permute-done.14.refs_2_ = f32[256,512]{1,0:T(8,128)S(1)} collective-permute-done((f32[256,512]{1,0:T(8,128)S(1)}, f32[256,512]{1,0:T(8,128)S(1)}, u32[]{:S(2)}, u32[]{:S(2)}) %collective-permute-start.14) | collective-permute-done | bytes 524320 | tf_op jit(solution)/shard_map/ppermute | solution.py:338
  72.6 0.0 collective-permute-done.15.refs_3_
  72.6 2.6 %shard_map.64 = f32[2,256,512]{2,1,0:T(8,128)} custom-call(s32[3]{0:T(128)S(1)} %pad_add_fusion.refs_0_, f32[256,512]{1,0:T(8,128)S(1)} %get-tuple-element.44.refs_1_, f32[256,512]{1,0:T(8,128)S(1)} %collective-permute-done.14.refs_2_, f32[256,512]{1,0:T(8,128)S(1)} %collective-permute-done.15.refs_3_, bf16[512,512]{1,0:T(8,128)(2,1)S(1)} %get-tuple-element.47.refs_4_, ...), custom_call_target="tpu_custom_call" | custom-call | flops 805306368 | bytes 5242880 | tf_op jit(solution)/shard_map/pallas_call | solution.py:172
Async XLA Ops:
  0.6 5.2 %copy-start.2 = (f32[2,256,512]{2,1,0:T(8,128)S(1)}, f32[2,256,512]{2,1,0:T(8,128)}, u32[]{:S(2)}) copy-start(f32[2,256,512]{2,1,0:T(8,128)} %refs_11_.1) | copy-start | bytes 3145732
  0.6 5.2 %collective-permute-start = (f32[2,256,512]{2,1,0:T(8,128)}, f32[2,256,512]{2,1,0:T(8,128)}, u32[]{:S(2)}, u32[]{:S(2)}) collective-permute-start(f32[2,256,512]{2,1,0:T(8,128)} %refs_11_.1), channel_id=1, source_target_pairs={{0,1},{1,0},{2,3},{3,2},{4,5},{5,4},{6,7},{7,6},{8,9},{9,8},{10,11... | collective-permute-start | bytes 3145736 | tf_op jit(solution)/shard_map/ppermute | solution.py:335
  0.7 21.6 %collective-permute-start.2 = (f32[2,256,512]{2,1,0:T(8,128)}, f32[2,256,512]{2,1,0:T(8,128)S(1)}, u32[]{:S(2)}, u32[]{:S(2)}) collective-permute-start(f32[2,256,512]{2,1,0:T(8,128)} %refs_12_.1), channel_id=1, source_target_pairs={{0,1},{1,0},{2,3},{3,2},{4,5},{5,4},{6,7},{7,6},{8,9},{9,8},{10,11... | collective-permute-start | bytes 3145736 | tf_op jit(solution)/shard_map/ppermute | solution.py:335
  2.3 20.0 %collective-permute-start.3 = (f32[256,512]{1,0:T(8,128)S(1)}, f32[256,512]{1,0:T(8,128)S(1)}, u32[]{:S(2)}, u32[]{:S(2)}) collective-permute-start(f32[256,512]{1,0:T(8,128)S(1)} %slice_bitcast_fusion), channel_id=1, source_target_pairs={{0,2},{2,4},{4,6},{6,8},{8,10},{10,12},{12,14},{14,16},{16,18},{18... | collective-permute-start | bytes 1572872 | tf_op jit(solution)/shard_map/ppermute | solution.py:338
  5.8 16.5 %copy-start = (f32[2,256,512]{2,1,0:T(8,128)S(1)}, f32[2,256,512]{2,1,0:T(8,128)}, u32[]{:S(2)}) copy-start(f32[2,256,512]{2,1,0:T(8,128)} %refs_12_.1) | copy-start | bytes 3145732
  5.8 16.6 %copy-start.1 = (f32[2,256,512]{2,1,0:T(8,128)S(1)}, f32[2,256,512]{2,1,0:T(8,128)}, u32[]{:S(2)}) copy-start(f32[2,256,512]{2,1,0:T(8,128)} %refs_8_.1) | copy-start | bytes 3145732
  14.8 15.5 %collective-permute-start.1 = (f32[640,128]{1,0:T(8,128)S(1)}, f32[640,128]{1,0:T(8,128)S(1)}, u32[]{:S(2)}, u32[]{:S(2)}) collective-permute-start(f32[640,128]{1,0:T(8,128)S(1)} %get-tuple-element.27), channel_id=1, source_target_pairs={{0,2},{2,4},{4,6},{6,8},{8,10},{10,12},{12,14},{14,16},{16,18},{18... | collective-permute-start | bytes 983048 | tf_op jit(solution)/shard_map/ppermute | solution.py:338
  22.3 12.8 %collective-permute-start.5 = (f32[256,512]{1,0:T(8,128)S(1)}, f32[256,512]{1,0:T(8,128)S(1)}, u32[]{:S(2)}, u32[]{:S(2)}) collective-permute-start(f32[256,512]{1,0:T(8,128)S(1)} %collective-permute-done.3.refs_7_.refs_5_.refs_8_), channel_id=1, source_target_pairs={{0,1},{1,0},{2,3},{3,2},{4,5},{5,4},{6,7},{7,6},{8,9},{9,8},{10,11... | collective-permute-start | bytes 1572872 | tf_op jit(solution)/shard_map/ppermute | solution.py:335
  30.3 1.6 %collective-permute-start.4 = (f32[640,128]{1,0:T(8,128)S(1)}, f32[640,128]{1,0:T(8,128)S(1)}, u32[]{:S(2)}, u32[]{:S(2)}) collective-permute-start(f32[640,128]{1,0:T(8,128)S(1)} %collective-permute-done.1.refs_1_.refs_4_), channel_id=1, source_target_pairs={{0,1},{1,0},{2,3},{3,2},{4,5},{5,4},{6,7},{7,6},{8,9},{9,8},{10,11... | collective-permute-start | bytes 983048 | tf_op jit(solution)/shard_map/ppermute | solution.py:335
  30.3 19.4 %collective-permute-start.13 = (f32[256,512]{1,0:T(8,128)S(1)}, f32[256,512]{1,0:T(8,128)S(1)}, u32[]{:S(2)}, u32[]{:S(2)}) collective-permute-start(f32[256,512]{1,0:T(8,128)S(1)} %get-tuple-element.41.refs_5_), channel_id=1, source_target_pairs={{0,2},{4,6},{8,10},{12,14},{16,18},{20,22},{24,26},{28,30},{32,34}... | collective-permute-start | bytes 1572872 | tf_op jit(solution)/shard_map/ppermute | solution.py:338
  32.5 20.2 %collective-permute-start.10 = (f32[256,512]{1,0:T(8,128)S(1)}, f32[256,512]{1,0:T(8,128)S(1)}, u32[]{:S(2)}, u32[]{:S(2)}) collective-permute-start(f32[256,512]{1,0:T(8,128)S(1)} %get-tuple-element.35.refs_2_), channel_id=1, source_target_pairs={{2,4},{6,8},{10,12},{14,16},{18,20},{22,24},{26,28},{30,32},{34,36... | collective-permute-start | bytes 1572872 | tf_op jit(solution)/shard_map/ppermute | solution.py:338
  33.8 15.9 %collective-permute-start.6 = (f32[256,512]{1,0:T(8,128)S(1)}, f32[256,512]{1,0:T(8,128)S(1)}, u32[]{:S(2)}, u32[]{:S(2)}) collective-permute-start(f32[256,512]{1,0:T(8,128)S(1)} %get-tuple-element.35.refs_2_), channel_id=1, source_target_pairs={{2,0},{6,4},{10,8},{14,12},{18,16},{22,20},{26,24},{30,28},{34,32}... | collective-permute-start | bytes 1572872 | tf_op jit(solution)/shard_map/ppermute | solution.py:341
  38.5 22.1 %collective-permute-start.11 = (f32[640,128]{1,0:T(8,128)S(1)}, f32[640,128]{1,0:T(8,128)S(1)}, u32[]{:S(2)}, u32[]{:S(2)}) collective-permute-start(f32[640,128]{1,0:T(8,128)S(1)} %get-tuple-element.37), channel_id=1, source_target_pairs={{2,4},{6,8},{10,12},{14,16},{18,20},{22,24},{26,28},{30,32},{34,36... | collective-permute-start | bytes 983048 | tf_op jit(solution)/shard_map/ppermute | solution.py:338
  39.8 20.8 %collective-permute-start.8 = (f32[640,128]{1,0:T(8,128)S(1)}, f32[640,128]{1,0:T(8,128)S(1)}, u32[]{:S(2)}, u32[]{:S(2)}) collective-permute-start(f32[640,128]{1,0:T(8,128)S(1)} %get-tuple-element.37), channel_id=1, source_target_pairs={{2,0},{6,4},{10,8},{14,12},{18,16},{22,20},{26,24},{30,28},{34,32}... | collective-permute-start | bytes 983048 | tf_op jit(solution)/shard_map/ppermute | solution.py:341
  49.7 12.9 %collective-permute-start.7 = (f32[256,512]{1,0:T(8,128)S(1)}, f32[256,512]{1,0:T(8,128)S(1)}, u32[]{:S(2)}, u32[]{:S(2)}) collective-permute-start(f32[256,512]{1,0:T(8,128)S(1)} %collective-permute-done.6.refs_4_.refs_7_), channel_id=1, source_target_pairs={{0,1},{1,0},{2,3},{3,2},{4,5},{5,4},{6,7},{7,6},{8,9},{9,8},{10,11... | collective-permute-start | bytes 1572872 | tf_op jit(solution)/shard_map/ppermute | solution.py:335
  53.3 19.3 %collective-permute-start.14 = (f32[256,512]{1,0:T(8,128)S(1)}, f32[256,512]{1,0:T(8,128)S(1)}, u32[]{:S(2)}, u32[]{:S(2)}) collective-permute-start(f32[256,512]{1,0:T(8,128)S(1)} %get-tuple-element.45), channel_id=1, source_target_pairs={{2,4},{6,8},{10,12},{14,16},{18,20},{22,24},{26,28},{30,32},{34,36... | collective-permute-start | bytes 1572872 | tf_op jit(solution)/shard_map/ppermute | solution.py:338
  54.6 18.0 %collective-permute-start.15 = (f32[256,512]{1,0:T(8,128)S(1)}, f32[256,512]{1,0:T(8,128)S(1)}, u32[]{:S(2)}, u32[]{:S(2)}) collective-permute-start(f32[256,512]{1,0:T(8,128)S(1)} %get-tuple-element.46), channel_id=1, source_target_pairs={{2,0},{6,4},{10,8},{14,12},{18,16},{22,20},{26,24},{30,28},{34,32}... | collective-permute-start | bytes 1572872 | tf_op jit(solution)/shard_map/ppermute | solution.py:341
  60.6 1.6 %collective-permute-start.12 = (f32[640,128]{1,0:T(8,128)S(1)}, f32[640,128]{1,0:T(8,128)S(1)}, u32[]{:S(2)}, u32[]{:S(2)}) collective-permute-start(f32[640,128]{1,0:T(8,128)S(1)} %collective-permute-done.11.refs_9_), channel_id=1, source_target_pairs={{0,1},{1,0},{2,3},{3,2},{4,5},{5,4},{6,7},{7,6},{8,9},{9,8},{10,11... | collective-permute-start | bytes 983048 | tf_op jit(solution)/shard_map/ppermute | solution.py:335
  60.6 2.1 %collective-permute-start.9 = (f32[640,128]{1,0:T(8,128)S(1)}, f32[640,128]{1,0:T(8,128)S(1)}, u32[]{:S(2)}, u32[]{:S(2)}) collective-permute-start(f32[640,128]{1,0:T(8,128)S(1)} %collective-permute-done.8.refs_6_), channel_id=1, source_target_pairs={{0,1},{1,0},{2,3},{3,2},{4,5},{5,4},{6,7},{7,6},{8,9},{9,8},{10,11... | collective-permute-start | bytes 983048 | tf_op jit(solution)/shard_map/ppermute | solution.py:335
